TPU v7x, 128 devices: a whole 4x4x4 slice. The times are simulated.
128 devices in a mesh: aa: 8 (over z, core), ba: 16 (over x, y).
Axes of the slice: x: 4, y: 4, z: 4, core: 2. Of those that a mesh axis runs over, the one named last changes fastest.
Arguments:
- points_a: float32 [8192, 256], P(('aa', 'ba')), may hold values from -20 to 20, as said below
- points_b: float32 [65536, 256], P(('ba', 'aa')), may hold values from -20 to 20, as said below
Outputs:
- potential_a: float32 [8192], P('aa')
- potential_b: float32 [65536], P('ba')
- grad_a: float32 [8192, 256], P(('aa', 'ba'))
Inputs may be any that keep to these rules, and one draw needn't show every extreme that they name: `points_a`: Real-valued embeddings whose entries stay within the range. `points_b`: Real-valued embeddings whose entries stay within the range.
All inputs are finite; a program needn't handle non-finite values.
Results may differ from a plain program's by a relative error of at most 0.0003.
Values sent between devices are 32-bit elements; how exact they have to be, the bound alone decides.
No kernel may reach another device: no remote copies, remote signals or barrier semaphores. Data moves between devices by JAX's collectives and lax.ppermute only.
A program may use at most 64 MiB of HBM per device.

v0:
```python
import math

import jax
import jax.numpy as jnp
from jax import lax
from jax.sharding import PartitionSpec as P

ITERS = 2


HIGH = lax.Precision.HIGHEST


def cost_tile(rows, row_norms, cols, col_norms):
    cross = jnp.einsum("iw,jw->ij", rows, cols, precision=HIGH, preferred_element_type=jnp.float32)
    return row_norms[:, None] + col_norms[None, :] - 2.0 * cross


def combine_pairs(first, second):
    peak = jnp.maximum(first[0], second[0])
    total = first[1] * jnp.exp(first[0] - peak) + second[1] * jnp.exp(second[0] - peak)
    return (peak, total)


def body(points_a, points_b):
    whole_a = lax.all_gather(points_a, "ba", axis=0, tiled=True)
    whole_b = lax.all_gather(points_b, "aa", axis=0, tiled=True)
    rows_a, width = whole_a.shape
    rows_b = whole_b.shape[0]
    eps = width / 8.0
    log_a = -math.log(rows_a * lax.axis_size("aa"))
    log_b = -math.log(rows_b * lax.axis_size("ba"))
    norms_a = jnp.sum(whole_a * whole_a, axis=1)
    norms_b = jnp.sum(whole_b * whole_b, axis=1)
    block = min(256, rows_a)
    number = rows_a // block
    blocks_a = whole_a.reshape(number, block, width)
    bnorms_a = norms_a.reshape(number, block)

    def row_update(pot_b):

        def one_block(item):
            xs, ns = item
            scores = (pot_b[None, :] - cost_tile(xs, ns, whole_b, norms_b)) / eps + log_b
            peak = jnp.max(scores, axis=1)
            return (peak, jnp.sum(jnp.exp(scores - peak[:, None]), axis=1))

        peak, total = lax.map(one_block, (blocks_a, bnorms_a))
        peak = peak.reshape(rows_a)
        total = total.reshape(rows_a)
        top = lax.pmax(peak, "ba")
        total = lax.psum(total * jnp.exp(peak - top), "ba")
        return -eps * (top + jnp.log(total))

    def col_update(pot_a):
        blocks_f = pot_a.reshape(number, block)

        def step(carry, item):
            xs, ns, fs = item
            scores = (fs[:, None] - cost_tile(xs, ns, whole_b, norms_b)) / eps + log_a
            peak = jnp.max(scores, axis=0)
            total = jnp.sum(jnp.exp(scores - peak[None, :]), axis=0)
            return (combine_pairs(carry, (peak, total)), None)

        init = (jnp.full((rows_b,), -1e30, jnp.float32), jnp.zeros((rows_b,), jnp.float32))
        (peak, total), unused = lax.scan(step, init, (blocks_a, bnorms_a, blocks_f))
        top = lax.pmax(peak, "aa")
        total = lax.psum(total * jnp.exp(peak - top), "aa")
        return -eps * (top + jnp.log(total))

    pot_b = jnp.zeros((rows_b,), jnp.float32)
    pot_a = jnp.zeros((rows_a,), jnp.float32)
    for turn in range(ITERS):
        pot_a = row_update(pot_b)
        pot_b = col_update(pot_a)
    sub = math.gcd(rows_a, block)
    pieces = rows_a // sub
    xs_all = whole_a.reshape(pieces, sub, width)
    ns_all = norms_a.reshape(pieces, sub)
    fs_all = pot_a.reshape(pieces, sub)

    def grad_block(item):
        xs, ns, fs = item
        tile_q = jnp.exp(
            (fs[:, None] + pot_b[None, :] - cost_tile(xs, ns, whole_b, norms_b)) / eps + log_b
        )
        mass = jnp.sum(tile_q, axis=1)
        pulled = jnp.dot(tile_q, whole_b, precision=HIGH, preferred_element_type=jnp.float32)
        return 2.0 * (xs * mass[:, None] - pulled)

    summed = lax.psum(lax.map(grad_block, (xs_all, ns_all, fs_all)).reshape(rows_a, width), "ba")
    share = rows_a // lax.axis_size("ba")
    grad_a = lax.dynamic_slice_in_dim(summed, lax.axis_index("ba") * share, share, 0)
    return (pot_a, pot_b, grad_a)


def solution(mesh):
    placed = (P(("aa", "ba"), None), P(("ba", "aa"), None))
    return jax.shard_map(
        body,
        mesh=mesh,
        in_specs=placed,
        out_specs=(P("aa"), P("ba"), P(("aa", "ba"), None)),
        check_vma=False,
    )
```

profile of v0, /device:TPU:0, one launch (start us, length us, event | category | flops | bytes accessed | tf_op | source)
XLA Modules:
  0.0 584.8 jit_solution(204015368165632645)
XLA Ops:
  8.7 46.5 %all-gather.3.cloned.1.call-done = f32[1024,256]{1,0:T(8,128)} async-done(((f32[64,256]{1,0:T(8,128)}), f32[1024,256]{1,0:T(8,128)}) %all-gather.3.cloned.1.call-update) | async-done | bytes 1048592 | tf_op jit(solution)/shard_map/all_gather | solution.py:26
  56.8 31.8 %all-gather.5.cloned.1.call-done = f32[4096,256]{1,0:T(8,128)} async-done(((f32[512,256]{1,0:T(8,128)}), f32[4096,256]{1,0:T(8,128)}) %all-gather.5.cloned.1.call-update) | async-done | bytes 4194320 | tf_op jit(solution)/shard_map/all_gather | solution.py:27
  91.4 29.3 %while.60 = (s32[]{:T(128)}, f32[4,256]{1,0:T(4,128)S(1)}, f32[4,256]{1,0:T(4,128)S(1)}, f32[4,256]{1,0:T(4,128)S(1)}, f32[4096]{0:T(1024)S(1)}, /*index=5*/f32[...) while((s32[]{:T(128)}, f32[4,256]{1,0:T(4,128)S(1)}, f32[4,256]{1,0:T(4,128)S(1)}, ...), condition=%wide.region_5.6_spmd, body=%wide.region_2.5_spmd.sunk | while | flops 3230662144 | bytes 12871789 | solution.py:48
  120.7 40.3 %pmax.28 = f32[1024]{0:T(1024)S(1)} all-reduce(f32[1024]{0:T(1024)S(1)} %bitcast.119), channel_id=1, replica_groups=mesh['aa'=8,'ba'=16] {'ba'}, use_global_device_ids=true, to_apply=%region_6.7 | all-reduce | flops 1024 | bytes 8192 | tf_op jit(solution)/shard_map/pmax | solution.py:51
  161.1 35.5 %psum.35 = f32[1024]{0:T(1024)S(1)} all-reduce(f32[1024]{0:T(1024)S(1)} %exponential_multiply_fusion.3), channel_id=1, replica_groups=mesh['aa'=8,'ba'=16] {'ba'}, use_global_device_ids=true, to_apply=%region_7.8 | all-reduce | flops 1024 | bytes 8192 | tf_op jit(solution)/shard_map/psum | solution.py:52
  196.6 28.0 %while.63 = (s32[]{:T(128)}, f32[4096]{0:T(1024)S(1)}, f32[4096]{0:T(1024)S(1)}, f32[4,256]{1,0:T(4,128)S(1)}, f32[4,256]{1,0:T(4,128)S(1)}, /*index=5*/f32[4096...) while((s32[]{:T(128)}, f32[4096]{0:T(1024)S(1)}, ...), condition=%wide.region_11.12_spmd.clone, body=%wide.region_8.11_spmd.clone.sunk | while | flops 3230687232 | bytes 13015159 | solution.py:66
  224.6 23.6 %pmax.29 = f32[4096]{0:T(1024)S(1)} all-reduce(f32[4096]{0:T(1024)S(1)} %get-tuple-element.214), channel_id=1, replica_groups=mesh['aa'=8,'ba'=16] {'aa'}, use_global_device_ids=true, to_apply=%region_12.13 | all-reduce | flops 4096 | bytes 32768 | tf_op jit(solution)/shard_map/pmax | solution.py:67
  248.2 23.6 %psum.36 = f32[4096]{0:T(1024)S(1)} all-reduce(f32[4096]{0:T(1024)S(1)} %exponential_multiply_fusion.1), channel_id=1, replica_groups=mesh['aa'=8,'ba'=16] {'aa'}, use_global_device_ids=true, to_apply=%region_13.14 | all-reduce | flops 4096 | bytes 32768 | tf_op jit(solution)/shard_map/psum | solution.py:68
  271.8 29.5 %while.61 = (s32[]{:T(128)}, f32[4,256]{1,0:T(4,128)S(1)}, f32[4,256]{1,0:T(4,128)S(1)}, f32[4096]{0:T(1024)S(1)}, f32[4,256]{1,0:T(4,128)S(1)}, /*index=5*/f32[...) while((s32[]{:T(128)}, f32[4,256]{1,0:T(4,128)S(1)}, ...), condition=%wide.region_17.18_spmd, body=%wide.region_14.17_spmd.sunk | while | flops 3230662144 | bytes 12888181 | solution.py:48
  271.8 6.5 %fusion.71 = (f32[256]{0:T(256)S(1)}, f32[256,4096]{1,0:T(8,128)S(1)}) fusion(f32[4096,256]{1,0:T(8,128)} %get-tuple-element.736, f32[4,256,256]{2,1,0:T(8,128)S(1)} %get-tuple-element.735, s32[]{:T(128)} %get-tuple-element.719, f32[4096]{0:T(1024)S(1)} %get-tuple-element.734, f32[256]{0:T(256)S(1)} %bitcast.124, f32[4096]{0:T(1024)S(1)} %get-tuple-element.732), kind=kOutput, calls=%fused_computation.76.clone.1 | convolution fusion | flops 3228565248 | bytes 8685572 | tf_op jit(solution)/shard_map/while/body/eval_jaxpr/iw,jw->ij/dot_general | solution.py:15
  279.2 6.5 %fusion.71 = (f32[256]{0:T(256)S(1)}, f32[256,4096]{1,0:T(8,128)S(1)}) fusion(f32[4096,256]{1,0:T(8,128)} %get-tuple-element.736, f32[4,256,256]{2,1,0:T(8,128)S(1)} %get-tuple-element.735, s32[]{:T(128)} %get-tuple-element.719, f32[4096]{0:T(1024)S(1)} %get-tuple-element.734, f32[256]{0:T(256)S(1)} %bitcast.124, f32[4096]{0:T(1024)S(1)} %get-tuple-element.732), kind=kOutput, calls=%fused_computation.76.clone.1 | convolution fusion | flops 3228565248 | bytes 8685572 | tf_op jit(solution)/shard_map/while/body/eval_jaxpr/iw,jw->ij/dot_general | solution.py:15
  286.5 6.5 %fusion.71 = (f32[256]{0:T(256)S(1)}, f32[256,4096]{1,0:T(8,128)S(1)}) fusion(f32[4096,256]{1,0:T(8,128)} %get-tuple-element.736, f32[4,256,256]{2,1,0:T(8,128)S(1)} %get-tuple-element.735, s32[]{:T(128)} %get-tuple-element.719, f32[4096]{0:T(1024)S(1)} %get-tuple-element.734, f32[256]{0:T(256)S(1)} %bitcast.124, f32[4096]{0:T(1024)S(1)} %get-tuple-element.732), kind=kOutput, calls=%fused_computation.76.clone.1 | convolution fusion | flops 3228565248 | bytes 8685572 | tf_op jit(solution)/shard_map/while/body/eval_jaxpr/iw,jw->ij/dot_general | solution.py:15
  293.9 6.5 %fusion.71 = (f32[256]{0:T(256)S(1)}, f32[256,4096]{1,0:T(8,128)S(1)}) fusion(f32[4096,256]{1,0:T(8,128)} %get-tuple-element.736, f32[4,256,256]{2,1,0:T(8,128)S(1)} %get-tuple-element.735, s32[]{:T(128)} %get-tuple-element.719, f32[4096]{0:T(1024)S(1)} %get-tuple-element.734, f32[256]{0:T(256)S(1)} %bitcast.124, f32[4096]{0:T(1024)S(1)} %get-tuple-element.732), kind=kOutput, calls=%fused_computation.76.clone.1 | convolution fusion | flops 3228565248 | bytes 8685572 | tf_op jit(solution)/shard_map/while/body/eval_jaxpr/iw,jw->ij/dot_general | solution.py:15
  301.2 37.5 %pmax.30 = f32[1024]{0:T(1024)S(1)} all-reduce(f32[1024]{0:T(1024)S(1)} %bitcast.121), channel_id=1, replica_groups=mesh['aa'=8,'ba'=16] {'ba'}, use_global_device_ids=true, to_apply=%region_18.19 | all-reduce | flops 1024 | bytes 8192 | tf_op jit(solution)/shard_map/pmax | solution.py:51
  338.7 35.7 %psum.37 = f32[1024]{0:T(1024)S(1)} all-reduce(f32[1024]{0:T(1024)S(1)} %exponential_multiply_fusion.2), channel_id=1, replica_groups=mesh['aa'=8,'ba'=16] {'ba'}, use_global_device_ids=true, to_apply=%region_19.20 | all-reduce | flops 1024 | bytes 8192 | tf_op jit(solution)/shard_map/psum | solution.py:52
  375.0 28.2 %while.64 = (s32[]{:T(128)}, f32[4096]{0:T(1024)S(1)}, f32[4096]{0:T(1024)S(1)}, f32[4,256]{1,0:T(4,128)S(1)}, f32[4,256]{1,0:T(4,128)S(1)}, /*index=5*/f32[4096...) while((s32[]{:T(128)}, f32[4096]{0:T(1024)S(1)}, ...), condition=%wide.region_23.24_spmd.clone, body=%wide.region_20.23_spmd.clone.sunk | while | flops 3230687232 | bytes 13015159 | solution.py:66
  403.2 23.6 %pmax.31 = f32[4096]{0:T(1024)S(1)} all-reduce(f32[4096]{0:T(1024)S(1)} %get-tuple-element.218), channel_id=1, replica_groups=mesh['aa'=8,'ba'=16] {'aa'}, use_global_device_ids=true, to_apply=%region_24.25 | all-reduce | flops 4096 | bytes 32768 | tf_op jit(solution)/shard_map/pmax | solution.py:67
  426.8 23.6 %psum.38 = f32[4096]{0:T(1024)S(1)} all-reduce(f32[4096]{0:T(1024)S(1)} %exponential_multiply_fusion), channel_id=1, replica_groups=mesh['aa'=8,'ba'=16] {'aa'}, use_global_device_ids=true, to_apply=%region_25.26 | all-reduce | flops 4096 | bytes 32768 | tf_op jit(solution)/shard_map/psum | solution.py:68
  450.3 43.1 %while.62 = (s32[]{:T(128)}, f32[4,256,256]{2,1,0:T(8,128)S(1)}, f32[4,256,256]{2,1,0:T(8,128)S(1)}, f32[4,256]{1,0:T(4,128)S(1)}, f32[4096]{0:T(1024)S(1)}, /*i...) while((s32[]{:T(128)}, f32[4,256,256]{2,1,0:T(8,128)S(1)}, ...), condition=%wide.region_28.29_spmd, body=%wide.region_26.28_spmd.sunk | while | flops 6451036160 | bytes 34381956 | solution.py:91
  450.4 7.2 %fusion.75 = (f32[256]{0:T(256)S(1)}, f32[256,4096]{1,0:T(8,128)S(1)}) fusion(f32[4096,256]{1,0:T(8,128)} %get-tuple-element.794, f32[4,256,256]{2,1,0:T(8,128)S(1)} %get-tuple-element.789, s32[]{:T(128)} %get-tuple-element.778, f32[4096]{0:T(1024)S(1)} %get-tuple-element.793, f32[256]{0:T(256)S(1)} %bitcast.129, f32[4096]{0:T(1024)S(1)} %get-tuple-element.791, ...), kind=kOutput, calls=%fused_computation.77.clone.1 | convolution fusion | flops 3229613824 | bytes 8686596 | tf_op jit(solution)/shard_map/while/body/eval_jaxpr/iw,jw->ij/dot_general | solution.py:15
  461.1 7.2 %fusion.75 = (f32[256]{0:T(256)S(1)}, f32[256,4096]{1,0:T(8,128)S(1)}) fusion(f32[4096,256]{1,0:T(8,128)} %get-tuple-element.794, f32[4,256,256]{2,1,0:T(8,128)S(1)} %get-tuple-element.789, s32[]{:T(128)} %get-tuple-element.778, f32[4096]{0:T(1024)S(1)} %get-tuple-element.793, f32[256]{0:T(256)S(1)} %bitcast.129, f32[4096]{0:T(1024)S(1)} %get-tuple-element.791, ...), kind=kOutput, calls=%fused_computation.77.clone.1 | convolution fusion | flops 3229613824 | bytes 8686596 | tf_op jit(solution)/shard_map/while/body/eval_jaxpr/iw,jw->ij/dot_general | solution.py:15
  471.9 7.2 %fusion.75 = (f32[256]{0:T(256)S(1)}, f32[256,4096]{1,0:T(8,128)S(1)}) fusion(f32[4096,256]{1,0:T(8,128)} %get-tuple-element.794, f32[4,256,256]{2,1,0:T(8,128)S(1)} %get-tuple-element.789, s32[]{:T(128)} %get-tuple-element.778, f32[4096]{0:T(1024)S(1)} %get-tuple-element.793, f32[256]{0:T(256)S(1)} %bitcast.129, f32[4096]{0:T(1024)S(1)} %get-tuple-element.791, ...), kind=kOutput, calls=%fused_computation.77.clone.1 | convolution fusion | flops 3229613824 | bytes 8686596 | tf_op jit(solution)/shard_map/while/body/eval_jaxpr/iw,jw->ij/dot_general | solution.py:15
  482.7 7.2 %fusion.75 = (f32[256]{0:T(256)S(1)}, f32[256,4096]{1,0:T(8,128)S(1)}) fusion(f32[4096,256]{1,0:T(8,128)} %get-tuple-element.794, f32[4,256,256]{2,1,0:T(8,128)S(1)} %get-tuple-element.789, s32[]{:T(128)} %get-tuple-element.778, f32[4096]{0:T(1024)S(1)} %get-tuple-element.793, f32[256]{0:T(256)S(1)} %bitcast.129, f32[4096]{0:T(1024)S(1)} %get-tuple-element.791, ...), kind=kOutput, calls=%fused_computation.77.clone.1 | convolution fusion | flops 3229613824 | bytes 8686596 | tf_op jit(solution)/shard_map/while/body/eval_jaxpr/iw,jw->ij/dot_general | solution.py:15
  494.4 82.3 %all-reduce.2.cloned.1.call-done = f32[1024,256]{1,0:T(8,128)} async-done(((f32[1024,256]{1,0:T(8,128)}), f32[1024,256]{1,0:T(8,128)}) %all-reduce.2.cloned.1.call-update) | async-done | bytes 1048592 | tf_op jit(solution)/shard_map/psum | solution.py:91
  (125 shorter events, 111.5 us)
Async XLA Ops:
  7.2 48.0 %all-gather.3.cloned.1.call-start = ((), (), s32[]{:S(2)}) async-start(), calls=%async_computation | async-start | bytes 1114112 | tf_op jit(solution)/shard_map/all_gather | solution.py:26
  7.9 80.7 %all-gather.5.cloned.1.call-start = ((), (), s32[]{:S(2)}) async-start(), calls=%async_computation.1 | async-start | bytes 4718592 | tf_op jit(solution)/shard_map/all_gather | solution.py:27
  8.6 568.1 %all-reduce.2.cloned.1.call-start = ((), (), s32[]{:S(2)}) async-start(), calls=%async_computation.2 | async-start | bytes 2097152 | tf_op jit(solution)/shard_map/psum | solution.py:91
  55.2 36.2 %copy-start.1 = (f32[1024,256]{1,0:T(8,128)S(1)}, f32[1024,256]{1,0:T(8,128)}, u32[]{:S(2)}) copy-start(f32[1024,256]{1,0:T(8,128)} %all-gather.3.cloned.1.call-done) | copy-start | bytes 3145732
  374.4 0.6 copy-start.4
  450.4 7.2 %copy-start = (f32[4096,256]{1,0:T(8,128)S(1)}, f32[4096,256]{1,0:T(8,128)}, u32[]{:S(2)}) copy-start(f32[4096,256]{1,0:T(8,128)} %get-tuple-element.794) | copy-start | bytes 12582916 | tf_op jit(solution)/shard_map/while
  461.1 7.2 %copy-start = (f32[4096,256]{1,0:T(8,128)S(1)}, f32[4096,256]{1,0:T(8,128)}, u32[]{:S(2)}) copy-start(f32[4096,256]{1,0:T(8,128)} %get-tuple-element.794) | copy-start | bytes 12582916 | tf_op jit(solution)/shard_map/while
  471.9 7.2 %copy-start = (f32[4096,256]{1,0:T(8,128)S(1)}, f32[4096,256]{1,0:T(8,128)}, u32[]{:S(2)}) copy-start(f32[4096,256]{1,0:T(8,128)} %get-tuple-element.794) | copy-start | bytes 12582916 | tf_op jit(solution)/shard_map/while
  482.6 7.2 %copy-start = (f32[4096,256]{1,0:T(8,128)S(1)}, f32[4096,256]{1,0:T(8,128)}, u32[]{:S(2)}) copy-start(f32[4096,256]{1,0:T(8,128)} %get-tuple-element.794) | copy-start | bytes 12582916 | tf_op jit(solution)/shard_map/while
  493.4 1.0 copy-start.2
  493.4 84.8 %copy-start.3 = (f32[4096]{0:T(1024)}, f32[4096]{0:T(1024)S(1)}, u32[]{:S(2)}) copy-start(f32[4096]{0:T(1024)S(1)} %get-tuple-element.824) | copy-start | bytes 49156
Sparse Core Ops, SparseCore 0:
  10.1 45.0 all-gather.2
  56.9 31.5 all-gather.4
  494.6 82.1 all-reduce.1
where the time goes:
time: 585 us
  blocking collectives  243 us (42%)
  waiting for transfers between devices  162 us (28%)
  matrix products  146 us (25%)
  other arithmetic  15 us (3%)
  between operations  13.9 us (2%)
    dot_general x20, matrix products, cost_tile(): jnp.einsum('iw,jw->ij', rows, cols, precision=HIGH, preferred_element_typ...  132 us
    psum x1, waiting for transfers between devices, body(): lax.psum(lax.map(grad_block, (xs_all, ns_all, fs_all)).reshape(rows_a, wi...  82.3 us
    pmax x2, blocking collectives, row_update(): top = lax.pmax(peak, 'ba')  77.8 us
    psum x2, blocking collectives, row_update(): total = lax.psum(total * jnp.exp(peak - top), 'ba')  71.1 us
    pmax x2, blocking collectives, col_update(): top = lax.pmax(peak, 'aa')  47.1 us
    psum x2, blocking collectives, col_update(): total = lax.psum(total * jnp.exp(peak - top), 'aa')  47.1 us
    all_gather x1, waiting for transfers between devices, body(): whole_a = lax.all_gather(points_a, 'ba', axis=0, tiled=True)  46.5 us
    all_gather x1, waiting for transfers between devices, body(): whole_b = lax.all_gather(points_b, 'aa', axis=0, tiled=True)  31.8 us
  transfers between devices with their start and end apart: 3, of which 3 were waited for; matrix products, arithmetic and copies ran while one was open for 0% of the time, Pallas kernels for 0%

commit v1 on v0

v1 whole, which is shorter than its diff:
```python
import math

import jax
import jax.numpy as jnp
from jax import lax
from jax.experimental import pallas as pl
from jax.experimental.pallas import tpu as pltpu
from jax.sharding import PartitionSpec as P

ITERS = 2
LOG2E = math.log2(math.e)
LANES = 128
MIB = 1024 * 1024


def split(x):
    hi = x.astype(jnp.bfloat16)
    return hi, (x - hi.astype(jnp.float32)).astype(jnp.bfloat16)


def row_norms(x):
    sq = x * x
    part = sq[:, :LANES]
    for k in range(LANES, sq.shape[1], LANES):
        part = part + sq[:, k:k + LANES]
    return jnp.sum(part.T, axis=0, keepdims=True)


def combine(parts):
    top = jnp.max(parts, axis=0, keepdims=True)
    return top + jnp.log2(jnp.sum(jnp.exp2(parts - top), axis=0, keepdims=True))


def scores_kernel(eps, places, a_ref, *refs):
    pieces, (s_ref, bhi_ref, blo_ref, a2_ref, b2_ref, left) = refs[:len(places)], refs[len(places):]
    x = a_ref[...]
    a2_ref[...] = row_norms(x) * (LOG2E / eps)
    hi, lo = split(x * (2.0 * LOG2E / eps))
    left[...] = jnp.concatenate([hi, hi, lo], axis=1)
    me = lax.axis_index("aa")
    dims = (((1,), (1,)), ((), ()))
    for ref, place in zip(pieces, places):
        rows = ref.shape[0]
        at = pl.ds(pl.multiple_of(place(me), rows), rows)
        y = ref[...]
        b2_ref[:, at] = row_norms(y) * (LOG2E / eps)
        hi, lo = split(y)
        bhi_ref[at, :] = hi
        blo_ref[at, :] = lo
        right = jnp.concatenate([hi, lo, hi], axis=1)
        s_ref[:, at] = lax.dot_general(left[...], right, dims, preferred_element_type=jnp.float32)


def row_pass_kernel(log_a, first, part_ref, b2_ref, s_ref, out_ref, beta_ref, wide, top, tot):
    beta = -b2_ref[...] if first else -combine(part_ref[...]) - log_a
    beta_ref[...] = beta
    wide[...] = jnp.broadcast_to(beta, wide.shape)
    cols = s_ref.shape[1] // LANES

    def group(r, carry):
        rows = pl.ds(pl.multiple_of(r * 8, 8), 8)
        x = [s_ref[rows, k * LANES:(k + 1) * LANES] + wide[:, k * LANES:(k + 1) * LANES] for k in range(cols)]
        m = tree(jnp.maximum, x)
        top[rows, :] = m
        tot[rows, :] = tree(jnp.add, [jnp.exp2(v - m) for v in x])
        return carry

    lax.fori_loop(0, s_ref.shape[0] // 8, group, 0, unroll=2)
    m = top[...].T
    peak = jnp.max(m, axis=0, keepdims=True)
    total = jnp.sum(tot[...].T * jnp.exp2(m - peak), axis=0, keepdims=True)
    out_ref[...] = jnp.broadcast_to(peak + jnp.log2(total), out_ref.shape)


def tree(op, xs):
    xs = list(xs)
    while len(xs) > 1:
        xs = [op(xs[i], xs[i + 1]) if i + 1 < len(xs) else xs[i] for i in range(0, len(xs), 2)]
    return xs[0]


def col_pass_kernel(log_b, part_ref, s_ref, out_ref, alpha_ref, wide):
    alpha = -combine(part_ref[...]) - log_b
    alpha_ref[...] = alpha
    wide[...] = jnp.broadcast_to(alpha, (LANES, alpha.shape[1])).T
    rows = s_ref.shape[0]
    piece = 256

    def group(c, carry):
        cols = pl.ds(pl.multiple_of(c * LANES, LANES), LANES)
        m = l = None
        for r in range(0, rows, piece):
            x = [s_ref[r + q:r + q + 8, cols] + wide[r + q:r + q + 8, :] for q in range(0, piece, 8)]
            top = tree(jnp.maximum, x)
            if m is None:
                m = top
                l = tree(jnp.add, [jnp.exp2(v - m) for v in x])
            else:
                new = jnp.maximum(m, top)
                l = l * jnp.exp2(m - new) + tree(jnp.add, [jnp.exp2(v - new) for v in x])
                m = new
        peak = jnp.max(m, axis=0, keepdims=True)
        total = jnp.sum(l * jnp.exp2(m - peak), axis=0, keepdims=True)
        out_ref[:, cols] = jnp.broadcast_to(peak + jnp.log2(total), (out_ref.shape[0], LANES))
        return carry

    lax.fori_loop(0, s_ref.shape[1] // LANES, group, 0)


def grad_kernel(log_a, log_b, part_ref, alpha_ref, a_ref, bhi_ref, blo_ref, s_ref, g_ref, beta_ref, awide, bwide, mass):
    beta = -combine(part_ref[...]) - log_a
    beta_ref[...] = beta
    bwide[...] = jnp.broadcast_to(beta + log_b, bwide.shape)
    awide[...] = jnp.broadcast_to(alpha_ref[...], (LANES, alpha_ref.shape[1])).T
    g_ref[...] = jnp.zeros_like(g_ref)
    mass[...] = jnp.zeros_like(mass)
    step, piece = 512, 256
    rows = s_ref.shape[0]

    def chunk(k, carry):
        at = pl.ds(pl.multiple_of(k * step, step), step)
        hi_b, lo_b = bhi_ref[at, :], blo_ref[at, :]
        right = jnp.concatenate([hi_b, lo_b, hi_b], axis=0)
        col = bwide[:, at][:1, :]
        for r in range(0, rows, piece):
            alpha = awide[r:r + piece, :]
            p = jnp.exp2(s_ref[r:r + piece, at] + jnp.concatenate([alpha] * (step // LANES), axis=1) + col)
            mass[r:r + piece, :] += tree(jnp.add, [p[:, q:q + LANES] for q in range(0, step, LANES)])
            hi, lo = split(p)
            left = jnp.concatenate([hi, hi, lo], axis=1)
            g_ref[r:r + piece, :] += jnp.dot(left, right, preferred_element_type=jnp.float32)
        return carry

    lax.fori_loop(0, s_ref.shape[1] // step, chunk, 0)
    total = jnp.sum(mass[...], axis=1, keepdims=True)
    g_ref[...] = 2.0 * (a_ref[...] * total - g_ref[...])


VM = pl.BlockSpec(memory_space=pltpu.VMEM)


def call(kernel, outs, scratch, *args, limit):
    return pl.pallas_call(
        kernel,
        out_shape=outs,
        in_specs=[VM] * len(args),
        out_specs=[VM] * len(outs),
        scratch_shapes=scratch,
        compiler_params=pltpu.CompilerParams(vmem_limit_bytes=limit),
    )(*args)


def f32(*shape):
    return jax.ShapeDtypeStruct(shape, jnp.float32)


def v16(*shape):
    return pltpu.VMEM(shape, jnp.bfloat16)


def v32(*shape):
    return pltpu.VMEM(shape, jnp.float32)


def spread(x, axis):
    return lax.all_to_all(x, axis, 0, 0, tiled=True)


def gather_a(points_a):
    size = lax.axis_size("ba")
    wide = jnp.broadcast_to(points_a[None], (size,) + points_a.shape)
    return lax.all_to_all(wide, "ba", 0, 0, tiled=True).reshape(size * points_a.shape[0], -1)


def gather_b(points_b):
    size = lax.axis_size("aa")
    rows = points_b.shape[0]
    half = rows // 2

    def move(x, by):
        return lax.ppermute(x, "aa", [(i, (i + 2 * by) % size) for i in range(size)])

    def swap(x):
        return lax.ppermute(x, "aa", [(i, i ^ 1) for i in range(size)])

    def place(by, flip, start):
        return lambda me: lax.rem(lax.bitwise_xor(me, flip) + 2 * by, size) * rows + start

    up, down = move(points_b, 1), move(points_b, -1)
    low, high = move(up[:half], 1), move(down[half:], -1)
    kept = [(points_b, 0, 0), (up, 3, 0), (down, 1, 0), (low, 2, 0), (high, 2, half)]
    pieces = [x for x, by, start in kept] + [swap(x) for x, by, start in kept]
    places = [place(by, flip, start) for flip in (0, 1) for x, by, start in kept]
    return pieces, places


def body(points_a, points_b):
    pieces, places = gather_b(points_b)
    return compute(gather_a(points_a), pieces, places, spread)


def compute(whole_a, pieces, places, spread):
    rows_a, width = whole_a.shape
    rows_b = sum(x.shape[0] for x in pieces)
    na, nb = lax.axis_size("aa"), lax.axis_size("ba")
    eps = width / 8.0
    log_a = -math.log2(rows_a * na)
    log_b = -math.log2(rows_b * nb)
    s, bhi, blo, a2, b2 = call(
        lambda *r: scores_kernel(eps, places, *r),
        [v32(rows_a, rows_b), v16(rows_b, width), v16(rows_b, width), f32(1, rows_a), f32(1, rows_b)],
        [v16(rows_a, 3 * width)],
        whole_a, *pieces, limit=16 * MIB)
    part = jnp.zeros((na, rows_b), jnp.float32)
    for turn in range(ITERS):
        rows, beta = call(
            lambda *r, first=turn == 0: row_pass_kernel(log_a, first, *r),
            [f32(nb, rows_a), f32(1, rows_b)],
            [v32(8, rows_b), v32(rows_a, LANES), v32(rows_a, LANES)],
            part, b2, s, limit=8 * MIB)
        cols, alpha = call(
            lambda *r: col_pass_kernel(log_b, *r),
            [f32(na, rows_b), f32(1, rows_a)],
            [v32(rows_a, LANES)],
            spread(rows, "ba"), s, limit=8 * MIB)
        part = spread(cols, "aa")
    g, beta = call(
        lambda *r: grad_kernel(log_a, log_b, *r),
        [f32(rows_a, width), f32(1, rows_b)],
        [v32(rows_a, LANES), v32(8, rows_b), v32(rows_a, LANES)],
        part, alpha, whole_a, bhi, blo, s, limit=12 * MIB)
    scale = eps / LOG2E
    pot_a = (scale * (alpha + a2)).reshape(rows_a)
    pot_b = (scale * (beta + b2)).reshape(rows_b)
    shares = lax.all_to_all(g.reshape(nb, rows_a // nb, width), "ba", 0, 0, tiled=True)
    return (pot_a, pot_b, jnp.sum(shares, axis=0))


def solution(mesh):
    placed = (P(("aa", "ba"), None), P(("ba", "aa"), None))
    return jax.shard_map(
        body,
        mesh=mesh,
        in_specs=placed,
        out_specs=(P("aa"), P("ba"), P(("aa", "ba"), None)),
        check_vma=False,
    )
```

time: 585 us -> 135 us (0.23)
  blocking collectives: 243 us -> 40.7 us
  matrix products: 146 us -> 0 us
  waiting for transfers between devices: 162 us -> 29.3 us
  Pallas kernels: 0 us -> 39.6 us
  starting transfers between devices: 0.11 us -> 19.4 us
  between operations: 13.9 us -> 0.77 us
  other arithmetic: 15 us -> 1.92 us
    dot_general x24 -> x0, matrix products: 146 us -> none  [the longest x20 132 us: cost_tile(): jnp.einsum('iw,jw->ij', rows, cols, precision=HIGH, preferred_element_typ...]
    pmax x4 -> x0, blocking collectives: 125 us -> none  [the longest x2 77.8 us: row_update(): top = lax.pmax(peak, 'ba')]
    psum x4 -> x0, blocking collectives: 118 us -> none  [the longest x2 71.1 us: row_update(): total = lax.psum(total * jnp.exp(peak - top), 'ba')]
    psum x1 -> x0, waiting for transfers between devices: 82.3 us -> none  [body(): lax.psum(lax.map(grad_block, (xs_all, ns_all, fs_all)).reshape(rows_a, wi...]
    all_gather x2 -> x0, waiting for transfers between devices: 78.3 us -> none  [the longest x1 46.5 us: body(): whole_a = lax.all_gather(points_a, 'ba', axis=0, tiled=True)]
    all_to_all x0 -> x4, blocking collectives: none -> 40.7 us  [spread(): return lax.all_to_all(x, axis, 0, 0, tiled=True)]
    pallas_call x0 -> x6, Pallas kernels: none -> 39.6 us  [call(): pl.pallas_call(kernel, out_shape=outs, in_specs=[VM] * len(args), out_spe...]
    all_to_all x0 -> x2, waiting for transfers between devices: none -> 21.4 us  [the longest x1 16.6 us: compute(): lax.all_to_all(g.reshape(nb, rows_a // nb, width), 'ba', 0, 0, tiled=True)]
  transfers between devices with their start and end apart: 3 -> 11, of which waited for: 3 -> 4; matrix products, arithmetic and copies ran while one was open for 0% -> 2% of each run, Pallas kernels for 0% -> 0%
where the time goes in v1:
time: 135 us; the launch traced here: 134 us
  blocking collectives  40.7 us (30%)
  Pallas kernels  39.6 us (29%)
  waiting for transfers between devices  29.3 us (22%)
  starting transfers between devices  19.4 us (14%)
  local copies, waits for them, and re-layouts  2.57 us (2%)
  other arithmetic  1.92 us (1%)
    all_to_all x4, blocking collectives, spread(): return lax.all_to_all(x, axis, 0, 0, tiled=True)  40.7 us
    pallas_call x6, Pallas kernels, call(): pl.pallas_call(kernel, out_shape=outs, in_specs=[VM] * len(args), out_spe...  39.6 us
    all_to_all x1, waiting for transfers between devices, compute(): lax.all_to_all(g.reshape(nb, rows_a // nb, width), 'ba', 0, 0, tiled=True)  16.6 us
    ppermute x4, waiting for transfers between devices, move(): lax.ppermute(x, 'aa', [(i, (i + 2 * by) % size) for i in range(size)])  7.85 us
    ppermute x4, starting transfers between devices, move(): lax.ppermute(x, 'aa', [(i, (i + 2 * by) % size) for i in range(size)])  7.62 us
    all_to_all x1, starting transfers between devices, gather_a(): lax.all_to_all(wide, 'ba', 0, 0, tiled=True)  7.03 us
    all_to_all x1, waiting for transfers between devices, gather_a(): lax.all_to_all(wide, 'ba', 0, 0, tiled=True)  4.87 us
    all_to_all x1, starting transfers between devices, compute(): lax.all_to_all(g.reshape(nb, rows_a // nb, width), 'ba', 0, 0, tiled=True)  3.65 us
  transfers between devices with their start and end apart: 11, of which 4 were waited for; matrix products, arithmetic and copies ran while one was open for 2% of the time, Pallas kernels for 0%

profile of v1, /device:TPU:0, one launch (start us, length us, event | category | flops | bytes accessed | tf_op | source)
XLA Modules:
  0.0 134.3 jit_solution(5779458650029164026)
XLA Ops:
  0.6 2.1 %collective-permute-start = (f32[512,256]{1,0:T(8,128)}, f32[512,256]{1,0:T(8,128)S(1)}, u32[]{:S(2)}, u32[]{:S(2)}) collective-permute-start(f32[512,256]{1,0:T(8,128)} %r_1_.1), channel_id=1, source_target_pairs={{0,32},{16,48},{32,64},{48,80},{64,96},{80,112},{96,0},{112,16},{1... | collective-permute-start | bytes 1572872 | tf_op jit(solution)/shard_map/ppermute | solution.py:181
  2.7 2.2 %collective-permute-start.1 = (f32[512,256]{1,0:T(8,128)}, f32[512,256]{1,0:T(8,128)S(1)}, u32[]{:S(2)}, u32[]{:S(2)}) collective-permute-start(f32[512,256]{1,0:T(8,128)} %r_1_.1), channel_id=1, source_target_pairs={{0,96},{16,112},{32,0},{48,16},{64,32},{80,48},{96,64},{112,80},{1... | collective-permute-start | bytes 1572872 | tf_op jit(solution)/shard_map/ppermute | solution.py:181
  4.9 1.9 %broadcast_in_dim.10 = f32[16,64,256]{2,1,0:T(8,128)} broadcast(f32[64,256]{1,0:T(8,128)} %param.2), dimensions={1,2} | broadcast | bytes 1114112 | tf_op jit(solution)/shard_map/broadcast_in_dim | solution.py:171
  6.8 7.0 %all-to-all-start = ((f32[16,64,256]{2,1,0:T(8,128)}), f32[16,64,256]{2,1,0:T(8,128)S(1)}, u32[]{:S(2)}, u32[]{:S(2)}) async-start(f32[16,64,256]{2,1,0:T(8,128)} %broadcast_in_dim.10), calls=%async_computation | async-start | bytes 2097152 | tf_op jit(solution)/shard_map/all_to_all | solution.py:172
  14.0 3.0 %collective-permute-done.r_2_ = f32[512,256]{1,0:T(8,128)S(1)} collective-permute-done((f32[512,256]{1,0:T(8,128)}, f32[512,256]{1,0:T(8,128)S(1)}, u32[]{:S(2)}, u32[]{:S(2)}) %collective-permute-start) | collective-permute-done | bytes 524320 | tf_op jit(solution)/shard_map/ppermute | solution.py:181
  17.1 3.3 %collective-permute-start.3 = (f32[256,256]{1,0:T(8,128)S(1)}, f32[256,256]{1,0:T(8,128)}, u32[]{:S(2)}, u32[]{:S(2)}) collective-permute-start(f32[256,256]{1,0:T(8,128)S(1)} %slice.9), channel_id=1, source_target_pairs={{0,96},{16,112},{32,0},{48,16},{64,32},{80,48},{96,64},{112,80},{1... | collective-permute-start | bytes 786440 | tf_op jit(solution)/shard_map/ppermute | solution.py:181
  20.9 4.9 %collective-permute-done.2.r_4_ = f32[256,256]{1,0:T(8,128)S(1)} collective-permute-done((f32[256,256]{1,0:T(8,128)S(1)}, f32[256,256]{1,0:T(8,128)S(1)}, u32[]{:S(2)}, u32[]{:S(2)}) %collective-permute-start.2) | collective-permute-done | bytes 262176 | tf_op jit(solution)/shard_map/ppermute | solution.py:181
  25.8 0.5 collective-permute-start.8
  26.3 4.9 %all-to-all-done = f32[16,64,256]{2,1,0:T(8,128)S(1)} async-done(((f32[16,64,256]{2,1,0:T(8,128)}), f32[16,64,256]{2,1,0:T(8,128)S(1)}, u32[]{:S(2)}, u32[]{:S(2)}) %all-to-all-start) | async-done | bytes 1048608 | tf_op jit(solution)/shard_map/all_to_all | solution.py:172
  31.2 8.9 %shard_map.49 = (f32[1024,4096]{1,0:T(8,128)S(1)}, bf16[4096,256]{1,0:T(8,128)(2,1)S(1)}, bf16[4096,256]{1,0:T(8,128)(2,1)S(1)}, f32[1,1024]{1,0:T(1,128)S(1)}, f32[1,4096]{1,0:T(1,128)S(1)}) custom-call(f32[1024,256]{1,0:T(8,128)S(1)} %bitcast.20, f32[512,256]{1,0:T(8,128)S(1)} %copy-done, f32[512,256]{1,0:T(8,128)S(1)} %collective-permute-done.r_2_, ...), custom_call_target="tpu_custom_call" | custom-call | tf_op jit(solution)/shard_map/pallas_call | solution.py:143
  40.1 4.8 %shard_map.50 = (f32[16,1024]{1,0:T(8,128)S(1)}, f32[1,4096]{1,0:T(1,128)}) custom-call(f32[8,4096]{1,0:T(8,128)S(1)} %broadcast_in_dim.4.r_0_, f32[1,4096]{1,0:T(1,128)S(1)} %get-tuple-element.15.r_1_, f32[1024,4096]{1,0:T(8,128)S(1)} %get-tuple-element.16.r_2_.r_1_.r_5_), custom_call_target="tpu_custom_call" | custom-call | tf_op jit(solution)/shard_map/pallas_call | solution.py:143
  44.9 11.3 %all_to_all.54 = f32[16,1,1024]{2,1,0:T(1,128)S(1)} all-to-all(f32[16,1,1024]{2,1,0:T(1,128)S(1)} %copy.5), channel_id=1, replica_groups=mesh['aa'=8,'ba'=16] {'ba'}, dimensions={0} | all-to-all | bytes 131072 | tf_op jit(solution)/shard_map/all_to_all | solution.py:166
  56.3 5.7 %shard_map.51 = (f32[8,4096]{1,0:T(8,128)S(1)}, f32[1,1024]{1,0:T(1,128)}) custom-call(f32[16,1024]{1,0:T(8,128)S(1)} %bitcast.24, f32[1024,4096]{1,0:T(8,128)S(1)} %get-tuple-element.16.r_2_.r_1_.r_5_), custom_call_target="tpu_custom_call" | custom-call | tf_op jit(solution)/shard_map/pallas_call | solution.py:143
  62.1 10.0 %all_to_all.55 = f32[8,1,4096]{2,1,0:T(1,128)S(1)} all-to-all(f32[8,1,4096]{2,1,0:T(1,128)S(1)} %copy.6), channel_id=1, replica_groups=mesh['aa'=8,'ba'=16] {'aa'}, dimensions={0} | all-to-all | bytes 262144 | tf_op jit(solution)/shard_map/all_to_all | solution.py:166
  72.2 4.9 %shard_map.52 = (f32[16,1024]{1,0:T(8,128)S(1)}, f32[1,4096]{1,0:T(1,128)}) custom-call(f32[8,4096]{1,0:T(8,128)S(1)} %bitcast.23, f32[1,4096]{1,0:T(1,128)S(1)} %get-tuple-element.15.r_1_, f32[1024,4096]{1,0:T(8,128)S(1)} %get-tuple-element.16.r_2_.r_1_.r_5_), custom_call_target="tpu_custom_call" | custom-call | tf_op jit(solution)/shard_map/pallas_call | solution.py:143
  77.1 10.9 %all_to_all.56 = f32[16,1,1024]{2,1,0:T(1,128)S(1)} all-to-all(f32[16,1,1024]{2,1,0:T(1,128)S(1)} %copy.7), channel_id=1, replica_groups=mesh['aa'=8,'ba'=16] {'ba'}, dimensions={0} | all-to-all | bytes 131072 | tf_op jit(solution)/shard_map/all_to_all | solution.py:166
  88.0 5.3 %shard_map.53 = (f32[8,4096]{1,0:T(8,128)S(1)}, f32[1,1024]{1,0:T(1,128)S(1)}) custom-call(f32[16,1024]{1,0:T(8,128)S(1)} %bitcast.25, f32[1024,4096]{1,0:T(8,128)S(1)} %get-tuple-element.16.r_2_.r_1_.r_5_), custom_call_target="tpu_custom_call" | custom-call | tf_op jit(solution)/shard_map/pallas_call | solution.py:143
  93.4 8.5 %all_to_all.57 = f32[8,1,4096]{2,1,0:T(1,128)S(1)} all-to-all(f32[8,1,4096]{2,1,0:T(1,128)S(1)} %copy.8), channel_id=1, replica_groups=mesh['aa'=8,'ba'=16] {'aa'}, dimensions={0} | all-to-all | bytes 262144 | tf_op jit(solution)/shard_map/all_to_all | solution.py:166
  102.0 10.1 %shard_map.54 = (f32[1024,256]{1,0:T(8,128)}, f32[1,4096]{1,0:T(1,128)S(1)}) custom-call(f32[8,4096]{1,0:T(8,128)S(1)} %bitcast.22, f32[1,1024]{1,0:T(1,128)S(1)} %get-tuple-element.20.r_1_, f32[1024,256]{1,0:T(8,128)S(1)} %bitcast.21, bf16[4096,256]{1,0:T(8,128)(2,1)S(1)} %get-tuple-element.23.r_3_, bf16[4096,256]{1,0:T(8,128)(2,1)S(1)} %get-tuple-element.24.r_4_, ...), custom_call_target="tpu_custom_call" | custom-call | tf_op jit(solution)/shard_map/pallas_call | solution.py:143
  112.1 3.7 %all-to-all-start.5 = ((f32[16,64,256]{2,1,0:T(8,128)}), f32[16,64,256]{2,1,0:T(8,128)S(1)}, u32[]{:S(2)}, u32[]{:S(2)}) async-start(f32[16,64,256]{2,1,0:T(8,128)} %bitcast.7), calls=%async_computation.5 | async-start | bytes 2097152 | tf_op jit(solution)/shard_map/all_to_all | solution.py:235
  115.8 0.6 add_multiply_fusion.1
  116.4 0.6 add_multiply_fusion
  117.0 16.6 %all-to-all-done.5 = f32[16,64,256]{2,1,0:T(8,128)S(1)} async-done(((f32[16,64,256]{2,1,0:T(8,128)}), f32[16,64,256]{2,1,0:T(8,128)S(1)}, u32[]{:S(2)}, u32[]{:S(2)}) %all-to-all-start.5) | async-done | bytes 1048608 | tf_op jit(solution)/shard_map/all_to_all | solution.py:235
  133.6 0.7 reduce_sum.9
  (25 shorter events, 1.3 us)
Async XLA Ops:
  0.6 13.3 %copy-start = (f32[512,256]{1,0:T(8,128)S(1)}, f32[512,256]{1,0:T(8,128)}, u32[]{:S(2)}) copy-start(f32[512,256]{1,0:T(8,128)} %r_1_.1) | copy-start | bytes 1572868
  0.6 16.3 %collective-permute-start = (f32[512,256]{1,0:T(8,128)}, f32[512,256]{1,0:T(8,128)S(1)}, u32[]{:S(2)}, u32[]{:S(2)}) collective-permute-start(f32[512,256]{1,0:T(8,128)} %r_1_.1), channel_id=1, source_target_pairs={{0,32},{16,48},{32,64},{48,80},{64,96},{80,112},{96,0},{112,16},{1... | collective-permute-start | bytes 1572872 | tf_op jit(solution)/shard_map/ppermute | solution.py:181
  2.7 14.4 %collective-permute-start.1 = (f32[512,256]{1,0:T(8,128)}, f32[512,256]{1,0:T(8,128)S(1)}, u32[]{:S(2)}, u32[]{:S(2)}) collective-permute-start(f32[512,256]{1,0:T(8,128)} %r_1_.1), channel_id=1, source_target_pairs={{0,96},{16,112},{32,0},{48,16},{64,32},{80,48},{96,64},{112,80},{1... | collective-permute-start | bytes 1572872 | tf_op jit(solution)/shard_map/ppermute | solution.py:181
  6.8 24.3 %all-to-all-start = ((f32[16,64,256]{2,1,0:T(8,128)}), f32[16,64,256]{2,1,0:T(8,128)S(1)}, u32[]{:S(2)}, u32[]{:S(2)}) async-start(f32[16,64,256]{2,1,0:T(8,128)} %broadcast_in_dim.10), calls=%async_computation | async-start | bytes 2097152 | tf_op jit(solution)/shard_map/all_to_all | solution.py:172
  13.9 12.4 %collective-permute-start.4 = (f32[512,256]{1,0:T(8,128)S(1)}, f32[512,256]{1,0:T(8,128)S(1)}, u32[]{:S(2)}, u32[]{:S(2)}) collective-permute-start(f32[512,256]{1,0:T(8,128)S(1)} %copy-done), channel_id=1, source_target_pairs={{0,16},{16,0},{32,48},{48,32},{64,80},{80,64},{96,112},{112,96},{1... | collective-permute-start | bytes 1572872 | tf_op jit(solution)/shard_map/ppermute | solution.py:184
  17.0 8.8 %collective-permute-start.2 = (f32[256,256]{1,0:T(8,128)S(1)}, f32[256,256]{1,0:T(8,128)S(1)}, u32[]{:S(2)}, u32[]{:S(2)}) collective-permute-start(f32[256,256]{1,0:T(8,128)S(1)} %slice.8), channel_id=1, source_target_pairs={{0,32},{16,48},{32,64},{48,80},{64,96},{80,112},{96,0},{112,16},{1... | collective-permute-start | bytes 786440 | tf_op jit(solution)/shard_map/ppermute | solution.py:181
  17.1 8.7 %collective-permute-start.3 = (f32[256,256]{1,0:T(8,128)S(1)}, f32[256,256]{1,0:T(8,128)}, u32[]{:S(2)}, u32[]{:S(2)}) collective-permute-start(f32[256,256]{1,0:T(8,128)S(1)} %slice.9), channel_id=1, source_target_pairs={{0,96},{16,112},{32,0},{48,16},{64,32},{80,48},{96,64},{112,80},{1... | collective-permute-start | bytes 786440 | tf_op jit(solution)/shard_map/ppermute | solution.py:181
  20.4 10.8 %collective-permute-start.5 = (f32[512,256]{1,0:T(8,128)S(1)}, f32[512,256]{1,0:T(8,128)}, u32[]{:S(2)}, u32[]{:S(2)}) collective-permute-start(f32[512,256]{1,0:T(8,128)S(1)} %collective-permute-done.r_2_), channel_id=1, source_target_pairs={{0,16},{16,0},{32,48},{48,32},{64,80},{80,64},{96,112},{112,96},{1... | collective-permute-start | bytes 1572872 | tf_op jit(solution)/shard_map/ppermute | solution.py:184
  20.4 10.8 %collective-permute-start.6 = (f32[512,256]{1,0:T(8,128)S(1)}, f32[512,256]{1,0:T(8,128)}, u32[]{:S(2)}, u32[]{:S(2)}) collective-permute-start(f32[512,256]{1,0:T(8,128)S(1)} %collective-permute-done.1.r_3_), channel_id=1, source_target_pairs={{0,16},{16,0},{32,48},{48,32},{64,80},{80,64},{96,112},{112,96},{1... | collective-permute-start | bytes 1572872 | tf_op jit(solution)/shard_map/ppermute | solution.py:184
  25.8 5.4 %collective-permute-start.7 = (f32[256,256]{1,0:T(8,128)S(1)}, f32[256,256]{1,0:T(8,128)}, u32[]{:S(2)}, u32[]{:S(2)}) collective-permute-start(f32[256,256]{1,0:T(8,128)S(1)} %collective-permute-done.2.r_4_), channel_id=1, source_target_pairs={{0,16},{16,0},{32,48},{48,32},{64,80},{80,64},{96,112},{112,96},{1... | collective-permute-start | bytes 786440 | tf_op jit(solution)/shard_map/ppermute | solution.py:184
  25.8 5.4 %collective-permute-start.8 = (f32[256,256]{1,0:T(8,128)}, f32[256,256]{1,0:T(8,128)}, u32[]{:S(2)}, u32[]{:S(2)}) collective-permute-start(f32[256,256]{1,0:T(8,128)} %collective-permute-done.3.r_5_), channel_id=1, source_target_pairs={{0,16},{16,0},{32,48},{48,32},{64,80},{80,64},{96,112},{112,96},{1... | collective-permute-start | bytes 786440 | tf_op jit(solution)/shard_map/ppermute | solution.py:184
  112.1 21.4 %all-to-all-start.5 = ((f32[16,64,256]{2,1,0:T(8,128)}), f32[16,64,256]{2,1,0:T(8,128)S(1)}, u32[]{:S(2)}, u32[]{:S(2)}) async-start(f32[16,64,256]{2,1,0:T(8,128)} %bitcast.7), calls=%async_computation.5 | async-start | bytes 2097152 | tf_op jit(solution)/shard_map/all_to_all | solution.py:235

commit v2 on v1

v2 whole, which is shorter than its diff:
```python
import math

import jax
import jax.numpy as jnp
from jax import lax
from jax.experimental import pallas as pl
from jax.experimental.pallas import tpu as pltpu
from jax.sharding import PartitionSpec as P

ITERS = 2
LOG2E = math.log2(math.e)
LANES = 128
MIB = 1024 * 1024


def split(x):
    hi = x.astype(jnp.bfloat16)
    return hi, (x - hi.astype(jnp.float32)).astype(jnp.bfloat16)


def row_norms(x):
    sq = x * x
    part = sq[:, :LANES]
    for k in range(LANES, sq.shape[1], LANES):
        part = part + sq[:, k:k + LANES]
    return jnp.sum(part.T, axis=0, keepdims=True)


def combine(parts):
    top = jnp.max(parts, axis=0, keepdims=True)
    return top + jnp.log2(jnp.sum(jnp.exp2(parts - top), axis=0, keepdims=True))


def prepare_kernel(eps, a_ref, left_ref, a2_ref):
    x = a_ref[...]
    a2_ref[...] = row_norms(x) * (LOG2E / eps)
    hi, lo = split(x * (2.0 * LOG2E / eps))
    left_ref[...] = jnp.concatenate([hi, hi, lo], axis=1)


def scores_kernel(eps, places, sizes, fresh, last, left, *refs):
    pieces, refs = refs[:sum(sizes)], refs[sum(sizes) + (0 if fresh else 6):]
    s_ref, bhi_ref, blo_ref, b2_ref, top_ref, tot_ref = refs[:6]
    me = lax.axis_index("aa")
    dims = (((1,), (1,)), ((), ()))
    for place, size in zip(places, sizes):
        y = jnp.concatenate([ref[...] for ref in pieces[:size]], axis=0)
        pieces = pieces[size:]
        at = pl.ds(pl.multiple_of(place(me), y.shape[0]), y.shape[0])
        norms = row_norms(y) * (LOG2E / eps)
        b2_ref[:, at] = norms
        hi, lo = split(y)
        bhi_ref[at, :] = hi
        blo_ref[at, :] = lo
        right = jnp.concatenate([hi, lo, hi], axis=1)
        x = lax.dot_general(left[...], right, dims, preferred_element_type=jnp.float32)
        s_ref[:, at] = x
        x = x - norms
        parts = [x[:, k:k + LANES] for k in range(0, y.shape[0], LANES)]
        top = tree(jnp.maximum, parts)
        if fresh:
            tot_ref[...] = tree(jnp.add, [jnp.exp2(v - top) for v in parts])
        else:
            old = top_ref[...]
            top = jnp.maximum(old, top)
            tot_ref[...] = tot_ref[...] * jnp.exp2(old - top) + tree(jnp.add, [jnp.exp2(v - top) for v in parts])
        top_ref[...] = top
        fresh = False
    if last:
        finish_rows(top_ref, tot_ref, refs[6])


def finish_rows(top_ref, tot_ref, out_ref):
    m = top_ref[...].T
    peak = jnp.max(m, axis=0, keepdims=True)
    total = jnp.sum(tot_ref[...].T * jnp.exp2(m - peak), axis=0, keepdims=True)
    out_ref[...] = jnp.broadcast_to(peak + jnp.log2(total), out_ref.shape)


def row_pass_kernel(log_a, part_ref, s_ref, out_ref, wide, top, tot):
    wide[...] = jnp.broadcast_to(-combine(part_ref[...]) - log_a, wide.shape)
    cols = s_ref.shape[1] // LANES

    def group(r, carry):
        rows = pl.ds(pl.multiple_of(r * 8, 8), 8)
        m, l = None, None
        for half in range(0, cols, 16):
            x = [s_ref[rows, k * LANES:(k + 1) * LANES] + wide[:, k * LANES:(k + 1) * LANES]
                 for k in range(half, min(cols, half + 16))]
            m, l = online(m, l, x)
        top[rows, :] = m
        tot[rows, :] = l
        return carry

    lax.fori_loop(0, s_ref.shape[0] // 8, group, 0, unroll=8)
    finish_rows(top, tot, out_ref)


def online(m, l, x):
    top = tree(jnp.maximum, x)
    if m is None:
        return top, tree(jnp.add, [jnp.exp2(v - top) for v in x])
    new = jnp.maximum(m, top)
    return new, l * jnp.exp2(m - new) + tree(jnp.add, [jnp.exp2(v - new) for v in x])


def tree(op, xs):
    xs = list(xs)
    while len(xs) > 1:
        xs = [op(xs[i], xs[i + 1]) if i + 1 < len(xs) else xs[i] for i in range(0, len(xs), 2)]
    return xs[0]


def col_pass_kernel(log_b, part_ref, s_ref, out_ref, alpha_ref, wide):
    alpha = -combine(part_ref[...]) - log_b
    alpha_ref[...] = alpha
    wide[...] = jnp.broadcast_to(alpha, (LANES, alpha.shape[1])).T
    rows = s_ref.shape[0]
    piece, across = 64, 8

    def group(c, carry):
        cols = [pl.ds(pl.multiple_of((c * across + k) * LANES, LANES), LANES) for k in range(across)]
        m, l = [None] * across, [None] * across
        for r in range(0, rows, piece):
            shift = [wide[r + q:r + q + 8, :] for q in range(0, piece, 8)]
            for k in range(across):
                x = [s_ref[r + q:r + q + 8, cols[k]] + shift[q // 8] for q in range(0, piece, 8)]
                m[k], l[k] = online(m[k], l[k], x)
        for k in range(across):
            peak = jnp.max(m[k], axis=0, keepdims=True)
            total = jnp.sum(l[k] * jnp.exp2(m[k] - peak), axis=0, keepdims=True)
            out_ref[:, cols[k]] = jnp.broadcast_to(peak + jnp.log2(total), (out_ref.shape[0], LANES))
        return carry

    lax.fori_loop(0, s_ref.shape[1] // (LANES * across), group, 0)


def grad_kernel(log_a, log_b, start, part_ref, alpha_ref, a_ref, bhi_ref, blo_ref, s_ref, g_ref, beta_ref, awide, bwide, mass, acc):
    beta = -combine(part_ref[...]) - log_a
    beta_ref[...] = beta
    bwide[...] = jnp.broadcast_to(beta + log_b, bwide.shape)
    awide[...] = jnp.broadcast_to(alpha_ref[...], (LANES, alpha_ref.shape[1])).T
    shares, n = g_ref.shape[:2]
    share = s_ref.shape[0] // shares
    step, group = 1024, 256 // n

    def take(ref, first, cols):
        return jnp.concatenate([ref[pl.ds(d * share + start, n), cols] for d in range(first, first + group)], axis=0)

    def chunk(k, begin):
        at = pl.ds(pl.multiple_of(k * step, step), step)
        hi_b, lo_b = bhi_ref[at, :], blo_ref[at, :]
        right = jnp.concatenate([hi_b, lo_b, hi_b], axis=0)
        col = bwide[:, at][:1, :]
        for first in range(0, shares, group):
            rows = slice(first * n, (first + group) * n)
            alpha = take(awide, first, slice(None))
            p = jnp.exp2(take(s_ref, first, at) + jnp.concatenate([alpha] * (step // LANES), axis=1) + col)
            part = tree(jnp.add, [p[:, q:q + LANES] for q in range(0, step, LANES)])
            hi, lo = split(p)
            left = jnp.concatenate([hi, hi, lo], axis=1)
            pulled = jnp.dot(left, right, preferred_element_type=jnp.float32)
            mass[rows, :] = part if begin else mass[rows, :] + part
            acc[rows, :] = pulled if begin else acc[rows, :] + pulled

    chunk(0, True)
    lax.fori_loop(1, s_ref.shape[1] // step, lambda k, carry: chunk(k, False), None)
    total = jnp.sum(mass[...], axis=1, keepdims=True)
    for d in range(shares):
        rows = slice(d * n, (d + 1) * n)
        g_ref[d] = 2.0 * (a_ref[pl.ds(d * share + start, n), :] * total[rows] - acc[rows, :])


VM = pl.BlockSpec(memory_space=pltpu.VMEM)


def call(kernel, outs, scratch, *args, limit=12 * MIB, aliases={}, cost=None):
    return pl.pallas_call(
        kernel,
        out_shape=outs,
        in_specs=[VM] * len(args),
        out_specs=[VM] * len(outs),
        scratch_shapes=scratch,
        input_output_aliases=aliases,
        cost_estimate=cost,
        compiler_params=pltpu.CompilerParams(vmem_limit_bytes=limit),
    )(*args)


def f32(*shape):
    return jax.ShapeDtypeStruct(shape, jnp.float32)


def v16(*shape):
    return pltpu.VMEM(shape, jnp.bfloat16)


def v32(*shape):
    return pltpu.VMEM(shape, jnp.float32)


def spread(x, axis):
    return lax.all_to_all(x, axis, 0, 0, tiled=True)


def gather_a(points_a):
    size = lax.axis_size("ba")
    wide = jnp.broadcast_to(points_a[None], (size,) + points_a.shape)
    return lax.all_to_all(wide, "ba", 0, 0, tiled=True).reshape(size * points_a.shape[0], -1)


def gather_b(points_b):
    size = lax.axis_size("aa")
    rows = points_b.shape[0]
    half = rows // 2

    def move(x, by):
        return lax.ppermute(x, "aa", [(i, (i + 2 * by) % size) for i in range(size)])

    def swap(x):
        return lax.ppermute(x, "aa", [(i, i ^ 1) for i in range(size)])

    def place(by, flip):
        return lambda me: lax.rem(lax.bitwise_xor(me, flip) + 2 * by, size) * rows

    up, down = move(points_b, 1), move(points_b, -1)
    low, high = move(up[:half], 1), move(down[half:], -1)
    def stage(*items):
        return [(pieces, place(by, flip)) for pieces, by, flip in items]

    up, down = move(points_b, 1), move(points_b, -1)
    low, high = move(up[:half], 1), move(down[half:], -1)
    return [
        stage(([points_b], 0, 0), ([swap(points_b)], 0, 1)),
        stage(([up], 3, 0), ([down], 1, 0)),
        stage(([swap(up)], 3, 1), ([swap(down)], 1, 1)),
        stage(([low, high], 2, 0), ([swap(low), swap(high)], 2, 1)),
    ]


def body(points_a, points_b):
    stages = gather_b(points_b)
    whole_a = gather_a(points_a)
    rows_a, width = whole_a.shape
    na, nb = lax.axis_size("aa"), lax.axis_size("ba")
    rows_b = points_b.shape[0] * na
    eps = width / 8.0
    log_a = -math.log2(rows_a * na)
    log_b = -math.log2(rows_b * nb)
    left, a2 = call(lambda *r: prepare_kernel(eps, *r), [v16(rows_a, 3 * width), f32(1, rows_a)], [], whole_a)
    held = []
    for k, stage in enumerate(stages):
        places = [place for pieces, place in stage]
        sizes = [len(pieces) for pieces, place in stage]
        flat = [x for pieces, place in stage for x in pieces]
        last = k == len(stages) - 1
        outs = [v32(rows_a, rows_b), v16(rows_b, width), v16(rows_b, width), v32(1, rows_b), v32(rows_a, LANES), v32(rows_a, LANES)]
        held = call(
            lambda *r: scores_kernel(eps, places, sizes, k == 0, last, *r),
            outs + ([f32(nb, rows_a)] if last else []),
            [], left, *flat, *held,
            aliases={1 + len(flat) + i: i for i in range(len(held))},
            cost=pl.CostEstimate(flops=6 * rows_a * width * sum(x.shape[0] for x in flat), bytes_accessed=4 * MIB, transcendentals=0))
    s, bhi, blo, b2, _, _, rows = held
    for turn in range(ITERS):
        if turn > 0:
            rows, = call(
                lambda *r: row_pass_kernel(log_a, *r),
                [f32(nb, rows_a)],
                [v32(8, rows_b), v32(rows_a, LANES), v32(rows_a, LANES)],
                part, s)
        cols, alpha = call(
            lambda *r: col_pass_kernel(log_b, *r),
            [f32(na, rows_b), f32(1, rows_a)],
            [v32(rows_a, LANES)],
            spread(rows, "ba"), s)
        part = spread(cols, "aa")
    share = rows_a // nb
    cut = share // 2
    sums = []
    for start in range(0, share, cut):
        g, beta = call(
            lambda *r: grad_kernel(log_a, log_b, start, *r),
            [f32(nb, cut, width), f32(1, rows_b)],
            [v32(rows_a, LANES), v32(8, rows_b), v32(nb * cut, LANES), v32(nb * cut, width)],
            part, alpha, whole_a, bhi, blo, s,
            cost=pl.CostEstimate(flops=6 * nb * cut * width * rows_b, bytes_accessed=4 * MIB, transcendentals=0))
        sums.append(jnp.sum(spread(g, "ba"), axis=0))
    scale = eps / LOG2E
    pot_a = (scale * (alpha + a2)).reshape(rows_a)
    pot_b = (scale * (beta + b2)).reshape(rows_b)
    return (pot_a, pot_b, jnp.concatenate(sums, axis=0))


def solution(mesh):
    placed = (P(("aa", "ba"), None), P(("ba", "aa"), None))
    return jax.shard_map(
        body,
        mesh=mesh,
        in_specs=placed,
        out_specs=(P("aa"), P("ba"), P(("aa", "ba"), None)),
        check_vma=False,
    )
```

time: 135 us -> 150 us (1.11)
  local copies, waits for them, and re-layouts: 2.57 us -> 16.4 us
  starting transfers between devices: 19.4 us -> 26.8 us
  Pallas kernels: 39.6 us -> 32.8 us
  waiting for transfers between devices: 29.3 us -> 24.8 us
  blocking collectives: 40.7 us -> 44.3 us
    unnamed x6 -> x24, local copies, waits for them, and re-layouts: 0.19 us -> 12.1 us
    all_to_all x1 -> x2, starting transfers between devices: 3.65 us -> 11.4 us  [spread(): return lax.all_to_all(x, axis, 0, 0, tiled=True)]
    ppermute x4, waiting for transfers between devices: 7.85 us -> 15.6 us  [move(): lax.ppermute(x, 'aa', [(i, (i + 2 * by) % size) for i in range(size)])]
    all_to_all x1 -> x2, waiting for transfers between devices: 16.6 us -> 9.27 us  [spread(): return lax.all_to_all(x, axis, 0, 0, tiled=True)]
    pallas_call x6 -> x10, Pallas kernels: 39.6 us -> 32.8 us  [call(): pl.pallas_call(kernel, out_shape=outs, in_specs=[VM] * len(args), out_spe...]
    all_to_all x1, waiting for transfers between devices: 4.87 us -> 0.01 us  [gather_a(): lax.all_to_all(wide, 'ba', 0, 0, tiled=True)]
    all_to_all x4, blocking collectives: 40.7 us -> 44.3 us  [spread(): return lax.all_to_all(x, axis, 0, 0, tiled=True)]
    slice x2, local copies, waits for them, and re-layouts: 0.04 us -> 1.94 us  [gather_b(): low, high = (move(up[:half], 1), move(down[half:], -1))]
  transfers between devices with their start and end apart: 11 -> 12, of which waited for: 4 -> 4; matrix products, arithmetic and copies ran while one was open for 2% -> 3% of each run, Pallas kernels for 0% -> 9%
where the time goes in v2:
time: 150 us; the launch traced here: 149 us
  blocking collectives  44.3 us (30%)
  Pallas kernels  32.8 us (22%)
  starting transfers between devices  26.8 us (18%)
  waiting for transfers between devices  24.8 us (17%)
  local copies, waits for them, and re-layouts  16.4 us (11%)
  other arithmetic  2.98 us (2%)
    all_to_all x4, blocking collectives, spread(): return lax.all_to_all(x, axis, 0, 0, tiled=True)  44.3 us
    pallas_call x10, Pallas kernels, call(): pl.pallas_call(kernel, out_shape=outs, in_specs=[VM] * len(args), out_spe...  32.8 us
    ppermute x4, waiting for transfers between devices, move(): lax.ppermute(x, 'aa', [(i, (i + 2 * by) % size) for i in range(size)])  15.6 us
    unnamed x24, local copies, waits for them, and re-layouts  12.1 us
    all_to_all x2, starting transfers between devices, spread(): return lax.all_to_all(x, axis, 0, 0, tiled=True)  11.4 us
    all_to_all x2, waiting for transfers between devices, spread(): return lax.all_to_all(x, axis, 0, 0, tiled=True)  9.27 us
    ppermute x4, starting transfers between devices, move(): lax.ppermute(x, 'aa', [(i, (i + 2 * by) % size) for i in range(size)])  7.55 us
    all_to_all x1, starting transfers between devices, gather_a(): lax.all_to_all(wide, 'ba', 0, 0, tiled=True)  7.12 us
  transfers between devices with their start and end apart: 12, of which 4 were waited for; matrix products, arithmetic and copies ran while one was open for 3% of the time, Pallas kernels for 9%

profile of v2, /device:TPU:0, one launch (start us, length us, event | category | flops | bytes accessed | tf_op | source)
XLA Modules:
  0.0 149.0 jit_solution(13036189356563912236)
XLA Ops:
  0.6 2.0 %broadcast_in_dim.2 = f32[16,64,256]{2,1,0:T(8,128)} broadcast(f32[64,256]{1,0:T(8,128)} %param.2), dimensions={1,2} | broadcast | bytes 1114112 | tf_op jit(solution)/shard_map/broadcast_in_dim | solution.py:208
  2.7 7.1 %all-to-all-start = ((f32[16,64,256]{2,1,0:T(8,128)}), f32[16,64,256]{2,1,0:T(8,128)S(1)}, u32[]{:S(2)}, u32[]{:S(2)}) async-start(f32[16,64,256]{2,1,0:T(8,128)} %broadcast_in_dim.2), calls=%async_computation | async-start | bytes 2097152 | tf_op jit(solution)/shard_map/all_to_all | solution.py:209
  9.8 2.0 %collective-permute-start = (f32[512,256]{1,0:T(8,128)S(1)}, f32[512,256]{1,0:T(8,128)}, u32[]{:S(2)}, u32[]{:S(2)}) collective-permute-start(f32[512,256]{1,0:T(8,128)S(1)} %copy-done.6), channel_id=1, source_target_pairs={{0,32},{16,48},{32,64},{48,80},{64,96},{80,112},{96,0},{112,16},{1... | collective-permute-start | bytes 1572872 | tf_op jit(solution)/shard_map/ppermute | solution.py:218
  11.8 2.2 %collective-permute-start.2 = (f32[512,256]{1,0:T(8,128)S(1)}, f32[512,256]{1,0:T(8,128)}, u32[]{:S(2)}, u32[]{:S(2)}) collective-permute-start(f32[512,256]{1,0:T(8,128)S(1)} %copy-done.6), channel_id=1, source_target_pairs={{0,96},{16,112},{32,0},{48,16},{64,32},{80,48},{96,64},{112,80},{1... | collective-permute-start | bytes 1572872 | tf_op jit(solution)/shard_map/ppermute | solution.py:218
  14.0 11.7 %collective-permute-done.r_1_ = f32[512,256]{1,0:T(8,128)} collective-permute-done((f32[512,256]{1,0:T(8,128)S(1)}, f32[512,256]{1,0:T(8,128)}, u32[]{:S(2)}, u32[]{:S(2)}) %collective-permute-start) | collective-permute-done | bytes 524320 | tf_op jit(solution)/shard_map/ppermute | solution.py:218
  27.7 3.3 %collective-permute-start.3 = (f32[256,256]{1,0:T(8,128)S(1)}, f32[256,256]{1,0:T(8,128)}, u32[]{:S(2)}, u32[]{:S(2)}) collective-permute-start(f32[256,256]{1,0:T(8,128)S(1)} %slice.9), channel_id=1, source_target_pairs={{0,96},{16,112},{32,0},{48,16},{64,32},{80,48},{96,64},{112,80},{1... | collective-permute-start | bytes 786440 | tf_op jit(solution)/shard_map/ppermute | solution.py:218
  31.5 3.6 %collective-permute-done.1.r_1_ = f32[256,256]{1,0:T(8,128)S(1)} collective-permute-done((f32[256,256]{1,0:T(8,128)S(1)}, f32[256,256]{1,0:T(8,128)S(1)}, u32[]{:S(2)}, u32[]{:S(2)}) %collective-permute-start.1) | collective-permute-done | bytes 262176 | tf_op jit(solution)/shard_map/ppermute | solution.py:218
  38.8 2.1 %shard_map.50 = (f32[1024,4096]{1,0:T(8,128)S(1)}, bf16[4096,256]{1,0:T(8,128)(2,1)S(1)}, bf16[4096,256]{1,0:T(8,128)(2,1)S(1)}, f32[1,4096]{1,0:T(1,128)S(1)}, ...) custom-call(bf16[1024,768]{1,0:T(8,128)(2,1)S(1)} %get-tuple-element.34.r_0_, f32[512,256]{1,0:T(8,128)S(1)} %copy-done.7, ...), custom_call_target="tpu_custom_call" | custom-call | flops 1610612736 | bytes 4194304 | tf_op jit(solution)/shard_map/pallas_call | solution.py:178
  40.9 3.4 %shard_map.51 = (f32[1024,4096]{1,0:T(8,128)S(1)}, bf16[4096,256]{1,0:T(8,128)(2,1)S(1)}, bf16[4096,256]{1,0:T(8,128)(2,1)S(1)}, f32[1,4096]{1,0:T(1,128)S(1)}, ...) custom-call(bf16[1024,768]{1,0:T(8,128)(2,1)S(1)} %get-tuple-element, ...), custom_call_target="tpu_custom_call", output_to_operand_aliasing={{0}: (3, {}), {1}: (4, {}), {2}: (5, {}), {3}: (6, {}), {4}... | custom-call | flops 1610612736 | bytes 4194304 | tf_op jit(solution)/shard_map/pallas_call | solution.py:178
  44.4 3.4 %shard_map.52 = (f32[1024,4096]{1,0:T(8,128)S(1)}, bf16[4096,256]{1,0:T(8,128)(2,1)S(1)}, bf16[4096,256]{1,0:T(8,128)(2,1)S(1)}, f32[1,4096]{1,0:T(1,128)S(1)}, ...) custom-call(bf16[1024,768]{1,0:T(8,128)(2,1)S(1)} %get-tuple-element, ...), custom_call_target="tpu_custom_call", output_to_operand_aliasing={{0}: (3, {}), {1}: (4, {}), {2}: (5, {}), {3}: (6, {}), {4}... | custom-call | flops 1610612736 | bytes 4194304 | tf_op jit(solution)/shard_map/pallas_call | solution.py:178
  47.9 3.5 %shard_map.53 = (f32[1024,4096]{1,0:T(8,128)S(1)}, bf16[4096,256]{1,0:T(8,128)(2,1)S(1)}, bf16[4096,256]{1,0:T(8,128)(2,1)S(1)}, f32[1,4096]{1,0:T(1,128)S(1)}, ...) custom-call(bf16[1024,768]{1,0:T(8,128)(2,1)S(1)} %get-tuple-element, ...), custom_call_target="tpu_custom_call", output_to_operand_aliasing={{0}: (5, {}), {1}: (6, {}), {2}: (7, {}), {3}: (8, {}), {4}... | custom-call | flops 1610612736 | bytes 4194304 | tf_op jit(solution)/shard_map/pallas_call | solution.py:178
  51.5 14.1 %all_to_all.59 = f32[16,1,1024]{2,1,0:T(1,128)S(1)} all-to-all(f32[16,1,1024]{2,1,0:T(1,128)S(1)} %copy.23), channel_id=1, replica_groups=mesh['aa'=8,'ba'=16] {'ba'}, dimensions={0} | all-to-all | bytes 131072 | tf_op jit(solution)/shard_map/all_to_all | solution.py:203
  65.6 3.9 %shard_map.54 = (f32[8,4096]{1,0:T(8,128)S(1)}, f32[1,1024]{1,0:T(1,128)}) custom-call(f32[16,1024]{1,0:T(8,128)S(1)} %bitcast.25, f32[1024,4096]{1,0:T(8,128)S(1)} %get-tuple-element.54.r_1_.r_5_), custom_call_target="tpu_custom_call" | custom-call | tf_op jit(solution)/shard_map/pallas_call | solution.py:178
  69.6 10.8 %all_to_all.60 = f32[8,1,4096]{2,1,0:T(1,128)S(1)} all-to-all(f32[8,1,4096]{2,1,0:T(1,128)S(1)} %copy.24), channel_id=1, replica_groups=mesh['aa'=8,'ba'=16] {'aa'}, dimensions={0} | all-to-all | bytes 262144 | tf_op jit(solution)/shard_map/all_to_all | solution.py:203
  80.5 3.4 %shard_map.55 = f32[16,1024]{1,0:T(8,128)S(1)} custom-call(f32[8,4096]{1,0:T(8,128)S(1)} %bitcast.24, f32[1024,4096]{1,0:T(8,128)S(1)} %get-tuple-element.54.r_1_.r_5_), custom_call_target="tpu_custom_call" | custom-call | tf_op jit(solution)/shard_map/pallas_call | solution.py:178
  84.0 10.9 %all_to_all.61 = f32[16,1,1024]{2,1,0:T(1,128)S(1)} all-to-all(f32[16,1,1024]{2,1,0:T(1,128)S(1)} %copy.25), channel_id=1, replica_groups=mesh['aa'=8,'ba'=16] {'ba'}, dimensions={0} | all-to-all | bytes 131072 | tf_op jit(solution)/shard_map/all_to_all | solution.py:203
  94.9 3.6 %shard_map.56 = (f32[8,4096]{1,0:T(8,128)S(1)}, f32[1,1024]{1,0:T(1,128)S(1)}) custom-call(f32[16,1024]{1,0:T(8,128)S(1)} %bitcast.26, f32[1024,4096]{1,0:T(8,128)S(1)} %get-tuple-element.54.r_1_.r_5_), custom_call_target="tpu_custom_call" | custom-call | tf_op jit(solution)/shard_map/pallas_call | solution.py:178
  98.7 8.5 %all_to_all.62 = f32[8,1,4096]{2,1,0:T(1,128)S(1)} all-to-all(f32[8,1,4096]{2,1,0:T(1,128)S(1)} %copy.26), channel_id=1, replica_groups=mesh['aa'=8,'ba'=16] {'aa'}, dimensions={0} | all-to-all | bytes 262144 | tf_op jit(solution)/shard_map/all_to_all | solution.py:203
  107.3 4.5 %shard_map.58 = (f32[16,32,256]{2,1,0:T(8,128)S(1)}, f32[1,4096]{1,0:T(1,128)}) custom-call(f32[8,4096]{1,0:T(8,128)S(1)} %bitcast.22, f32[1,1024]{1,0:T(1,128)S(1)} %get-tuple-element.56.r_1_, f32[1024,256]{1,0:T(8,128)S(1)} %bitcast.20, bf16[4096,256]{1,0:T(8,128)(2,1)S(1)} %get-tuple-element.59.r_3_, bf16[4096,256]{1,0:T(8,128)(2,1)S(1)} %get-tuple-element.60.r_4_, ...), custom_call_target="tpu_custom_call" | custom-call | flops 3221225472 | bytes 4194304 | tf_op jit(solution)/shard_map/pallas_call | solution.py:178
  112.7 4.2 %all-to-all-start.5 = ((f32[16,32,256]{2,1,0:T(8,128)}), f32[16,32,256]{2,1,0:T(8,128)}, u32[]{:S(2)}, u32[]{:S(2)}) async-start(f32[16,32,256]{2,1,0:T(8,128)} %copy-done.5), calls=%async_computation.5 | async-start | bytes 1048576 | tf_op jit(solution)/shard_map/all_to_all | solution.py:203
  117.5 5.8 %copy-done.1 = f32[1024,4096]{1,0:T(8,128)S(1)} copy-done((f32[1024,4096]{1,0:T(8,128)S(1)}, f32[1024,4096]{1,0:T(8,128)}, u32[]{:S(2)}) %copy-start.1) | copy-done | bytes 16777240
  124.9 4.5 %shard_map.57 = (f32[16,32,256]{2,1,0:T(8,128)S(1)}, f32[1,4096]{1,0:T(1,128)S(1)}) custom-call(f32[8,4096]{1,0:T(8,128)S(1)} %bitcast.23, f32[1,1024]{1,0:T(1,128)S(1)} %get-tuple-element.56.r_1_, f32[1024,256]{1,0:T(8,128)S(1)} %bitcast.21, bf16[4096,256]{1,0:T(8,128)(2,1)S(1)} %get-tuple-element.59.r_3_, bf16[4096,256]{1,0:T(8,128)(2,1)S(1)} %copy-done.3, ...), custom_call_target="tpu_custom_call" | custom-call | flops 3221225472 | bytes 4194304 | tf_op jit(solution)/shard_map/pallas_call | solution.py:178
  130.2 7.1 %all-to-all-start.6 = ((f32[16,32,256]{2,1,0:T(8,128)}), f32[16,32,256]{2,1,0:T(8,128)S(1)}, u32[]{:S(2)}, u32[]{:S(2)}) async-start(f32[16,32,256]{2,1,0:T(8,128)} %copy-done.4), calls=%async_computation.6 | async-start | bytes 1048576 | tf_op jit(solution)/shard_map/all_to_all | solution.py:203
  139.0 9.3 %all-to-all-done.6 = f32[16,32,256]{2,1,0:T(8,128)S(1)} async-done(((f32[16,32,256]{2,1,0:T(8,128)}), f32[16,32,256]{2,1,0:T(8,128)S(1)}, u32[]{:S(2)}, u32[]{:S(2)}) %all-to-all-start.6) | async-done | bytes 524320 | tf_op jit(solution)/shard_map/all_to_all | solution.py:203
  (50 shorter events, 13.0 us)
Async XLA Ops:
  0.6 9.2 %copy-start.6 = (f32[512,256]{1,0:T(8,128)S(1)}, f32[512,256]{1,0:T(8,128)}, u32[]{:S(2)}) copy-start(f32[512,256]{1,0:T(8,128)} %r_1_.1) | copy-start | bytes 1572868
  2.7 32.9 %all-to-all-start = ((f32[16,64,256]{2,1,0:T(8,128)}), f32[16,64,256]{2,1,0:T(8,128)S(1)}, u32[]{:S(2)}, u32[]{:S(2)}) async-start(f32[16,64,256]{2,1,0:T(8,128)} %broadcast_in_dim.2), calls=%async_computation | async-start | bytes 2097152 | tf_op jit(solution)/shard_map/all_to_all | solution.py:209
  9.8 15.9 %collective-permute-start = (f32[512,256]{1,0:T(8,128)S(1)}, f32[512,256]{1,0:T(8,128)}, u32[]{:S(2)}, u32[]{:S(2)}) collective-permute-start(f32[512,256]{1,0:T(8,128)S(1)} %copy-done.6), channel_id=1, source_target_pairs={{0,32},{16,48},{32,64},{48,80},{64,96},{80,112},{96,0},{112,16},{1... | collective-permute-start | bytes 1572872 | tf_op jit(solution)/shard_map/ppermute | solution.py:218
  11.8 14.9 %collective-permute-start.2 = (f32[512,256]{1,0:T(8,128)S(1)}, f32[512,256]{1,0:T(8,128)}, u32[]{:S(2)}, u32[]{:S(2)}) collective-permute-start(f32[512,256]{1,0:T(8,128)S(1)} %copy-done.6), channel_id=1, source_target_pairs={{0,96},{16,112},{32,0},{48,16},{64,32},{80,48},{96,64},{112,80},{1... | collective-permute-start | bytes 1572872 | tf_op jit(solution)/shard_map/ppermute | solution.py:218
  14.0 21.9 %collective-permute-start.8 = (f32[512,256]{1,0:T(8,128)S(1)}, f32[512,256]{1,0:T(8,128)S(1)}, u32[]{:S(2)}, u32[]{:S(2)}) collective-permute-start(f32[512,256]{1,0:T(8,128)S(1)} %copy-done.6), channel_id=1, source_target_pairs={{0,16},{16,0},{32,48},{48,32},{64,80},{80,64},{96,112},{112,96},{1... | collective-permute-start | bytes 1572872 | tf_op jit(solution)/shard_map/ppermute | solution.py:221
  26.6 8.5 %collective-permute-start.1 = (f32[256,256]{1,0:T(8,128)S(1)}, f32[256,256]{1,0:T(8,128)S(1)}, u32[]{:S(2)}, u32[]{:S(2)}) collective-permute-start(f32[256,256]{1,0:T(8,128)S(1)} %slice.8), channel_id=1, source_target_pairs={{0,32},{16,48},{32,64},{48,80},{64,96},{80,112},{96,0},{112,16},{1... | collective-permute-start | bytes 786440 | tf_op jit(solution)/shard_map/ppermute | solution.py:218
  27.7 7.7 %collective-permute-start.3 = (f32[256,256]{1,0:T(8,128)S(1)}, f32[256,256]{1,0:T(8,128)}, u32[]{:S(2)}, u32[]{:S(2)}) collective-permute-start(f32[256,256]{1,0:T(8,128)S(1)} %slice.9), channel_id=1, source_target_pairs={{0,96},{16,112},{32,0},{48,16},{64,32},{80,48},{96,64},{112,80},{1... | collective-permute-start | bytes 786440 | tf_op jit(solution)/shard_map/ppermute | solution.py:218
  31.0 13.4 %collective-permute-start.6 = (f32[512,256]{1,0:T(8,128)}, f32[512,256]{1,0:T(8,128)}, u32[]{:S(2)}, u32[]{:S(2)}) collective-permute-start(f32[512,256]{1,0:T(8,128)} %collective-permute-done.r_1_), channel_id=1, source_target_pairs={{0,16},{16,0},{32,48},{48,32},{64,80},{80,64},{96,112},{112,96},{1... | collective-permute-start | bytes 1572872 | tf_op jit(solution)/shard_map/ppermute | solution.py:221
  31.0 13.4 %collective-permute-start.7 = (f32[512,256]{1,0:T(8,128)}, f32[512,256]{1,0:T(8,128)}, u32[]{:S(2)}, u32[]{:S(2)}) collective-permute-start(f32[512,256]{1,0:T(8,128)} %collective-permute-done.2.r_2_), channel_id=1, source_target_pairs={{0,16},{16,0},{32,48},{48,32},{64,80},{80,64},{96,112},{112,96},{1... | collective-permute-start | bytes 1572872 | tf_op jit(solution)/shard_map/ppermute | solution.py:221
  35.1 12.8 %collective-permute-start.4 = (f32[256,256]{1,0:T(8,128)S(1)}, f32[256,256]{1,0:T(8,128)}, u32[]{:S(2)}, u32[]{:S(2)}) collective-permute-start(f32[256,256]{1,0:T(8,128)S(1)} %collective-permute-done.1.r_1_), channel_id=1, source_target_pairs={{0,16},{16,0},{32,48},{48,32},{64,80},{80,64},{96,112},{112,96},{1... | collective-permute-start | bytes 786440 | tf_op jit(solution)/shard_map/ppermute | solution.py:221
  35.4 12.5 %collective-permute-start.5 = (f32[256,256]{1,0:T(8,128)}, f32[256,256]{1,0:T(8,128)}, u32[]{:S(2)}, u32[]{:S(2)}) collective-permute-start(f32[256,256]{1,0:T(8,128)} %collective-permute-done.3.r_2_), channel_id=1, source_target_pairs={{0,16},{16,0},{32,48},{48,32},{64,80},{80,64},{96,112},{112,96},{1... | collective-permute-start | bytes 786440 | tf_op jit(solution)/shard_map/ppermute | solution.py:221
  35.9 0.8 copy-start.8
  36.7 1.0 copy-start.7
  37.7 1.0 copy-start.9
  51.4 55.9 %copy-start = (f32[1024,4096]{1,0:T(8,128)}, f32[1024,4096]{1,0:T(8,128)S(1)}, u32[]{:S(2)}) copy-start(f32[1024,4096]{1,0:T(8,128)S(1)} %get-tuple-element.54.r_1_.r_5_) | copy-start | bytes 50331652
  51.4 55.9 %copy-start.2 = (bf16[4096,256]{1,0:T(8,128)(2,1)}, bf16[4096,256]{1,0:T(8,128)(2,1)S(1)}, u32[]{:S(2)}) copy-start(bf16[4096,256]{1,0:T(8,128)(2,1)S(1)} %get-tuple-element.60.r_4_) | copy-start | bytes 6291460
  111.9 0.8 copy-start.5
  112.7 17.5 %all-to-all-start.5 = ((f32[16,32,256]{2,1,0:T(8,128)}), f32[16,32,256]{2,1,0:T(8,128)}, u32[]{:S(2)}, u32[]{:S(2)}) async-start(f32[16,32,256]{2,1,0:T(8,128)} %copy-done.5), calls=%async_computation.5 | async-start | bytes 1048576 | tf_op jit(solution)/shard_map/all_to_all | solution.py:203
  117.5 5.8 %copy-start.1 = (f32[1024,4096]{1,0:T(8,128)S(1)}, f32[1024,4096]{1,0:T(8,128)}, u32[]{:S(2)}) copy-start(f32[1024,4096]{1,0:T(8,128)} %copy-done) | copy-start | bytes 50331652
  123.3 1.6 %copy-start.3 = (bf16[4096,256]{1,0:T(8,128)(2,1)S(1)}, bf16[4096,256]{1,0:T(8,128)(2,1)}, u32[]{:S(2)}) copy-start(bf16[4096,256]{1,0:T(8,128)(2,1)} %copy-done.2) | copy-start | bytes 6291460
  129.4 0.8 copy-start.4
  130.2 18.1 %all-to-all-start.6 = ((f32[16,32,256]{2,1,0:T(8,128)}), f32[16,32,256]{2,1,0:T(8,128)S(1)}, u32[]{:S(2)}, u32[]{:S(2)}) async-start(f32[16,32,256]{2,1,0:T(8,128)} %copy-done.4), calls=%async_computation.6 | async-start | bytes 1048576 | tf_op jit(solution)/shard_map/all_to_all | solution.py:203

commit v3 on v2

--- a/solution.py
+++ b/solution.py
@@ -111,9 +111,10 @@
     return xs[0]
 
 
-def col_pass_kernel(log_b, part_ref, s_ref, out_ref, alpha_ref, wide):
+def col_pass_kernel(log_b, eps, part_ref, a2_ref, s_ref, out_ref, alpha_ref, pot_ref, wide):
     alpha = -combine(part_ref[...]) - log_b
     alpha_ref[...] = alpha
+    pot_ref[...] = (alpha + a2_ref[...]) * (eps / LOG2E)
     wide[...] = jnp.broadcast_to(alpha, (LANES, alpha.shape[1])).T
     rows = s_ref.shape[0]
     piece, across = 64, 8
@@ -135,46 +136,52 @@
     lax.fori_loop(0, s_ref.shape[1] // (LANES * across), group, 0)
 
 
-def grad_kernel(log_a, log_b, start, part_ref, alpha_ref, a_ref, bhi_ref, blo_ref, s_ref, g_ref, beta_ref, awide, bwide, mass, acc):
+def weights_kernel(log_a, log_b, eps, part_ref, alpha_ref, b2_ref, awide_ref, bwide_ref, pot_ref):
     beta = -combine(part_ref[...]) - log_a
-    beta_ref[...] = beta
-    bwide[...] = jnp.broadcast_to(beta + log_b, bwide.shape)
-    awide[...] = jnp.broadcast_to(alpha_ref[...], (LANES, alpha_ref.shape[1])).T
-    shares, n = g_ref.shape[:2]
-    share = s_ref.shape[0] // shares
-    step, group = 1024, 256 // n
-
-    def take(ref, first, cols):
-        return jnp.concatenate([ref[pl.ds(d * share + start, n), cols] for d in range(first, first + group)], axis=0)
+    pot_ref[...] = (beta + b2_ref[...]) * (eps / LOG2E)
+    bwide_ref[...] = jnp.broadcast_to(beta + log_b, bwide_ref.shape)
+    awide_ref[...] = jnp.broadcast_to(alpha_ref[...], (LANES, alpha_ref.shape[1])).T
+
+
+def grad_kernel(first, awide_ref, bwide_ref, a_ref, bhi_ref, blo_ref, s_ref, g_ref, mass):
+    n = g_ref.shape[0]
+    rows = pl.ds(pl.multiple_of(first(), n), n)
+    step = 1024
 
     def chunk(k, begin):
         at = pl.ds(pl.multiple_of(k * step, step), step)
         hi_b, lo_b = bhi_ref[at, :], blo_ref[at, :]
         right = jnp.concatenate([hi_b, lo_b, hi_b], axis=0)
-        col = bwide[:, at][:1, :]
-        for first in range(0, shares, group):
-            rows = slice(first * n, (first + group) * n)
-            alpha = take(awide, first, slice(None))
-            p = jnp.exp2(take(s_ref, first, at) + jnp.concatenate([alpha] * (step // LANES), axis=1) + col)
-            part = tree(jnp.add, [p[:, q:q + LANES] for q in range(0, step, LANES)])
-            hi, lo = split(p)
-            left = jnp.concatenate([hi, hi, lo], axis=1)
-            pulled = jnp.dot(left, right, preferred_element_type=jnp.float32)
-            mass[rows, :] = part if begin else mass[rows, :] + part
-            acc[rows, :] = pulled if begin else acc[rows, :] + pulled
+        alpha = awide_ref[rows, :]
+        p = jnp.exp2(s_ref[rows, at] + jnp.concatenate([alpha] * (step // LANES), axis=1) + bwide_ref[:, at][:1, :])
+        part = tree(jnp.add, [p[:, q:q + LANES] for q in range(0, step, LANES)])
+        hi, lo = split(p)
+        left = jnp.concatenate([hi, hi, lo], axis=1)
+        pulled = jnp.dot(left, right, preferred_element_type=jnp.float32)
+        mass[...] = part if begin else mass[...] + part
+        g_ref[...] = pulled if begin else g_ref[...] + pulled
 
     chunk(0, True)
     lax.fori_loop(1, s_ref.shape[1] // step, lambda k, carry: chunk(k, False), None)
-    total = jnp.sum(mass[...], axis=1, keepdims=True)
-    for d in range(shares):
-        rows = slice(d * n, (d + 1) * n)
-        g_ref[d] = 2.0 * (a_ref[pl.ds(d * share + start, n), :] * total[rows] - acc[rows, :])
+    g_ref[...] = 2.0 * (a_ref[rows, :] * jnp.sum(mass[...], axis=1, keepdims=True) - g_ref[...])
+
+
+def turn_sum_kernel(order, *refs):
+    parts, outs = refs[:2], refs[2:]
+    n = outs[0].shape[0]
+    for out_ref, first in zip(outs, order()):
+        rows = pl.ds(pl.multiple_of(first * n, n), n)
+        out_ref[...] = tree(jnp.add, [part[rows, :] for part in parts])
+
+
+def sum_kernel(*refs):
+    refs[-1][...] = tree(jnp.add, [part[...] for part in refs[:-1]])
 
 
 VM = pl.BlockSpec(memory_space=pltpu.VMEM)
 
 
-def call(kernel, outs, scratch, *args, limit=12 * MIB, aliases={}, cost=None):
+def call(kernel, outs, scratch, *args, limit=6 * MIB, aliases={}, cost=None):
     return pl.pallas_call(
         kernel,
         out_shape=outs,
@@ -203,51 +210,35 @@
     return lax.all_to_all(x, axis, 0, 0, tiled=True)
 
 
-def gather_a(points_a):
-    size = lax.axis_size("ba")
-    wide = jnp.broadcast_to(points_a[None], (size,) + points_a.shape)
-    return lax.all_to_all(wide, "ba", 0, 0, tiled=True).reshape(size * points_a.shape[0], -1)
-
-
-def gather_b(points_b):
-    size = lax.axis_size("aa")
-    rows = points_b.shape[0]
-    half = rows // 2
-
-    def move(x, by):
-        return lax.ppermute(x, "aa", [(i, (i + 2 * by) % size) for i in range(size)])
-
-    def swap(x):
-        return lax.ppermute(x, "aa", [(i, i ^ 1) for i in range(size)])
-
-    def place(by, flip):
-        return lambda me: lax.rem(lax.bitwise_xor(me, flip) + 2 * by, size) * rows
-
-    up, down = move(points_b, 1), move(points_b, -1)
-    low, high = move(up[:half], 1), move(down[half:], -1)
-    def stage(*items):
-        return [(pieces, place(by, flip)) for pieces, by, flip in items]
-
-    up, down = move(points_b, 1), move(points_b, -1)
-    low, high = move(up[:half], 1), move(down[half:], -1)
-    return [
-        stage(([points_b], 0, 0), ([swap(points_b)], 0, 1)),
-        stage(([up], 3, 0), ([down], 1, 0)),
-        stage(([swap(up)], 3, 1), ([swap(down)], 1, 1)),
-        stage(([low, high], 2, 0), ([swap(low), swap(high)], 2, 1)),
-    ]
-
-
 def body(points_a, points_b):
-    stages = gather_b(points_b)
-    whole_a = gather_a(points_a)
-    rows_a, width = whole_a.shape
     na, nb = lax.axis_size("aa"), lax.axis_size("ba")
-    rows_b = points_b.shape[0] * na
+    share, width = points_a.shape
+    piece = points_b.shape[0]
+    rows_a, rows_b = share * nb, piece * na
     eps = width / 8.0
     log_a = -math.log2(rows_a * na)
     log_b = -math.log2(rows_b * nb)
-    left, a2 = call(lambda *r: prepare_kernel(eps, *r), [v16(rows_a, 3 * width), f32(1, rows_a)], [], whole_a)
+
+    def move(x, by):
+        return lax.ppermute(x, "aa", [(i, (i + 2 * by) % na) for i in range(na)])
+
+    def swap(x):
+        return lax.ppermute(x, "aa", [(i, i ^ 1) for i in range(na)])
+
+    def place(by, flip):
+        return lambda me: lax.rem(lax.bitwise_xor(me, flip) + 2 * by, na) * piece
+
+    half = piece // 2
+    up, down = move(points_b, 1), move(points_b, -1)
+    low, high = move(up[:half], 1), move(down[half:], -1)
+    wide = jnp.broadcast_to(points_a[None], (nb, share, width))
+    whole_a = spread(wide, "ba").reshape(rows_a, width)
+    stages = [
+        [([points_b], place(0, 0)), ([swap(points_b)], place(0, 1)),
+         ([up], place(3, 0)), ([down], place(1, 0)), ([swap(up)], place(3, 1)), ([swap(down)], place(1, 1)),
+         ([low, high], place(2, 0)), ([swap(low), swap(high)], place(2, 1))],
+    ]
+    left, a2 = call(lambda *r: prepare_kernel(eps, *r), [v16(rows_a, 3 * width), v32(1, rows_a)], [], whole_a)
     held = []
     for k, stage in enumerate(stages):
         places = [place for pieces, place in stage]
@@ -257,8 +248,8 @@
         outs = [v32(rows_a, rows_b), v16(rows_b, width), v16(rows_b, width), v32(1, rows_b), v32(rows_a, LANES), v32(rows_a, LANES)]
         held = call(
             lambda *r: scores_kernel(eps, places, sizes, k == 0, last, *r),
-            outs + ([f32(nb, rows_a)] if last else []),
-            [], left, *flat, *held,
+            outs + ([v32(nb, rows_a)] if last else []),
+            [], left, *flat, *held, limit=12 * MIB,
             aliases={1 + len(flat) + i: i for i in range(len(held))},
             cost=pl.CostEstimate(flops=6 * rows_a * width * sum(x.shape[0] for x in flat), bytes_accessed=4 * MIB, transcendentals=0))
     s, bhi, blo, b2, _, _, rows = held
@@ -269,27 +260,40 @@
                 [f32(nb, rows_a)],
                 [v32(8, rows_b), v32(rows_a, LANES), v32(rows_a, LANES)],
                 part, s)
-        cols, alpha = call(
-            lambda *r: col_pass_kernel(log_b, *r),
-            [f32(na, rows_b), f32(1, rows_a)],
+        cols, alpha, pot_a = call(
+            lambda *r: col_pass_kernel(log_b, eps, *r),
+            [f32(na, rows_b), v32(1, rows_a), f32(1, rows_a)],
             [v32(rows_a, LANES)],
-            spread(rows, "ba"), s)
+            spread(rows, "ba"), a2, s)
         part = spread(cols, "aa")
-    share = rows_a // nb
-    cut = share // 2
-    sums = []
-    for start in range(0, share, cut):
-        g, beta = call(
-            lambda *r: grad_kernel(log_a, log_b, start, *r),
-            [f32(nb, cut, width), f32(1, rows_b)],
-            [v32(rows_a, LANES), v32(8, rows_b), v32(nb * cut, LANES), v32(nb * cut, width)],
-            part, alpha, whole_a, bhi, blo, s,
-            cost=pl.CostEstimate(flops=6 * nb * cut * width * rows_b, bytes_accessed=4 * MIB, transcendentals=0))
-        sums.append(jnp.sum(spread(g, "ba"), axis=0))
-    scale = eps / LOG2E
-    pot_a = (scale * (alpha + a2)).reshape(rows_a)
-    pot_b = (scale * (beta + b2)).reshape(rows_b)
-    return (pot_a, pot_b, jnp.concatenate(sums, axis=0))
+    awide, bwide, pot_b = call(
+        lambda *r: weights_kernel(log_a, log_b, eps, *r),
+        [v32(rows_a, LANES), v32(8, rows_b), f32(1, rows_b)], [], part, alpha, b2)
+
+    def along_x(v, by):
+        return lax.ppermute(v, "ba", [(i, (i + side * by) % nb) for i in range(nb)])
+
+    def along_y(v, by):
+        return lax.ppermute(v, "ba", [(i, i // side * side + (i + by) % side) for i in range(nb)])
+
+    side = math.isqrt(nb)
+    step = pl.CostEstimate(flops=6 * rows_a // side * width * rows_b, bytes_accessed=4 * MIB, transcendentals=0)
+    held = []
+    for by in [*range(1, side), 0]:
+        g, = call(
+            lambda *r: grad_kernel(lambda: lax.rem(lax.axis_index("ba") // side + by, side) * (rows_a // side), *r),
+            [v32(rows_a // side, width)], [v32(rows_a // side, LANES)],
+            awide, bwide, whole_a, bhi, blo, s,
+            cost=step)
+        held.append(along_x(g, by) if by else g)
+    *arrived, total = held
+    for g in arrived[:-1]:
+        total, = call(sum_kernel, [v32(rows_a // side, width)], [], total, g, cost=step)
+    cuts = call(
+        lambda *r: turn_sum_kernel(lambda: [lax.rem(lax.rem(lax.axis_index("ba"), side) + by, side) for by in range(side)], *r),
+        [v32(share, width)] * side, [], total, arrived[-1])
+    grad, = call(sum_kernel, [f32(share, width)], [], cuts[0], *[along_y(cuts[by], by) for by in range(1, side)])
+    return (pot_a.reshape(rows_a), pot_b.reshape(rows_b), grad)
 
 
 def solution(mesh):

time: 150 us -> 125 us (0.83)
  local copies, waits for them, and re-layouts: 16.4 us -> 2.57 us
  starting transfers between devices: 26.8 us -> 23 us
  other arithmetic: 2.98 us -> 0 us
  blocking collectives: 44.3 us -> 41.9 us
  waiting for transfers between devices: 24.8 us -> 22.8 us
    unnamed x24 -> x6, local copies, waits for them, and re-layouts: 12.1 us -> 0.19 us
    ppermute x9 -> x15, starting transfers between devices: 8.27 us -> 16 us  [the longest x4 7.53 us: move(): return lax.ppermute(x, 'aa', [(i, (i + 2 * by) % na) for i in range(na)])]
    all_to_all x1 -> x0, starting transfers between devices: 7.12 us -> none  [gather_a(): lax.all_to_all(wide, 'ba', 0, 0, tiled=True)]
    all_to_all x2 -> x1, waiting for transfers between devices: 9.27 us -> 4.53 us  [spread(): return lax.all_to_all(x, axis, 0, 0, tiled=True)]
    all_to_all x2 -> x1, starting transfers between devices: 11.4 us -> 7.03 us  [spread(): return lax.all_to_all(x, axis, 0, 0, tiled=True)]
    ppermute x9 -> x15, waiting for transfers between devices: 15.6 us -> 18.3 us  [the longest x4 8.98 us: move(): return lax.ppermute(x, 'aa', [(i, (i + 2 * by) % na) for i in range(na)])]
    all_to_all x4, blocking collectives: 44.3 us -> 41.9 us  [spread(): return lax.all_to_all(x, axis, 0, 0, tiled=True)]
    slice x2, local copies, waits for them, and re-layouts: 1.94 us -> 0.04 us  [body(): low, high = (move(up[:half], 1), move(down[half:], -1))]
  transfers between devices with their start and end apart: 12 -> 16, of which waited for: 4 -> 9; matrix products, arithmetic and copies ran while one was open for 3% -> 2% of each run, Pallas kernels for 9% -> 4%
where the time goes in v3:
time: 125 us
  blocking collectives  41.9 us (34%)
  Pallas kernels  33.8 us (27%)
  starting transfers between devices  23 us (18%)
  waiting for transfers between devices  22.8 us (18%)
  local copies, waits for them, and re-layouts  2.57 us (2%)
    all_to_all x4, blocking collectives, spread(): return lax.all_to_all(x, axis, 0, 0, tiled=True)  41.9 us
    pallas_call x14, Pallas kernels, call(): pl.pallas_call(kernel, out_shape=outs, in_specs=[VM] * len(args), out_spe...  33.8 us
    ppermute x4, waiting for transfers between devices, move(): return lax.ppermute(x, 'aa', [(i, (i + 2 * by) % na) for i in range(na)])  8.98 us
    ppermute x4, starting transfers between devices, move(): return lax.ppermute(x, 'aa', [(i, (i + 2 * by) % na) for i in range(na)])  7.53 us
    all_to_all x1, starting transfers between devices, spread(): return lax.all_to_all(x, axis, 0, 0, tiled=True)  7.03 us
    ppermute x3, waiting for transfers between devices, along_x(): return lax.ppermute(v, 'ba', [(i, (i + side * by) % nb) for i in range(nb)])  6.25 us
    all_to_all x1, waiting for transfers between devices, spread(): return lax.all_to_all(x, axis, 0, 0, tiled=True)  4.53 us
    ppermute x3, starting transfers between devices, along_y(): lax.ppermute(v, 'ba', [(i, i // side * side + (i + by) % side) for i in r...  4.09 us
  transfers between devices with their start and end apart: 16, of which 9 were waited for; matrix products, arithmetic and copies ran while one was open for 2% of the time, Pallas kernels for 4%

profile of v3, /device:TPU:0, one launch (start us, length us, event | category | flops | bytes accessed | tf_op | source)
XLA Modules:
  0.0 125.0 jit_solution(14644351153047738427)
XLA Ops:
  0.6 2.1 %collective-permute-start.1 = (f32[512,256]{1,0:T(8,128)}, f32[512,256]{1,0:T(8,128)S(1)}, u32[]{:S(2)}, u32[]{:S(2)}) collective-permute-start(f32[512,256]{1,0:T(8,128)} %r_1_.1), channel_id=1, source_target_pairs={{0,32},{16,48},{32,64},{48,80},{64,96},{80,112},{96,0},{112,16},{1... | collective-permute-start | bytes 1572872 | tf_op jit(solution)/shard_map/ppermute | solution.py:223
  2.7 2.2 %collective-permute-start.2 = (f32[512,256]{1,0:T(8,128)}, f32[512,256]{1,0:T(8,128)S(1)}, u32[]{:S(2)}, u32[]{:S(2)}) collective-permute-start(f32[512,256]{1,0:T(8,128)} %r_1_.1), channel_id=1, source_target_pairs={{0,96},{16,112},{32,0},{48,16},{64,32},{80,48},{96,64},{112,80},{1... | collective-permute-start | bytes 1572872 | tf_op jit(solution)/shard_map/ppermute | solution.py:223
  4.9 1.9 %broadcast_in_dim.2 = f32[16,64,256]{2,1,0:T(8,128)} broadcast(f32[64,256]{1,0:T(8,128)} %param.2), dimensions={1,2} | broadcast | bytes 1114112 | tf_op jit(solution)/shard_map/broadcast_in_dim | solution.py:234
  6.8 7.0 %all-to-all-start = ((f32[16,64,256]{2,1,0:T(8,128)}), f32[16,64,256]{2,1,0:T(8,128)S(1)}, u32[]{:S(2)}, u32[]{:S(2)}) async-start(f32[16,64,256]{2,1,0:T(8,128)} %broadcast_in_dim.2), calls=%async_computation | async-start | bytes 2097152 | tf_op jit(solution)/shard_map/all_to_all | solution.py:210
  14.0 3.0 %collective-permute-done.1.r_3_ = f32[512,256]{1,0:T(8,128)S(1)} collective-permute-done((f32[512,256]{1,0:T(8,128)}, f32[512,256]{1,0:T(8,128)S(1)}, u32[]{:S(2)}, u32[]{:S(2)}) %collective-permute-start.1) | collective-permute-done | bytes 524320 | tf_op jit(solution)/shard_map/ppermute | solution.py:223
  17.2 3.2 %collective-permute-start.6 = (f32[256,256]{1,0:T(8,128)S(1)}, f32[256,256]{1,0:T(8,128)}, u32[]{:S(2)}, u32[]{:S(2)}) collective-permute-start(f32[256,256]{1,0:T(8,128)S(1)} %slice.9), channel_id=1, source_target_pairs={{0,96},{16,112},{32,0},{48,16},{64,32},{80,48},{96,64},{112,80},{1... | collective-permute-start | bytes 786440 | tf_op jit(solution)/shard_map/ppermute | solution.py:223
  20.6 5.1 %collective-permute-done.5.r_7_ = f32[256,256]{1,0:T(8,128)S(1)} collective-permute-done((f32[256,256]{1,0:T(8,128)S(1)}, f32[256,256]{1,0:T(8,128)S(1)}, u32[]{:S(2)}, u32[]{:S(2)}) %collective-permute-start.5) | collective-permute-done | bytes 262176 | tf_op jit(solution)/shard_map/ppermute | solution.py:223
  26.6 4.5 %all-to-all-done = f32[16,64,256]{2,1,0:T(8,128)S(1)} async-done(((f32[16,64,256]{2,1,0:T(8,128)}), f32[16,64,256]{2,1,0:T(8,128)S(1)}, u32[]{:S(2)}, u32[]{:S(2)}) %all-to-all-start) | async-done | bytes 1048608 | tf_op jit(solution)/shard_map/all_to_all | solution.py:210
  31.5 10.9 %shard_map.50 = (f32[1024,4096]{1,0:T(8,128)S(1)}, bf16[4096,256]{1,0:T(8,128)(2,1)S(1)}, bf16[4096,256]{1,0:T(8,128)(2,1)S(1)}, f32[1,4096]{1,0:T(1,128)S(1)}, ...) custom-call(bf16[1024,768]{1,0:T(8,128)(2,1)S(1)} %get-tuple-element.21.r_0_, ...), custom_call_target="tpu_custom_call" | custom-call | flops 6442450944 | bytes 4194304 | tf_op jit(solution)/shard_map/pallas_call | solution.py:185
  42.4 11.5 %all_to_all.49 = f32[16,1,1024]{2,1,0:T(1,128)S(1)} all-to-all(f32[16,1,1024]{2,1,0:T(1,128)S(1)} %copy.5), channel_id=1, replica_groups=mesh['aa'=8,'ba'=16] {'ba'}, dimensions={0} | all-to-all | bytes 131072 | tf_op jit(solution)/shard_map/all_to_all | solution.py:210
  54.0 3.8 %shard_map.51 = (f32[8,4096]{1,0:T(8,128)S(1)}, f32[1,1024]{1,0:T(1,128)}, f32[1,1024]{1,0:T(1,128)}) custom-call(f32[16,1024]{1,0:T(8,128)S(1)} %bitcast.26, f32[1,1024]{1,0:T(1,128)S(1)} %get-tuple-element.23.r_1_, f32[1024,4096]{1,0:T(8,128)S(1)} %get-tuple-element.24.r_2_.r_1_.r_5_), custom_call_target="tpu_custom_call" | custom-call | tf_op jit(solution)/shard_map/pallas_call | solution.py:185
  57.9 11.0 %all_to_all.50 = f32[8,1,4096]{2,1,0:T(1,128)S(1)} all-to-all(f32[8,1,4096]{2,1,0:T(1,128)S(1)} %copy.6), channel_id=1, replica_groups=mesh['aa'=8,'ba'=16] {'aa'}, dimensions={0} | all-to-all | bytes 262144 | tf_op jit(solution)/shard_map/all_to_all | solution.py:210
  69.0 3.4 %shard_map.52 = f32[16,1024]{1,0:T(8,128)S(1)} custom-call(f32[8,4096]{1,0:T(8,128)S(1)} %bitcast.24, f32[1024,4096]{1,0:T(8,128)S(1)} %get-tuple-element.24.r_2_.r_1_.r_5_), custom_call_target="tpu_custom_call" | custom-call | tf_op jit(solution)/shard_map/pallas_call | solution.py:185
  72.5 10.9 %all_to_all.51 = f32[16,1,1024]{2,1,0:T(1,128)S(1)} all-to-all(f32[16,1,1024]{2,1,0:T(1,128)S(1)} %copy.7), channel_id=1, replica_groups=mesh['aa'=8,'ba'=16] {'ba'}, dimensions={0} | all-to-all | bytes 131072 | tf_op jit(solution)/shard_map/all_to_all | solution.py:210
  83.4 3.9 %shard_map.53 = (f32[8,4096]{1,0:T(8,128)S(1)}, f32[1,1024]{1,0:T(1,128)S(1)}, f32[1,1024]{1,0:T(1,128)}) custom-call(f32[16,1024]{1,0:T(8,128)S(1)} %bitcast.27, f32[1,1024]{1,0:T(1,128)S(1)} %get-tuple-element.23.r_1_, f32[1024,4096]{1,0:T(8,128)S(1)} %get-tuple-element.24.r_2_.r_1_.r_5_), custom_call_target="tpu_custom_call" | custom-call | tf_op jit(solution)/shard_map/pallas_call | solution.py:185
  87.4 8.5 %all_to_all.52 = f32[8,1,4096]{2,1,0:T(1,128)S(1)} all-to-all(f32[8,1,4096]{2,1,0:T(1,128)S(1)} %copy.8), channel_id=1, replica_groups=mesh['aa'=8,'ba'=16] {'aa'}, dimensions={0} | all-to-all | bytes 262144 | tf_op jit(solution)/shard_map/all_to_all | solution.py:210
  96.9 2.5 %shard_map.58 = f32[256,256]{1,0:T(8,128)S(1)} custom-call(f32[1024,128]{1,0:T(8,128)S(1)} %get-tuple-element.31.r_0_, f32[8,4096]{1,0:T(8,128)S(1)} %get-tuple-element.32.r_1_, f32[1024,256]{1,0:T(8,128)S(1)} %bitcast.20, bf16[4096,256]{1,0:T(8,128)(2,1)S(1)} %get-tuple-element.33.r_3_, bf16[4096,256]{1,0:T(8,128)(2,1)S(1)} %get-tuple-element.34.r_4_, ...), custom_call_target="tpu_custom_call" | custom-call | flops 1610612736 | bytes 4194304 | tf_op jit(solution)/shard_map/pallas_call | solution.py:185
  99.4 2.5 %shard_map.56 = f32[256,256]{1,0:T(8,128)S(1)} custom-call(f32[1024,128]{1,0:T(8,128)S(1)} %get-tuple-element.31.r_0_, f32[8,4096]{1,0:T(8,128)S(1)} %get-tuple-element.32.r_1_, f32[1024,256]{1,0:T(8,128)S(1)} %bitcast.21, bf16[4096,256]{1,0:T(8,128)(2,1)S(1)} %get-tuple-element.33.r_3_, bf16[4096,256]{1,0:T(8,128)(2,1)S(1)} %get-tuple-element.34.r_4_, ...), custom_call_target="tpu_custom_call" | custom-call | flops 1610612736 | bytes 4194304 | tf_op jit(solution)/shard_map/pallas_call | solution.py:185
  102.5 2.1 %collective-permute-start.10 = (f32[256,256]{1,0:T(8,128)S(1)}, f32[256,256]{1,0:T(8,128)S(1)}, u32[]{:S(2)}, u32[]{:S(2)}) collective-permute-start(f32[256,256]{1,0:T(8,128)S(1)} %shard_map.58), channel_id=1, source_target_pairs={{0,8},{1,9},{2,10},{3,11},{4,12},{5,13},{6,14},{7,15},{8,0},{9,1},... | collective-permute-start | bytes 786440 | tf_op jit(solution)/shard_map/ppermute | solution.py:274
  104.5 2.5 %shard_map.60 = f32[256,256]{1,0:T(8,128)S(1)} custom-call(f32[1024,128]{1,0:T(8,128)S(1)} %get-tuple-element.31.r_0_, f32[8,4096]{1,0:T(8,128)S(1)} %get-tuple-element.32.r_1_, f32[1024,256]{1,0:T(8,128)S(1)} %bitcast.22, bf16[4096,256]{1,0:T(8,128)(2,1)S(1)} %get-tuple-element.33.r_3_, bf16[4096,256]{1,0:T(8,128)(2,1)S(1)} %get-tuple-element.34.r_4_, ...), custom_call_target="tpu_custom_call" | custom-call | flops 1610612736 | bytes 4194304 | tf_op jit(solution)/shard_map/pallas_call | solution.py:185
  108.4 2.5 %shard_map.55.refs_0_ = f32[256,256]{1,0:T(8,128)S(1)} custom-call(f32[1024,128]{1,0:T(8,128)S(1)} %get-tuple-element.31.r_0_, f32[8,4096]{1,0:T(8,128)S(1)} %get-tuple-element.32.r_1_, f32[1024,256]{1,0:T(8,128)S(1)} %bitcast.23, bf16[4096,256]{1,0:T(8,128)(2,1)S(1)} %get-tuple-element.33.r_3_, bf16[4096,256]{1,0:T(8,128)(2,1)S(1)} %get-tuple-element.34.r_4_, ...), custom_call_target="tpu_custom_call" | custom-call | flops 1610612736 | bytes 4194304 | tf_op jit(solution)/shard_map/pallas_call | solution.py:185
  110.9 5.7 %collective-permute-done.9.refs_1_ = f32[256,256]{1,0:T(8,128)S(1)} collective-permute-done((f32[256,256]{1,0:T(8,128)S(1)}, f32[256,256]{1,0:T(8,128)S(1)}, u32[]{:S(2)}, u32[]{:S(2)}) %collective-permute-start.9) | collective-permute-done | bytes 262176 | tf_op jit(solution)/shard_map/ppermute | solution.py:274
  117.9 2.2 %collective-permute-start.13 = (f32[64,256]{1,0:T(8,128)S(1)}, f32[64,256]{1,0:T(8,128)S(1)}, u32[]{:S(2)}, u32[]{:S(2)}) collective-permute-start(f32[64,256]{1,0:T(8,128)S(1)} %get-tuple-element.37), channel_id=1, source_target_pairs={{0,2},{1,3},{2,0},{3,1},{4,6},{5,7},{6,4},{7,5},{8,10},{9,11},{10,... | collective-permute-start | bytes 196616 | tf_op jit(solution)/shard_map/ppermute | solution.py:277
  121.3 1.5 %collective-permute-done.12.refs_1_ = f32[64,256]{1,0:T(8,128)S(1)} collective-permute-done((f32[64,256]{1,0:T(8,128)S(1)}, f32[64,256]{1,0:T(8,128)S(1)}, u32[]{:S(2)}, u32[]{:S(2)}) %collective-permute-start.12) | collective-permute-done | bytes 65568 | tf_op jit(solution)/shard_map/ppermute | solution.py:277
  (39 shorter events, 9.7 us)
Async XLA Ops:
  0.6 13.3 %copy-start = (f32[512,256]{1,0:T(8,128)S(1)}, f32[512,256]{1,0:T(8,128)}, u32[]{:S(2)}) copy-start(f32[512,256]{1,0:T(8,128)} %r_1_.1) | copy-start | bytes 1572868
  0.6 16.3 %collective-permute-start.1 = (f32[512,256]{1,0:T(8,128)}, f32[512,256]{1,0:T(8,128)S(1)}, u32[]{:S(2)}, u32[]{:S(2)}) collective-permute-start(f32[512,256]{1,0:T(8,128)} %r_1_.1), channel_id=1, source_target_pairs={{0,32},{16,48},{32,64},{48,80},{64,96},{80,112},{96,0},{112,16},{1... | collective-permute-start | bytes 1572872 | tf_op jit(solution)/shard_map/ppermute | solution.py:223
  2.7 14.5 %collective-permute-start.2 = (f32[512,256]{1,0:T(8,128)}, f32[512,256]{1,0:T(8,128)S(1)}, u32[]{:S(2)}, u32[]{:S(2)}) collective-permute-start(f32[512,256]{1,0:T(8,128)} %r_1_.1), channel_id=1, source_target_pairs={{0,96},{16,112},{32,0},{48,16},{64,32},{80,48},{96,64},{112,80},{1... | collective-permute-start | bytes 1572872 | tf_op jit(solution)/shard_map/ppermute | solution.py:223
  6.8 24.3 %all-to-all-start = ((f32[16,64,256]{2,1,0:T(8,128)}), f32[16,64,256]{2,1,0:T(8,128)S(1)}, u32[]{:S(2)}, u32[]{:S(2)}) async-start(f32[16,64,256]{2,1,0:T(8,128)} %broadcast_in_dim.2), calls=%async_computation | async-start | bytes 2097152 | tf_op jit(solution)/shard_map/all_to_all | solution.py:210
  13.9 17.6 %collective-permute-start = (f32[512,256]{1,0:T(8,128)S(1)}, f32[512,256]{1,0:T(8,128)S(1)}, u32[]{:S(2)}, u32[]{:S(2)}) collective-permute-start(f32[512,256]{1,0:T(8,128)S(1)} %copy-done), channel_id=1, source_target_pairs={{0,16},{16,0},{32,48},{48,32},{64,80},{80,64},{96,112},{112,96},{1... | collective-permute-start | bytes 1572872 | tf_op jit(solution)/shard_map/ppermute | solution.py:226
  17.0 8.8 %collective-permute-start.5 = (f32[256,256]{1,0:T(8,128)S(1)}, f32[256,256]{1,0:T(8,128)S(1)}, u32[]{:S(2)}, u32[]{:S(2)}) collective-permute-start(f32[256,256]{1,0:T(8,128)S(1)} %slice.8), channel_id=1, source_target_pairs={{0,32},{16,48},{32,64},{48,80},{64,96},{80,112},{96,0},{112,16},{1... | collective-permute-start | bytes 786440 | tf_op jit(solution)/shard_map/ppermute | solution.py:223
  17.1 14.4 %collective-permute-start.3 = (f32[512,256]{1,0:T(8,128)S(1)}, f32[512,256]{1,0:T(8,128)}, u32[]{:S(2)}, u32[]{:S(2)}) collective-permute-start(f32[512,256]{1,0:T(8,128)S(1)} %collective-permute-done.1.r_3_), channel_id=1, source_target_pairs={{0,16},{16,0},{32,48},{48,32},{64,80},{80,64},{96,112},{112,96},{1... | collective-permute-start | bytes 1572872 | tf_op jit(solution)/shard_map/ppermute | solution.py:226
  17.2 9.4 %collective-permute-start.6 = (f32[256,256]{1,0:T(8,128)S(1)}, f32[256,256]{1,0:T(8,128)}, u32[]{:S(2)}, u32[]{:S(2)}) collective-permute-start(f32[256,256]{1,0:T(8,128)S(1)} %slice.9), channel_id=1, source_target_pairs={{0,96},{16,112},{32,0},{48,16},{64,32},{80,48},{96,64},{112,80},{1... | collective-permute-start | bytes 786440 | tf_op jit(solution)/shard_map/ppermute | solution.py:223
  20.4 11.1 %collective-permute-start.4 = (f32[512,256]{1,0:T(8,128)S(1)}, f32[512,256]{1,0:T(8,128)}, u32[]{:S(2)}, u32[]{:S(2)}) collective-permute-start(f32[512,256]{1,0:T(8,128)S(1)} %collective-permute-done.2.r_4_), channel_id=1, source_target_pairs={{0,16},{16,0},{32,48},{48,32},{64,80},{80,64},{96,112},{112,96},{1... | collective-permute-start | bytes 1572872 | tf_op jit(solution)/shard_map/ppermute | solution.py:226
  25.8 5.7 %collective-permute-start.7 = (f32[256,256]{1,0:T(8,128)S(1)}, f32[256,256]{1,0:T(8,128)}, u32[]{:S(2)}, u32[]{:S(2)}) collective-permute-start(f32[256,256]{1,0:T(8,128)S(1)} %collective-permute-done.5.r_7_), channel_id=1, source_target_pairs={{0,16},{16,0},{32,48},{48,32},{64,80},{80,64},{96,112},{112,96},{1... | collective-permute-start | bytes 786440 | tf_op jit(solution)/shard_map/ppermute | solution.py:226
  26.6 4.9 %collective-permute-start.8 = (f32[256,256]{1,0:T(8,128)}, f32[256,256]{1,0:T(8,128)}, u32[]{:S(2)}, u32[]{:S(2)}) collective-permute-start(f32[256,256]{1,0:T(8,128)} %collective-permute-done.6.r_8_), channel_id=1, source_target_pairs={{0,16},{16,0},{32,48},{48,32},{64,80},{80,64},{96,112},{112,96},{1... | collective-permute-start | bytes 786440 | tf_op jit(solution)/shard_map/ppermute | solution.py:226
  101.9 14.8 %collective-permute-start.9 = (f32[256,256]{1,0:T(8,128)S(1)}, f32[256,256]{1,0:T(8,128)S(1)}, u32[]{:S(2)}, u32[]{:S(2)}) collective-permute-start(f32[256,256]{1,0:T(8,128)S(1)} %shard_map.56), channel_id=1, source_target_pairs={{0,4},{1,5},{2,6},{3,7},{4,8},{5,9},{6,10},{7,11},{8,12},{9,13},{1... | collective-permute-start | bytes 786440 | tf_op jit(solution)/shard_map/ppermute | solution.py:274
  102.5 14.2 %collective-permute-start.10 = (f32[256,256]{1,0:T(8,128)S(1)}, f32[256,256]{1,0:T(8,128)S(1)}, u32[]{:S(2)}, u32[]{:S(2)}) collective-permute-start(f32[256,256]{1,0:T(8,128)S(1)} %shard_map.58), channel_id=1, source_target_pairs={{0,8},{1,9},{2,10},{3,11},{4,12},{5,13},{6,14},{7,15},{8,0},{9,1},... | collective-permute-start | bytes 786440 | tf_op jit(solution)/shard_map/ppermute | solution.py:274
  107.0 10.2 %collective-permute-start.11 = (f32[256,256]{1,0:T(8,128)S(1)}, f32[256,256]{1,0:T(8,128)S(1)}, u32[]{:S(2)}, u32[]{:S(2)}) collective-permute-start(f32[256,256]{1,0:T(8,128)S(1)} %shard_map.60), channel_id=1, source_target_pairs={{0,12},{1,13},{2,14},{3,15},{4,0},{5,1},{6,2},{7,3},{8,4},{9,5},{1... | collective-permute-start | bytes 786440 | tf_op jit(solution)/shard_map/ppermute | solution.py:274
  117.2 5.5 %collective-permute-start.12 = (f32[64,256]{1,0:T(8,128)S(1)}, f32[64,256]{1,0:T(8,128)S(1)}, u32[]{:S(2)}, u32[]{:S(2)}) collective-permute-start(f32[64,256]{1,0:T(8,128)S(1)} %get-tuple-element.36), channel_id=1, source_target_pairs={{0,1},{1,2},{2,3},{3,0},{4,5},{5,6},{6,7},{7,4},{8,9},{9,10},{10,1... | collective-permute-start | bytes 196616 | tf_op jit(solution)/shard_map/ppermute | solution.py:277
  117.9 5.8 %collective-permute-start.13 = (f32[64,256]{1,0:T(8,128)S(1)}, f32[64,256]{1,0:T(8,128)S(1)}, u32[]{:S(2)}, u32[]{:S(2)}) collective-permute-start(f32[64,256]{1,0:T(8,128)S(1)} %get-tuple-element.37), channel_id=1, source_target_pairs={{0,2},{1,3},{2,0},{3,1},{4,6},{5,7},{6,4},{7,5},{8,10},{9,11},{10,... | collective-permute-start | bytes 196616 | tf_op jit(solution)/shard_map/ppermute | solution.py:277
  120.0 4.3 %collective-permute-start.14 = (f32[64,256]{1,0:T(8,128)S(1)}, f32[64,256]{1,0:T(8,128)S(1)}, u32[]{:S(2)}, u32[]{:S(2)}) collective-permute-start(f32[64,256]{1,0:T(8,128)S(1)} %get-tuple-element.38), channel_id=1, source_target_pairs={{0,3},{1,0},{2,1},{3,2},{4,7},{5,4},{6,5},{7,6},{8,11},{9,8},{10,9... | collective-permute-start | bytes 196616 | tf_op jit(solution)/shard_map/ppermute | solution.py:277

commit v4 on v3

--- a/solution.py
+++ b/solution.py
@@ -31,6 +31,11 @@
     return top + jnp.log2(jnp.sum(jnp.exp2(parts - top), axis=0, keepdims=True))
 
 
+def repeat_kernel(a_ref, out_ref):
+    for d in range(out_ref.shape[0]):
+        out_ref[d] = a_ref[...]
+
+
 def prepare_kernel(eps, a_ref, left_ref, a2_ref):
     x = a_ref[...]
     a2_ref[...] = row_norms(x) * (LOG2E / eps)
@@ -38,36 +43,34 @@
     left_ref[...] = jnp.concatenate([hi, hi, lo], axis=1)
 
 
-def scores_kernel(eps, places, sizes, fresh, last, left, *refs):
-    pieces, refs = refs[:sum(sizes)], refs[sum(sizes) + (0 if fresh else 6):]
-    s_ref, bhi_ref, blo_ref, b2_ref, top_ref, tot_ref = refs[:6]
+def pieces_kernel(eps, places, *refs):
+    pieces, (bhi_ref, blo_ref, b2_ref) = refs[:len(places)], refs[-3:]
     me = lax.axis_index("aa")
-    dims = (((1,), (1,)), ((), ()))
-    for place, size in zip(places, sizes):
-        y = jnp.concatenate([ref[...] for ref in pieces[:size]], axis=0)
-        pieces = pieces[size:]
+    for ref, place in zip(pieces, places):
+        y = ref[...]
         at = pl.ds(pl.multiple_of(place(me), y.shape[0]), y.shape[0])
-        norms = row_norms(y) * (LOG2E / eps)
-        b2_ref[:, at] = norms
-        hi, lo = split(y)
-        bhi_ref[at, :] = hi
-        blo_ref[at, :] = lo
+        b2_ref[:, at] = row_norms(y) * (LOG2E / eps)
+        bhi_ref[at, :], blo_ref[at, :] = split(y)
+
+
+def scores_kernel(n, left, bhi_ref, blo_ref, b2_ref, s_ref, out_ref, top_ref, tot_ref):
+    for start in range(0, s_ref.shape[1], n):
+        at = pl.ds(start, n)
+        hi, lo = bhi_ref[at, :], blo_ref[at, :]
         right = jnp.concatenate([hi, lo, hi], axis=1)
-        x = lax.dot_general(left[...], right, dims, preferred_element_type=jnp.float32)
+        x = lax.dot_general(left[...], right, (((1,), (1,)), ((), ())), preferred_element_type=jnp.float32)
         s_ref[:, at] = x
-        x = x - norms
-        parts = [x[:, k:k + LANES] for k in range(0, y.shape[0], LANES)]
+        x = x - b2_ref[:, at]
+        parts = [x[:, k:k + LANES] for k in range(0, n, LANES)]
         top = tree(jnp.maximum, parts)
-        if fresh:
+        if start == 0:
             tot_ref[...] = tree(jnp.add, [jnp.exp2(v - top) for v in parts])
         else:
             old = top_ref[...]
             top = jnp.maximum(old, top)
             tot_ref[...] = tot_ref[...] * jnp.exp2(old - top) + tree(jnp.add, [jnp.exp2(v - top) for v in parts])
         top_ref[...] = top
-        fresh = False
-    if last:
-        finish_rows(top_ref, tot_ref, refs[6])
+    finish_rows(top_ref, tot_ref, out_ref)
 
 
 def finish_rows(top_ref, tot_ref, out_ref):
@@ -148,8 +151,8 @@
     rows = pl.ds(pl.multiple_of(first(), n), n)
     step = 1024
 
-    def chunk(k, begin):
-        at = pl.ds(pl.multiple_of(k * step, step), step)
+    for start in range(0, s_ref.shape[1], step):
+        at = pl.ds(start, step)
         hi_b, lo_b = bhi_ref[at, :], blo_ref[at, :]
         right = jnp.concatenate([hi_b, lo_b, hi_b], axis=0)
         alpha = awide_ref[rows, :]
@@ -158,11 +161,8 @@
         hi, lo = split(p)
         left = jnp.concatenate([hi, hi, lo], axis=1)
         pulled = jnp.dot(left, right, preferred_element_type=jnp.float32)
-        mass[...] = part if begin else mass[...] + part
-        g_ref[...] = pulled if begin else g_ref[...] + pulled
-
-    chunk(0, True)
-    lax.fori_loop(1, s_ref.shape[1] // step, lambda k, carry: chunk(k, False), None)
+        mass[...] = part if start == 0 else mass[...] + part
+        g_ref[...] = pulled if start == 0 else g_ref[...] + pulled
     g_ref[...] = 2.0 * (a_ref[rows, :] * jnp.sum(mass[...], axis=1, keepdims=True) - g_ref[...])
 
 
@@ -225,34 +225,27 @@
     def swap(x):
         return lax.ppermute(x, "aa", [(i, i ^ 1) for i in range(na)])
 
-    def place(by, flip):
-        return lambda me: lax.rem(lax.bitwise_xor(me, flip) + 2 * by, na) * piece
+    def place(by, flip, start=0):
+        return lambda me: lax.rem(lax.bitwise_xor(me, flip) + 2 * by, na) * piece + start
 
     half = piece // 2
     up, down = move(points_b, 1), move(points_b, -1)
     low, high = move(up[:half], 1), move(down[half:], -1)
-    wide = jnp.broadcast_to(points_a[None], (nb, share, width))
+    wide, = call(repeat_kernel, [f32(nb, share, width)], [], points_a)
     whole_a = spread(wide, "ba").reshape(rows_a, width)
-    stages = [
-        [([points_b], place(0, 0)), ([swap(points_b)], place(0, 1)),
-         ([up], place(3, 0)), ([down], place(1, 0)), ([swap(up)], place(3, 1)), ([swap(down)], place(1, 1)),
-         ([low, high], place(2, 0)), ([swap(low), swap(high)], place(2, 1))],
-    ]
+    pieces = [
+        (points_b, place(0, 0)), (up, place(3, 0)), (down, place(1, 0)), (low, place(2, 0)), (high, place(2, 0, half)),
+        (swap(points_b), place(0, 1)), (swap(up), place(3, 1)), (swap(down), place(1, 1)),
+        (swap(low), place(2, 1)), (swap(high), place(2, 1, half))]
+    bhi, blo, b2 = call(
+        lambda *r: pieces_kernel(eps, [p for x, p in pieces], *r),
+        [v16(rows_b, width), v16(rows_b, width), v32(1, rows_b)], [], *[x for x, p in pieces],
+        cost=pl.CostEstimate(flops=0, bytes_accessed=64 * MIB, transcendentals=0))
     left, a2 = call(lambda *r: prepare_kernel(eps, *r), [v16(rows_a, 3 * width), v32(1, rows_a)], [], whole_a)
-    held = []
-    for k, stage in enumerate(stages):
-        places = [place for pieces, place in stage]
-        sizes = [len(pieces) for pieces, place in stage]
-        flat = [x for pieces, place in stage for x in pieces]
-        last = k == len(stages) - 1
-        outs = [v32(rows_a, rows_b), v16(rows_b, width), v16(rows_b, width), v32(1, rows_b), v32(rows_a, LANES), v32(rows_a, LANES)]
-        held = call(
-            lambda *r: scores_kernel(eps, places, sizes, k == 0, last, *r),
-            outs + ([v32(nb, rows_a)] if last else []),
-            [], left, *flat, *held, limit=12 * MIB,
-            aliases={1 + len(flat) + i: i for i in range(len(held))},
-            cost=pl.CostEstimate(flops=6 * rows_a * width * sum(x.shape[0] for x in flat), bytes_accessed=4 * MIB, transcendentals=0))
-    s, bhi, blo, b2, _, _, rows = held
+    s, rows = call(
+        lambda *r: scores_kernel(piece, *r),
+        [v32(rows_a, rows_b), v32(nb, rows_a)], [v32(rows_a, LANES), v32(rows_a, LANES)],
+        left, bhi, blo, b2, limit=8 * MIB)
     for turn in range(ITERS):
         if turn > 0:
             rows, = call(
@@ -277,18 +270,18 @@
         return lax.ppermute(v, "ba", [(i, i // side * side + (i + by) % side) for i in range(nb)])
 
     side = math.isqrt(nb)
-    step = pl.CostEstimate(flops=6 * rows_a // side * width * rows_b, bytes_accessed=4 * MIB, transcendentals=0)
+    step = pl.CostEstimate(flops=2 * rows_a // side * width * rows_b, bytes_accessed=MIB, transcendentals=0)
     held = []
     for by in [*range(1, side), 0]:
         g, = call(
             lambda *r: grad_kernel(lambda: lax.rem(lax.axis_index("ba") // side + by, side) * (rows_a // side), *r),
             [v32(rows_a // side, width)], [v32(rows_a // side, LANES)],
-            awide, bwide, whole_a, bhi, blo, s,
-            cost=step)
+            awide, bwide, whole_a, bhi, blo, s, limit=12 * MIB, cost=step)
         held.append(along_x(g, by) if by else g)
     *arrived, total = held
+    long = pl.CostEstimate(flops=9 * step.flops, bytes_accessed=4 * MIB, transcendentals=0)
     for g in arrived[:-1]:
-        total, = call(sum_kernel, [v32(rows_a // side, width)], [], total, g, cost=step)
+        total, = call(sum_kernel, [v32(rows_a // side, width)], [], total, g, cost=long)
     cuts = call(
         lambda *r: turn_sum_kernel(lambda: [lax.rem(lax.rem(lax.axis_index("ba"), side) + by, side) for by in range(side)], *r),
         [v32(share, width)] * side, [], total, arrived[-1])

time: 125 us -> 123 us (0.984)
  Pallas kernels: 33.8 us -> 31.6 us
    pallas_call x14 -> x16, Pallas kernels: 33.8 us -> 31.6 us  [call(): pl.pallas_call(kernel, out_shape=outs, in_specs=[VM] * len(args), out_spe...]
    broadcast_in_dim x1 -> x0, local copies, waits for them, and re-layouts: 1.93 us -> none  [body(): wide = jnp.broadcast_to(points_a[None], (nb, share, width))]
  transfers between devices with their start and end apart: 16 -> 16, of which waited for: 9 -> 9; matrix products, arithmetic and copies ran while one was open for 2% -> 0% of each run, Pallas kernels for 4% -> 6%
where the time goes in v4:
time: 123 us
  blocking collectives  41.9 us (34%)
  Pallas kernels  31.6 us (26%)
  starting transfers between devices  23.6 us (19%)
  waiting for transfers between devices  23.5 us (19%)
  local copies, waits for them, and re-layouts  1.48 us (1%)
    all_to_all x4, blocking collectives, spread(): return lax.all_to_all(x, axis, 0, 0, tiled=True)  41.9 us
    pallas_call x16, Pallas kernels, call(): pl.pallas_call(kernel, out_shape=outs, in_specs=[VM] * len(args), out_spe...  31.6 us
    ppermute x4, waiting for transfers between devices, move(): return lax.ppermute(x, 'aa', [(i, (i + 2 * by) % na) for i in range(na)])  8.72 us
    ppermute x4, starting transfers between devices, move(): return lax.ppermute(x, 'aa', [(i, (i + 2 * by) % na) for i in range(na)])  7.56 us
    ppermute x3, waiting for transfers between devices, along_x(): return lax.ppermute(v, 'ba', [(i, (i + side * by) % nb) for i in range(nb)])  7.24 us
    all_to_all x1, starting transfers between devices, spread(): return lax.all_to_all(x, axis, 0, 0, tiled=True)  7.03 us
    all_to_all x1, waiting for transfers between devices, spread(): return lax.all_to_all(x, axis, 0, 0, tiled=True)  4.5 us
    ppermute x3, starting transfers between devices, along_x(): return lax.ppermute(v, 'ba', [(i, (i + side * by) % nb) for i in range(nb)])  4.27 us
  transfers between devices with their start and end apart: 16, of which 9 were waited for; matrix products, arithmetic and copies ran while one was open for 0% of the time, Pallas kernels for 6%

profile of v4, /device:TPU:0, one launch (start us, length us, event | category | flops | bytes accessed | tf_op | source)
XLA Modules:
  0.0 122.9 jit_solution(3837797863829062456)
XLA Ops:
  0.6 2.1 %collective-permute-start = (f32[512,256]{1,0:T(8,128)}, f32[512,256]{1,0:T(8,128)S(1)}, u32[]{:S(2)}, u32[]{:S(2)}) collective-permute-start(f32[512,256]{1,0:T(8,128)} %r_0_.1), channel_id=1, source_target_pairs={{0,32},{16,48},{32,64},{48,80},{64,96},{80,112},{96,0},{112,16},{1... | collective-permute-start | bytes 1572872 | tf_op jit(solution)/shard_map/ppermute | solution.py:223
  2.7 2.2 %collective-permute-start.1 = (f32[512,256]{1,0:T(8,128)}, f32[512,256]{1,0:T(8,128)S(1)}, u32[]{:S(2)}, u32[]{:S(2)}) collective-permute-start(f32[512,256]{1,0:T(8,128)} %r_0_.1), channel_id=1, source_target_pairs={{0,96},{16,112},{32,0},{48,16},{64,32},{80,48},{96,64},{112,80},{1... | collective-permute-start | bytes 1572872 | tf_op jit(solution)/shard_map/ppermute | solution.py:223
  6.8 7.0 %all-to-all-start = ((f32[16,64,256]{2,1,0:T(8,128)}), f32[16,64,256]{2,1,0:T(8,128)S(1)}, u32[]{:S(2)}, u32[]{:S(2)}) async-start(f32[16,64,256]{2,1,0:T(8,128)} %shard_map.49), calls=%async_computation | async-start | bytes 2097152 | tf_op jit(solution)/shard_map/all_to_all | solution.py:210
  14.0 3.0 %collective-permute-done.r_1_ = f32[512,256]{1,0:T(8,128)S(1)} collective-permute-done((f32[512,256]{1,0:T(8,128)}, f32[512,256]{1,0:T(8,128)S(1)}, u32[]{:S(2)}, u32[]{:S(2)}) %collective-permute-start) | collective-permute-done | bytes 524320 | tf_op jit(solution)/shard_map/ppermute | solution.py:223
  17.7 3.2 %collective-permute-start.3 = (f32[256,256]{1,0:T(8,128)S(1)}, f32[256,256]{1,0:T(8,128)}, u32[]{:S(2)}, u32[]{:S(2)}) collective-permute-start(f32[256,256]{1,0:T(8,128)S(1)} %slice.9), channel_id=1, source_target_pairs={{0,96},{16,112},{32,0},{48,16},{64,32},{80,48},{96,64},{112,80},{1... | collective-permute-start | bytes 786440 | tf_op jit(solution)/shard_map/ppermute | solution.py:223
  20.9 4.9 %collective-permute-done.2.r_3_ = f32[256,256]{1,0:T(8,128)S(1)} collective-permute-done((f32[256,256]{1,0:T(8,128)S(1)}, f32[256,256]{1,0:T(8,128)S(1)}, u32[]{:S(2)}, u32[]{:S(2)}) %collective-permute-start.2) | collective-permute-done | bytes 262176 | tf_op jit(solution)/shard_map/ppermute | solution.py:223
  26.6 4.5 %all-to-all-done = f32[16,64,256]{2,1,0:T(8,128)S(1)} async-done(((f32[16,64,256]{2,1,0:T(8,128)}), f32[16,64,256]{2,1,0:T(8,128)S(1)}, u32[]{:S(2)}, u32[]{:S(2)}) %all-to-all-start) | async-done | bytes 1048608 | tf_op jit(solution)/shard_map/all_to_all | solution.py:210
  31.5 2.5 %shard_map.51 = (bf16[4096,256]{1,0:T(8,128)(2,1)S(1)}, bf16[4096,256]{1,0:T(8,128)(2,1)S(1)}, f32[1,4096]{1,0:T(1,128)S(1)}) custom-call(f32[512,256]{1,0:T(8,128)S(1)} %copy-done, f32[512,256]{1,0:T(8,128)S(1)} %collective-permute-done.r_1_, f32[512,256]{1,0:T(8,128)S(1)} %collective-permute-done.1.r_2_, f32[256,256]{1,0:T(8,128)S(1)} %collective-permute-done.2.r_3_, ...), custom_call_target="tpu_custom_call" | custom-call | bytes 67108864 | tf_op jit(solution)/shard_map/pallas_call | solution.py:185
  33.9 7.5 %shard_map.52 = (f32[1024,4096]{1,0:T(8,128)S(1)}, f32[16,1024]{1,0:T(8,128)S(1)}) custom-call(bf16[1024,768]{1,0:T(8,128)(2,1)S(1)} %get-tuple-element.21.r_0_, bf16[4096,256]{1,0:T(8,128)(2,1)S(1)} %get-tuple-element.22.r_1_.r_3_, bf16[4096,256]{1,0:T(8,128)(2,1)S(1)} %get-tuple-element.23.r_2_.r_4_, f32[1,4096]{1,0:T(1,128)S(1)} %get-tuple-element.24.r_3_.r_2_), custom_call_target="tpu_custom_call" | custom-call | tf_op jit(solution)/shard_map/pallas_call | solution.py:185
  41.5 11.5 %all_to_all.49 = f32[16,1,1024]{2,1,0:T(1,128)S(1)} all-to-all(f32[16,1,1024]{2,1,0:T(1,128)S(1)} %copy.5), channel_id=1, replica_groups=mesh['aa'=8,'ba'=16] {'ba'}, dimensions={0} | all-to-all | bytes 131072 | tf_op jit(solution)/shard_map/all_to_all | solution.py:210
  53.0 3.8 %shard_map.53 = (f32[8,4096]{1,0:T(8,128)S(1)}, f32[1,1024]{1,0:T(1,128)}, f32[1,1024]{1,0:T(1,128)}) custom-call(f32[16,1024]{1,0:T(8,128)S(1)} %bitcast.26, f32[1,1024]{1,0:T(1,128)S(1)} %get-tuple-element.26.r_1_, f32[1024,4096]{1,0:T(8,128)S(1)} %get-tuple-element.27.r_2_.r_1_.r_5_), custom_call_target="tpu_custom_call" | custom-call | tf_op jit(solution)/shard_map/pallas_call | solution.py:185
  56.9 11.0 %all_to_all.50 = f32[8,1,4096]{2,1,0:T(1,128)S(1)} all-to-all(f32[8,1,4096]{2,1,0:T(1,128)S(1)} %copy.6), channel_id=1, replica_groups=mesh['aa'=8,'ba'=16] {'aa'}, dimensions={0} | all-to-all | bytes 262144 | tf_op jit(solution)/shard_map/all_to_all | solution.py:210
  68.0 3.4 %shard_map.54 = f32[16,1024]{1,0:T(8,128)S(1)} custom-call(f32[8,4096]{1,0:T(8,128)S(1)} %bitcast.24, f32[1024,4096]{1,0:T(8,128)S(1)} %get-tuple-element.27.r_2_.r_1_.r_5_), custom_call_target="tpu_custom_call" | custom-call | tf_op jit(solution)/shard_map/pallas_call | solution.py:185
  71.5 10.9 %all_to_all.51 = f32[16,1,1024]{2,1,0:T(1,128)S(1)} all-to-all(f32[16,1,1024]{2,1,0:T(1,128)S(1)} %copy.7), channel_id=1, replica_groups=mesh['aa'=8,'ba'=16] {'ba'}, dimensions={0} | all-to-all | bytes 131072 | tf_op jit(solution)/shard_map/all_to_all | solution.py:210
  82.4 3.9 %shard_map.55 = (f32[8,4096]{1,0:T(8,128)S(1)}, f32[1,1024]{1,0:T(1,128)S(1)}, f32[1,1024]{1,0:T(1,128)}) custom-call(f32[16,1024]{1,0:T(8,128)S(1)} %bitcast.27, f32[1,1024]{1,0:T(1,128)S(1)} %get-tuple-element.26.r_1_, f32[1024,4096]{1,0:T(8,128)S(1)} %get-tuple-element.27.r_2_.r_1_.r_5_), custom_call_target="tpu_custom_call" | custom-call | tf_op jit(solution)/shard_map/pallas_call | solution.py:185
  86.5 8.5 %all_to_all.52 = f32[8,1,4096]{2,1,0:T(1,128)S(1)} all-to-all(f32[8,1,4096]{2,1,0:T(1,128)S(1)} %copy.8), channel_id=1, replica_groups=mesh['aa'=8,'ba'=16] {'aa'}, dimensions={0} | all-to-all | bytes 262144 | tf_op jit(solution)/shard_map/all_to_all | solution.py:210
  95.9 1.9 %shard_map.58 = f32[256,256]{1,0:T(8,128)S(1)} custom-call(f32[1024,128]{1,0:T(8,128)S(1)} %get-tuple-element.33.r_0_, f32[8,4096]{1,0:T(8,128)S(1)} %get-tuple-element.34.r_1_, f32[1024,256]{1,0:T(8,128)S(1)} %bitcast.20, bf16[4096,256]{1,0:T(8,128)(2,1)S(1)} %get-tuple-element.22.r_1_.r_3_, bf16[4096,256]{1,0:T(8,128)(2,1)S(1)} %get-tuple-element.23.r_2_.r_4_, ...), custom_call_target="tpu_custom_call" | custom-call | flops 536870912 | bytes 1048576 | tf_op jit(solution)/shard_map/pallas_call | solution.py:185
  98.4 1.9 %shard_map.60 = f32[256,256]{1,0:T(8,128)S(1)} custom-call(f32[1024,128]{1,0:T(8,128)S(1)} %get-tuple-element.33.r_0_, f32[8,4096]{1,0:T(8,128)S(1)} %get-tuple-element.34.r_1_, f32[1024,256]{1,0:T(8,128)S(1)} %bitcast.21, bf16[4096,256]{1,0:T(8,128)(2,1)S(1)} %get-tuple-element.22.r_1_.r_3_, bf16[4096,256]{1,0:T(8,128)(2,1)S(1)} %get-tuple-element.23.r_2_.r_4_, ...), custom_call_target="tpu_custom_call" | custom-call | flops 536870912 | bytes 1048576 | tf_op jit(solution)/shard_map/pallas_call | solution.py:185
  100.3 2.1 %collective-permute-start.10 = (f32[256,256]{1,0:T(8,128)S(1)}, f32[256,256]{1,0:T(8,128)S(1)}, u32[]{:S(2)}, u32[]{:S(2)}) collective-permute-start(f32[256,256]{1,0:T(8,128)S(1)} %shard_map.60), channel_id=1, source_target_pairs={{0,8},{1,9},{2,10},{3,11},{4,12},{5,13},{6,14},{7,15},{8,0},{9,1},... | collective-permute-start | bytes 786440 | tf_op jit(solution)/shard_map/ppermute | solution.py:267
  102.4 1.9 %shard_map.62 = f32[256,256]{1,0:T(8,128)S(1)} custom-call(f32[1024,128]{1,0:T(8,128)S(1)} %get-tuple-element.33.r_0_, f32[8,4096]{1,0:T(8,128)S(1)} %get-tuple-element.34.r_1_, f32[1024,256]{1,0:T(8,128)S(1)} %bitcast.22, bf16[4096,256]{1,0:T(8,128)(2,1)S(1)} %get-tuple-element.22.r_1_.r_3_, bf16[4096,256]{1,0:T(8,128)(2,1)S(1)} %get-tuple-element.23.r_2_.r_4_, ...), custom_call_target="tpu_custom_call" | custom-call | flops 536870912 | bytes 1048576 | tf_op jit(solution)/shard_map/pallas_call | solution.py:185
  105.9 1.9 %shard_map.57.refs_0_ = f32[256,256]{1,0:T(8,128)S(1)} custom-call(f32[1024,128]{1,0:T(8,128)S(1)} %get-tuple-element.33.r_0_, f32[8,4096]{1,0:T(8,128)S(1)} %get-tuple-element.34.r_1_, f32[1024,256]{1,0:T(8,128)S(1)} %bitcast.23, bf16[4096,256]{1,0:T(8,128)(2,1)S(1)} %get-tuple-element.22.r_1_.r_3_, bf16[4096,256]{1,0:T(8,128)(2,1)S(1)} %get-tuple-element.23.r_2_.r_4_, ...), custom_call_target="tpu_custom_call" | custom-call | flops 536870912 | bytes 1048576 | tf_op jit(solution)/shard_map/pallas_call | solution.py:185
  107.8 4.7 %collective-permute-done.9.refs_1_ = f32[256,256]{1,0:T(8,128)S(1)} collective-permute-done((f32[256,256]{1,0:T(8,128)S(1)}, f32[256,256]{1,0:T(8,128)S(1)}, u32[]{:S(2)}, u32[]{:S(2)}) %collective-permute-start.9) | collective-permute-done | bytes 262176 | tf_op jit(solution)/shard_map/ppermute | solution.py:267
  112.6 2.5 %collective-permute-done.11.r_1_ = f32[256,256]{1,0:T(8,128)S(1)} collective-permute-done((f32[256,256]{1,0:T(8,128)S(1)}, f32[256,256]{1,0:T(8,128)S(1)}, u32[]{:S(2)}, u32[]{:S(2)}) %collective-permute-start.11) | collective-permute-done | bytes 262176 | tf_op jit(solution)/shard_map/ppermute | solution.py:267
  115.8 2.2 %collective-permute-start.13 = (f32[64,256]{1,0:T(8,128)S(1)}, f32[64,256]{1,0:T(8,128)S(1)}, u32[]{:S(2)}, u32[]{:S(2)}) collective-permute-start(f32[64,256]{1,0:T(8,128)S(1)} %get-tuple-element.37), channel_id=1, source_target_pairs={{0,2},{1,3},{2,0},{3,1},{4,6},{5,7},{6,4},{7,5},{8,10},{9,11},{10,... | collective-permute-start | bytes 196616 | tf_op jit(solution)/shard_map/ppermute | solution.py:270
  (42 shorter events, 13.1 us)
Async XLA Ops:
  0.6 13.2 %copy-start = (f32[512,256]{1,0:T(8,128)S(1)}, f32[512,256]{1,0:T(8,128)}, u32[]{:S(2)}) copy-start(f32[512,256]{1,0:T(8,128)} %r_0_.1) | copy-start | bytes 1572868
  0.6 16.3 %collective-permute-start = (f32[512,256]{1,0:T(8,128)}, f32[512,256]{1,0:T(8,128)S(1)}, u32[]{:S(2)}, u32[]{:S(2)}) collective-permute-start(f32[512,256]{1,0:T(8,128)} %r_0_.1), channel_id=1, source_target_pairs={{0,32},{16,48},{32,64},{48,80},{64,96},{80,112},{96,0},{112,16},{1... | collective-permute-start | bytes 1572872 | tf_op jit(solution)/shard_map/ppermute | solution.py:223
  2.7 14.5 %collective-permute-start.1 = (f32[512,256]{1,0:T(8,128)}, f32[512,256]{1,0:T(8,128)S(1)}, u32[]{:S(2)}, u32[]{:S(2)}) collective-permute-start(f32[512,256]{1,0:T(8,128)} %r_0_.1), channel_id=1, source_target_pairs={{0,96},{16,112},{32,0},{48,16},{64,32},{80,48},{96,64},{112,80},{1... | collective-permute-start | bytes 1572872 | tf_op jit(solution)/shard_map/ppermute | solution.py:223
  4.9 0.8 copy-start.1
  6.8 24.3 %all-to-all-start = ((f32[16,64,256]{2,1,0:T(8,128)}), f32[16,64,256]{2,1,0:T(8,128)S(1)}, u32[]{:S(2)}, u32[]{:S(2)}) async-start(f32[16,64,256]{2,1,0:T(8,128)} %shard_map.49), calls=%async_computation | async-start | bytes 2097152 | tf_op jit(solution)/shard_map/all_to_all | solution.py:210
  13.9 17.6 %collective-permute-start.4 = (f32[512,256]{1,0:T(8,128)S(1)}, f32[512,256]{1,0:T(8,128)S(1)}, u32[]{:S(2)}, u32[]{:S(2)}) collective-permute-start(f32[512,256]{1,0:T(8,128)S(1)} %copy-done), channel_id=1, source_target_pairs={{0,16},{16,0},{32,48},{48,32},{64,80},{80,64},{96,112},{112,96},{1... | collective-permute-start | bytes 1572872 | tf_op jit(solution)/shard_map/ppermute | solution.py:226
  17.0 8.8 %collective-permute-start.2 = (f32[256,256]{1,0:T(8,128)S(1)}, f32[256,256]{1,0:T(8,128)S(1)}, u32[]{:S(2)}, u32[]{:S(2)}) collective-permute-start(f32[256,256]{1,0:T(8,128)S(1)} %slice.8), channel_id=1, source_target_pairs={{0,32},{16,48},{32,64},{48,80},{64,96},{80,112},{96,0},{112,16},{1... | collective-permute-start | bytes 786440 | tf_op jit(solution)/shard_map/ppermute | solution.py:223
  17.1 14.4 %collective-permute-start.5 = (f32[512,256]{1,0:T(8,128)S(1)}, f32[512,256]{1,0:T(8,128)}, u32[]{:S(2)}, u32[]{:S(2)}) collective-permute-start(f32[512,256]{1,0:T(8,128)S(1)} %collective-permute-done.r_1_), channel_id=1, source_target_pairs={{0,16},{16,0},{32,48},{48,32},{64,80},{80,64},{96,112},{112,96},{1... | collective-permute-start | bytes 1572872 | tf_op jit(solution)/shard_map/ppermute | solution.py:226
  17.2 14.3 %collective-permute-start.6 = (f32[512,256]{1,0:T(8,128)S(1)}, f32[512,256]{1,0:T(8,128)}, u32[]{:S(2)}, u32[]{:S(2)}) collective-permute-start(f32[512,256]{1,0:T(8,128)S(1)} %collective-permute-done.1.r_2_), channel_id=1, source_target_pairs={{0,16},{16,0},{32,48},{48,32},{64,80},{80,64},{96,112},{112,96},{1... | collective-permute-start | bytes 1572872 | tf_op jit(solution)/shard_map/ppermute | solution.py:226
  17.7 8.9 %collective-permute-start.3 = (f32[256,256]{1,0:T(8,128)S(1)}, f32[256,256]{1,0:T(8,128)}, u32[]{:S(2)}, u32[]{:S(2)}) collective-permute-start(f32[256,256]{1,0:T(8,128)S(1)} %slice.9), channel_id=1, source_target_pairs={{0,96},{16,112},{32,0},{48,16},{64,32},{80,48},{96,64},{112,80},{1... | collective-permute-start | bytes 786440 | tf_op jit(solution)/shard_map/ppermute | solution.py:223
  25.8 5.7 %collective-permute-start.7 = (f32[256,256]{1,0:T(8,128)S(1)}, f32[256,256]{1,0:T(8,128)}, u32[]{:S(2)}, u32[]{:S(2)}) collective-permute-start(f32[256,256]{1,0:T(8,128)S(1)} %collective-permute-done.2.r_3_), channel_id=1, source_target_pairs={{0,16},{16,0},{32,48},{48,32},{64,80},{80,64},{96,112},{112,96},{1... | collective-permute-start | bytes 786440 | tf_op jit(solution)/shard_map/ppermute | solution.py:226
  26.6 4.8 %collective-permute-start.8 = (f32[256,256]{1,0:T(8,128)}, f32[256,256]{1,0:T(8,128)}, u32[]{:S(2)}, u32[]{:S(2)}) collective-permute-start(f32[256,256]{1,0:T(8,128)} %collective-permute-done.3.r_4_), channel_id=1, source_target_pairs={{0,16},{16,0},{32,48},{48,32},{64,80},{80,64},{96,112},{112,96},{1... | collective-permute-start | bytes 786440 | tf_op jit(solution)/shard_map/ppermute | solution.py:226
  97.8 14.7 %collective-permute-start.9 = (f32[256,256]{1,0:T(8,128)S(1)}, f32[256,256]{1,0:T(8,128)S(1)}, u32[]{:S(2)}, u32[]{:S(2)}) collective-permute-start(f32[256,256]{1,0:T(8,128)S(1)} %shard_map.58), channel_id=1, source_target_pairs={{0,4},{1,5},{2,6},{3,7},{4,8},{5,9},{6,10},{7,11},{8,12},{9,13},{1... | collective-permute-start | bytes 786440 | tf_op jit(solution)/shard_map/ppermute | solution.py:267
  100.3 12.3 %collective-permute-start.10 = (f32[256,256]{1,0:T(8,128)S(1)}, f32[256,256]{1,0:T(8,128)S(1)}, u32[]{:S(2)}, u32[]{:S(2)}) collective-permute-start(f32[256,256]{1,0:T(8,128)S(1)} %shard_map.60), channel_id=1, source_target_pairs={{0,8},{1,9},{2,10},{3,11},{4,12},{5,13},{6,14},{7,15},{8,0},{9,1},... | collective-permute-start | bytes 786440 | tf_op jit(solution)/shard_map/ppermute | solution.py:267
  104.4 10.8 %collective-permute-start.11 = (f32[256,256]{1,0:T(8,128)S(1)}, f32[256,256]{1,0:T(8,128)S(1)}, u32[]{:S(2)}, u32[]{:S(2)}) collective-permute-start(f32[256,256]{1,0:T(8,128)S(1)} %shard_map.62), channel_id=1, source_target_pairs={{0,12},{1,13},{2,14},{3,15},{4,0},{5,1},{6,2},{7,3},{8,4},{9,5},{1... | collective-permute-start | bytes 786440 | tf_op jit(solution)/shard_map/ppermute | solution.py:267
  115.2 5.5 %collective-permute-start.12 = (f32[64,256]{1,0:T(8,128)S(1)}, f32[64,256]{1,0:T(8,128)S(1)}, u32[]{:S(2)}, u32[]{:S(2)}) collective-permute-start(f32[64,256]{1,0:T(8,128)S(1)} %get-tuple-element.36), channel_id=1, source_target_pairs={{0,1},{1,2},{2,3},{3,0},{4,5},{5,6},{6,7},{7,4},{8,9},{9,10},{10,1... | collective-permute-start | bytes 196616 | tf_op jit(solution)/shard_map/ppermute | solution.py:270
  115.8 5.8 %collective-permute-start.13 = (f32[64,256]{1,0:T(8,128)S(1)}, f32[64,256]{1,0:T(8,128)S(1)}, u32[]{:S(2)}, u32[]{:S(2)}) collective-permute-start(f32[64,256]{1,0:T(8,128)S(1)} %get-tuple-element.37), channel_id=1, source_target_pairs={{0,2},{1,3},{2,0},{3,1},{4,6},{5,7},{6,4},{7,5},{8,10},{9,11},{10,... | collective-permute-start | bytes 196616 | tf_op jit(solution)/shard_map/ppermute | solution.py:270
  118.0 4.3 %collective-permute-start.14 = (f32[64,256]{1,0:T(8,128)S(1)}, f32[64,256]{1,0:T(8,128)S(1)}, u32[]{:S(2)}, u32[]{:S(2)}) collective-permute-start(f32[64,256]{1,0:T(8,128)S(1)} %get-tuple-element.38), channel_id=1, source_target_pairs={{0,3},{1,0},{2,1},{3,2},{4,7},{5,4},{6,5},{7,6},{8,11},{9,8},{10,9... | collective-permute-start | bytes 196616 | tf_op jit(solution)/shard_map/ppermute | solution.py:270

commit v5 on v4

--- a/solution.py
+++ b/solution.py
@@ -95,7 +95,7 @@
         tot[rows, :] = l
         return carry
 
-    lax.fori_loop(0, s_ref.shape[0] // 8, group, 0, unroll=8)
+    lax.fori_loop(0, s_ref.shape[0] // 8, group, 0, unroll=16)
     finish_rows(top, tot, out_ref)
 
 
@@ -121,22 +121,18 @@
     wide[...] = jnp.broadcast_to(alpha, (LANES, alpha.shape[1])).T
     rows = s_ref.shape[0]
     piece, across = 64, 8
-
-    def group(c, carry):
-        cols = [pl.ds(pl.multiple_of((c * across + k) * LANES, LANES), LANES) for k in range(across)]
+    for start in range(0, s_ref.shape[1], LANES * across):
+        cols = [slice(k, k + LANES) for k in range(start, start + LANES * across, LANES)]
         m, l = [None] * across, [None] * across
         for r in range(0, rows, piece):
-            shift = [wide[r + q:r + q + 8, :] for q in range(0, piece, 8)]
+            shift = [wide[q:q + 8, :] for q in range(r, r + piece, 8)]
             for k in range(across):
-                x = [s_ref[r + q:r + q + 8, cols[k]] + shift[q // 8] for q in range(0, piece, 8)]
+                x = [s_ref[q:q + 8, cols[k]] + shift[(q - r) // 8] for q in range(r, r + piece, 8)]
                 m[k], l[k] = online(m[k], l[k], x)
         for k in range(across):
             peak = jnp.max(m[k], axis=0, keepdims=True)
             total = jnp.sum(l[k] * jnp.exp2(m[k] - peak), axis=0, keepdims=True)
             out_ref[:, cols[k]] = jnp.broadcast_to(peak + jnp.log2(total), (out_ref.shape[0], LANES))
-        return carry
-
-    lax.fori_loop(0, s_ref.shape[1] // (LANES * across), group, 0)
 
 
 def weights_kernel(log_a, log_b, eps, part_ref, alpha_ref, b2_ref, awide_ref, bwide_ref, pot_ref):
@@ -181,14 +177,13 @@
 VM = pl.BlockSpec(memory_space=pltpu.VMEM)
 
 
-def call(kernel, outs, scratch, *args, limit=6 * MIB, aliases={}, cost=None):
+def call(kernel, outs, scratch, *args, limit=6 * MIB, cost=None):
     return pl.pallas_call(
         kernel,
         out_shape=outs,
         in_specs=[VM] * len(args),
         out_specs=[VM] * len(outs),
         scratch_shapes=scratch,
-        input_output_aliases=aliases,
         cost_estimate=cost,
         compiler_params=pltpu.CompilerParams(vmem_limit_bytes=limit),
     )(*args)
@@ -231,7 +226,7 @@
     half = piece // 2
     up, down = move(points_b, 1), move(points_b, -1)
     low, high = move(up[:half], 1), move(down[half:], -1)
-    wide, = call(repeat_kernel, [f32(nb, share, width)], [], points_a)
+    wide, = call(repeat_kernel, [v32(nb, share, width)], [], points_a)
     whole_a = spread(wide, "ba").reshape(rows_a, width)
     pieces = [
         (points_b, place(0, 0)), (up, place(3, 0)), (down, place(1, 0)), (low, place(2, 0)), (high, place(2, 0, half)),
@@ -272,7 +267,7 @@
     side = math.isqrt(nb)
     step = pl.CostEstimate(flops=2 * rows_a // side * width * rows_b, bytes_accessed=MIB, transcendentals=0)
     held = []
-    for by in [*range(1, side), 0]:
+    for by in [2, 1, 3, 0]:
         g, = call(
             lambda *r: grad_kernel(lambda: lax.rem(lax.axis_index("ba") // side + by, side) * (rows_a // side), *r),
             [v32(rows_a // side, width)], [v32(rows_a // side, LANES)],
@@ -285,7 +280,7 @@
     cuts = call(
         lambda *r: turn_sum_kernel(lambda: [lax.rem(lax.rem(lax.axis_index("ba"), side) + by, side) for by in range(side)], *r),
         [v32(share, width)] * side, [], total, arrived[-1])
-    grad, = call(sum_kernel, [f32(share, width)], [], cuts[0], *[along_y(cuts[by], by) for by in range(1, side)])
+    grad, = call(sum_kernel, [f32(share, width)], [], cuts[0], *[along_y(cuts[by], by) for by in (2, 1, 3)])
     return (pot_a.reshape(rows_a), pot_b.reshape(rows_b), grad)
 
 

time: 123 us -> 120 us (0.976)
  waiting for transfers between devices: 23.5 us -> 20.3 us
  Pallas kernels: 31.6 us -> 29.9 us
    ppermute x3, waiting for transfers between devices: 7.24 us -> 4.62 us  [along_x(): return lax.ppermute(v, 'ba', [(i, (i + side * by) % nb) for i in range(nb)])]
    pallas_call x16, Pallas kernels: 31.6 us -> 29.9 us  [call(): pl.pallas_call(kernel, out_shape=outs, in_specs=[VM] * len(args), out_spe...]
  transfers between devices with their start and end apart: 16 -> 16, of which waited for: 9 -> 8; matrix products, arithmetic and copies ran while one was open for 0% -> 0% of each run, Pallas kernels for 6% -> 6%
where the time goes in v5:
time: 120 us; the launch traced here: 119 us
  blocking collectives  41.9 us (35%)
  Pallas kernels  29.9 us (25%)
  starting transfers between devices  24.8 us (21%)
  waiting for transfers between devices  20.3 us (17%)
  local copies, waits for them, and re-layouts  1.48 us (1%)
    all_to_all x4, blocking collectives, spread(): return lax.all_to_all(x, axis, 0, 0, tiled=True)  41.9 us
    pallas_call x16, Pallas kernels, call(): pl.pallas_call(kernel, out_shape=outs, in_specs=[VM] * len(args), out_spe...  29.9 us
    ppermute x4, waiting for transfers between devices, move(): return lax.ppermute(x, 'aa', [(i, (i + 2 * by) % na) for i in range(na)])  8.72 us
    ppermute x4, starting transfers between devices, move(): return lax.ppermute(x, 'aa', [(i, (i + 2 * by) % na) for i in range(na)])  7.56 us
    all_to_all x1, starting transfers between devices, spread(): return lax.all_to_all(x, axis, 0, 0, tiled=True)  7.03 us
    ppermute x3, starting transfers between devices, along_x(): return lax.ppermute(v, 'ba', [(i, (i + side * by) % nb) for i in range(nb)])  4.88 us
    ppermute x3, starting transfers between devices, along_y(): lax.ppermute(v, 'ba', [(i, i // side * side + (i + by) % side) for i in r...  4.71 us
    ppermute x3, waiting for transfers between devices, along_x(): return lax.ppermute(v, 'ba', [(i, (i + side * by) % nb) for i in range(nb)])  4.62 us
  transfers between devices with their start and end apart: 16, of which 8 were waited for; matrix products, arithmetic and copies ran while one was open for 0% of the time, Pallas kernels for 6%

profile of v5, /device:TPU:0, one launch (start us, length us, event | category | flops | bytes accessed | tf_op | source)
XLA Modules:
  0.0 119.3 jit_solution(4328108012860914510)
XLA Ops:
  0.6 2.1 %collective-permute-start = (f32[512,256]{1,0:T(8,128)}, f32[512,256]{1,0:T(8,128)S(1)}, u32[]{:S(2)}, u32[]{:S(2)}) collective-permute-start(f32[512,256]{1,0:T(8,128)} %r_0_.1), channel_id=1, source_target_pairs={{0,32},{16,48},{32,64},{48,80},{64,96},{80,112},{96,0},{112,16},{1... | collective-permute-start | bytes 1572872 | tf_op jit(solution)/shard_map/ppermute | solution.py:218
  2.7 2.2 %collective-permute-start.1 = (f32[512,256]{1,0:T(8,128)}, f32[512,256]{1,0:T(8,128)S(1)}, u32[]{:S(2)}, u32[]{:S(2)}) collective-permute-start(f32[512,256]{1,0:T(8,128)} %r_0_.1), channel_id=1, source_target_pairs={{0,96},{16,112},{32,0},{48,16},{64,32},{80,48},{96,64},{112,80},{1... | collective-permute-start | bytes 1572872 | tf_op jit(solution)/shard_map/ppermute | solution.py:218
  6.8 7.0 %all-to-all-start = ((f32[16,64,256]{2,1,0:T(8,128)}), f32[16,64,256]{2,1,0:T(8,128)S(1)}, u32[]{:S(2)}, u32[]{:S(2)}) async-start(f32[16,64,256]{2,1,0:T(8,128)} %shard_map.49), calls=%async_computation | async-start | bytes 2097152 | tf_op jit(solution)/shard_map/all_to_all | solution.py:205
  14.0 3.0 %collective-permute-done.r_1_ = f32[512,256]{1,0:T(8,128)S(1)} collective-permute-done((f32[512,256]{1,0:T(8,128)}, f32[512,256]{1,0:T(8,128)S(1)}, u32[]{:S(2)}, u32[]{:S(2)}) %collective-permute-start) | collective-permute-done | bytes 524320 | tf_op jit(solution)/shard_map/ppermute | solution.py:218
  17.7 3.2 %collective-permute-start.3 = (f32[256,256]{1,0:T(8,128)S(1)}, f32[256,256]{1,0:T(8,128)}, u32[]{:S(2)}, u32[]{:S(2)}) collective-permute-start(f32[256,256]{1,0:T(8,128)S(1)} %slice.9), channel_id=1, source_target_pairs={{0,96},{16,112},{32,0},{48,16},{64,32},{80,48},{96,64},{112,80},{1... | collective-permute-start | bytes 786440 | tf_op jit(solution)/shard_map/ppermute | solution.py:218
  20.9 4.9 %collective-permute-done.2.r_3_ = f32[256,256]{1,0:T(8,128)S(1)} collective-permute-done((f32[256,256]{1,0:T(8,128)S(1)}, f32[256,256]{1,0:T(8,128)S(1)}, u32[]{:S(2)}, u32[]{:S(2)}) %collective-permute-start.2) | collective-permute-done | bytes 262176 | tf_op jit(solution)/shard_map/ppermute | solution.py:218
  26.6 4.5 %all-to-all-done = f32[16,64,256]{2,1,0:T(8,128)S(1)} async-done(((f32[16,64,256]{2,1,0:T(8,128)}), f32[16,64,256]{2,1,0:T(8,128)S(1)}, u32[]{:S(2)}, u32[]{:S(2)}) %all-to-all-start) | async-done | bytes 1048608 | tf_op jit(solution)/shard_map/all_to_all | solution.py:205
  31.5 2.5 %shard_map.51 = (bf16[4096,256]{1,0:T(8,128)(2,1)S(1)}, bf16[4096,256]{1,0:T(8,128)(2,1)S(1)}, f32[1,4096]{1,0:T(1,128)S(1)}) custom-call(f32[512,256]{1,0:T(8,128)S(1)} %copy-done, f32[512,256]{1,0:T(8,128)S(1)} %collective-permute-done.r_1_, f32[512,256]{1,0:T(8,128)S(1)} %collective-permute-done.1.r_2_, f32[256,256]{1,0:T(8,128)S(1)} %collective-permute-done.2.r_3_, ...), custom_call_target="tpu_custom_call" | custom-call | bytes 67108864 | tf_op jit(solution)/shard_map/pallas_call | solution.py:181
  33.9 7.5 %shard_map.52 = (f32[1024,4096]{1,0:T(8,128)S(1)}, f32[16,1024]{1,0:T(8,128)S(1)}) custom-call(bf16[1024,768]{1,0:T(8,128)(2,1)S(1)} %get-tuple-element.21.r_0_, bf16[4096,256]{1,0:T(8,128)(2,1)S(1)} %get-tuple-element.22.r_1_.r_3_, bf16[4096,256]{1,0:T(8,128)(2,1)S(1)} %get-tuple-element.23.r_2_.r_4_, f32[1,4096]{1,0:T(1,128)S(1)} %get-tuple-element.24.r_3_.r_2_), custom_call_target="tpu_custom_call" | custom-call | tf_op jit(solution)/shard_map/pallas_call | solution.py:181
  41.5 11.5 %all_to_all.49 = f32[16,1,1024]{2,1,0:T(1,128)S(1)} all-to-all(f32[16,1,1024]{2,1,0:T(1,128)S(1)} %copy.5), channel_id=1, replica_groups=mesh['aa'=8,'ba'=16] {'ba'}, dimensions={0} | all-to-all | bytes 131072 | tf_op jit(solution)/shard_map/all_to_all | solution.py:205
  53.0 3.1 %shard_map.53 = (f32[8,4096]{1,0:T(8,128)S(1)}, f32[1,1024]{1,0:T(1,128)}, f32[1,1024]{1,0:T(1,128)}) custom-call(f32[16,1024]{1,0:T(8,128)S(1)} %bitcast.26, f32[1,1024]{1,0:T(1,128)S(1)} %get-tuple-element.26.r_1_, f32[1024,4096]{1,0:T(8,128)S(1)} %get-tuple-element.27.r_2_.r_1_.r_5_), custom_call_target="tpu_custom_call" | custom-call | tf_op jit(solution)/shard_map/pallas_call | solution.py:181
  56.3 11.0 %all_to_all.50 = f32[8,1,4096]{2,1,0:T(1,128)S(1)} all-to-all(f32[8,1,4096]{2,1,0:T(1,128)S(1)} %copy.6), channel_id=1, replica_groups=mesh['aa'=8,'ba'=16] {'aa'}, dimensions={0} | all-to-all | bytes 262144 | tf_op jit(solution)/shard_map/all_to_all | solution.py:205
  67.3 3.3 %shard_map.54 = f32[16,1024]{1,0:T(8,128)S(1)} custom-call(f32[8,4096]{1,0:T(8,128)S(1)} %bitcast.24, f32[1024,4096]{1,0:T(8,128)S(1)} %get-tuple-element.27.r_2_.r_1_.r_5_), custom_call_target="tpu_custom_call" | custom-call | tf_op jit(solution)/shard_map/pallas_call | solution.py:181
  70.7 10.9 %all_to_all.51 = f32[16,1,1024]{2,1,0:T(1,128)S(1)} all-to-all(f32[16,1,1024]{2,1,0:T(1,128)S(1)} %copy.7), channel_id=1, replica_groups=mesh['aa'=8,'ba'=16] {'ba'}, dimensions={0} | all-to-all | bytes 131072 | tf_op jit(solution)/shard_map/all_to_all | solution.py:205
  81.6 3.1 %shard_map.55 = (f32[8,4096]{1,0:T(8,128)S(1)}, f32[1,1024]{1,0:T(1,128)S(1)}, f32[1,1024]{1,0:T(1,128)}) custom-call(f32[16,1024]{1,0:T(8,128)S(1)} %bitcast.27, f32[1,1024]{1,0:T(1,128)S(1)} %get-tuple-element.26.r_1_, f32[1024,4096]{1,0:T(8,128)S(1)} %get-tuple-element.27.r_2_.r_1_.r_5_), custom_call_target="tpu_custom_call" | custom-call | tf_op jit(solution)/shard_map/pallas_call | solution.py:181
  84.9 8.5 %all_to_all.52 = f32[8,1,4096]{2,1,0:T(1,128)S(1)} all-to-all(f32[8,1,4096]{2,1,0:T(1,128)S(1)} %copy.8), channel_id=1, replica_groups=mesh['aa'=8,'ba'=16] {'aa'}, dimensions={0} | all-to-all | bytes 262144 | tf_op jit(solution)/shard_map/all_to_all | solution.py:205
  94.3 1.9 %shard_map.58 = f32[256,256]{1,0:T(8,128)S(1)} custom-call(f32[1024,128]{1,0:T(8,128)S(1)} %get-tuple-element.33.r_0_, f32[8,4096]{1,0:T(8,128)S(1)} %get-tuple-element.34.r_1_, f32[1024,256]{1,0:T(8,128)S(1)} %bitcast.20, bf16[4096,256]{1,0:T(8,128)(2,1)S(1)} %get-tuple-element.22.r_1_.r_3_, bf16[4096,256]{1,0:T(8,128)(2,1)S(1)} %get-tuple-element.23.r_2_.r_4_, ...), custom_call_target="tpu_custom_call" | custom-call | flops 536870912 | bytes 1048576 | tf_op jit(solution)/shard_map/pallas_call | solution.py:181
  97.7 1.9 %shard_map.60 = f32[256,256]{1,0:T(8,128)S(1)} custom-call(f32[1024,128]{1,0:T(8,128)S(1)} %get-tuple-element.33.r_0_, f32[8,4096]{1,0:T(8,128)S(1)} %get-tuple-element.34.r_1_, f32[1024,256]{1,0:T(8,128)S(1)} %bitcast.21, bf16[4096,256]{1,0:T(8,128)(2,1)S(1)} %get-tuple-element.22.r_1_.r_3_, bf16[4096,256]{1,0:T(8,128)(2,1)S(1)} %get-tuple-element.23.r_2_.r_4_, ...), custom_call_target="tpu_custom_call" | custom-call | flops 536870912 | bytes 1048576 | tf_op jit(solution)/shard_map/pallas_call | solution.py:181
  100.4 1.9 %shard_map.62 = f32[256,256]{1,0:T(8,128)S(1)} custom-call(f32[1024,128]{1,0:T(8,128)S(1)} %get-tuple-element.33.r_0_, f32[8,4096]{1,0:T(8,128)S(1)} %get-tuple-element.34.r_1_, f32[1024,256]{1,0:T(8,128)S(1)} %bitcast.22, bf16[4096,256]{1,0:T(8,128)(2,1)S(1)} %get-tuple-element.22.r_1_.r_3_, bf16[4096,256]{1,0:T(8,128)(2,1)S(1)} %get-tuple-element.23.r_2_.r_4_, ...), custom_call_target="tpu_custom_call" | custom-call | flops 536870912 | bytes 1048576 | tf_op jit(solution)/shard_map/pallas_call | solution.py:181
  102.4 2.5 %collective-permute-start.11 = (f32[256,256]{1,0:T(8,128)S(1)}, f32[256,256]{1,0:T(8,128)S(1)}, u32[]{:S(2)}, u32[]{:S(2)}) collective-permute-start(f32[256,256]{1,0:T(8,128)S(1)} %shard_map.62), channel_id=1, source_target_pairs={{0,12},{1,13},{2,14},{3,15},{4,0},{5,1},{6,2},{7,3},{8,4},{9,5},{1... | collective-permute-start | bytes 786440 | tf_op jit(solution)/shard_map/ppermute | solution.py:262
  104.9 1.9 %shard_map.57.refs_0_ = f32[256,256]{1,0:T(8,128)S(1)} custom-call(f32[1024,128]{1,0:T(8,128)S(1)} %get-tuple-element.33.r_0_, f32[8,4096]{1,0:T(8,128)S(1)} %get-tuple-element.34.r_1_, f32[1024,256]{1,0:T(8,128)S(1)} %bitcast.23, bf16[4096,256]{1,0:T(8,128)(2,1)S(1)} %get-tuple-element.22.r_1_.r_3_, bf16[4096,256]{1,0:T(8,128)(2,1)S(1)} %get-tuple-element.23.r_2_.r_4_, ...), custom_call_target="tpu_custom_call" | custom-call | flops 536870912 | bytes 1048576 | tf_op jit(solution)/shard_map/pallas_call | solution.py:181
  107.3 4.2 %collective-permute-done.10.refs_1_ = f32[256,256]{1,0:T(8,128)S(1)} collective-permute-done((f32[256,256]{1,0:T(8,128)S(1)}, f32[256,256]{1,0:T(8,128)S(1)}, u32[]{:S(2)}, u32[]{:S(2)}) %collective-permute-start.10) | collective-permute-done | bytes 262176 | tf_op jit(solution)/shard_map/ppermute | solution.py:262
  113.7 2.5 %collective-permute-start.14 = (f32[64,256]{1,0:T(8,128)S(1)}, f32[64,256]{1,0:T(8,128)S(1)}, u32[]{:S(2)}, u32[]{:S(2)}) collective-permute-start(f32[64,256]{1,0:T(8,128)S(1)} %get-tuple-element.38), channel_id=1, source_target_pairs={{0,3},{1,0},{2,1},{3,2},{4,7},{5,4},{6,5},{7,6},{8,11},{9,8},{10,9... | collective-permute-start | bytes 196616 | tf_op jit(solution)/shard_map/ppermute | solution.py:265
  116.3 1.9 %collective-permute-done.12.refs_1_ = f32[64,256]{1,0:T(8,128)S(1)} collective-permute-done((f32[64,256]{1,0:T(8,128)S(1)}, f32[64,256]{1,0:T(8,128)S(1)}, u32[]{:S(2)}, u32[]{:S(2)}) %collective-permute-start.12) | collective-permute-done | bytes 65568 | tf_op jit(solution)/shard_map/ppermute | solution.py:265
  (42 shorter events, 11.5 us)
Async XLA Ops:
  0.6 13.2 %copy-start = (f32[512,256]{1,0:T(8,128)S(1)}, f32[512,256]{1,0:T(8,128)}, u32[]{:S(2)}) copy-start(f32[512,256]{1,0:T(8,128)} %r_0_.1) | copy-start | bytes 1572868
  0.6 16.3 %collective-permute-start = (f32[512,256]{1,0:T(8,128)}, f32[512,256]{1,0:T(8,128)S(1)}, u32[]{:S(2)}, u32[]{:S(2)}) collective-permute-start(f32[512,256]{1,0:T(8,128)} %r_0_.1), channel_id=1, source_target_pairs={{0,32},{16,48},{32,64},{48,80},{64,96},{80,112},{96,0},{112,16},{1... | collective-permute-start | bytes 1572872 | tf_op jit(solution)/shard_map/ppermute | solution.py:218
  2.7 14.5 %collective-permute-start.1 = (f32[512,256]{1,0:T(8,128)}, f32[512,256]{1,0:T(8,128)S(1)}, u32[]{:S(2)}, u32[]{:S(2)}) collective-permute-start(f32[512,256]{1,0:T(8,128)} %r_0_.1), channel_id=1, source_target_pairs={{0,96},{16,112},{32,0},{48,16},{64,32},{80,48},{96,64},{112,80},{1... | collective-permute-start | bytes 1572872 | tf_op jit(solution)/shard_map/ppermute | solution.py:218
  4.9 0.8 copy-start.1
  6.8 24.3 %all-to-all-start = ((f32[16,64,256]{2,1,0:T(8,128)}), f32[16,64,256]{2,1,0:T(8,128)S(1)}, u32[]{:S(2)}, u32[]{:S(2)}) async-start(f32[16,64,256]{2,1,0:T(8,128)} %shard_map.49), calls=%async_computation | async-start | bytes 2097152 | tf_op jit(solution)/shard_map/all_to_all | solution.py:205
  13.9 17.6 %collective-permute-start.4 = (f32[512,256]{1,0:T(8,128)S(1)}, f32[512,256]{1,0:T(8,128)S(1)}, u32[]{:S(2)}, u32[]{:S(2)}) collective-permute-start(f32[512,256]{1,0:T(8,128)S(1)} %copy-done), channel_id=1, source_target_pairs={{0,16},{16,0},{32,48},{48,32},{64,80},{80,64},{96,112},{112,96},{1... | collective-permute-start | bytes 1572872 | tf_op jit(solution)/shard_map/ppermute | solution.py:221
  17.0 8.8 %collective-permute-start.2 = (f32[256,256]{1,0:T(8,128)S(1)}, f32[256,256]{1,0:T(8,128)S(1)}, u32[]{:S(2)}, u32[]{:S(2)}) collective-permute-start(f32[256,256]{1,0:T(8,128)S(1)} %slice.8), channel_id=1, source_target_pairs={{0,32},{16,48},{32,64},{48,80},{64,96},{80,112},{96,0},{112,16},{1... | collective-permute-start | bytes 786440 | tf_op jit(solution)/shard_map/ppermute | solution.py:218
  17.1 14.4 %collective-permute-start.5 = (f32[512,256]{1,0:T(8,128)S(1)}, f32[512,256]{1,0:T(8,128)}, u32[]{:S(2)}, u32[]{:S(2)}) collective-permute-start(f32[512,256]{1,0:T(8,128)S(1)} %collective-permute-done.r_1_), channel_id=1, source_target_pairs={{0,16},{16,0},{32,48},{48,32},{64,80},{80,64},{96,112},{112,96},{1... | collective-permute-start | bytes 1572872 | tf_op jit(solution)/shard_map/ppermute | solution.py:221
  17.2 14.3 %collective-permute-start.6 = (f32[512,256]{1,0:T(8,128)S(1)}, f32[512,256]{1,0:T(8,128)}, u32[]{:S(2)}, u32[]{:S(2)}) collective-permute-start(f32[512,256]{1,0:T(8,128)S(1)} %collective-permute-done.1.r_2_), channel_id=1, source_target_pairs={{0,16},{16,0},{32,48},{48,32},{64,80},{80,64},{96,112},{112,96},{1... | collective-permute-start | bytes 1572872 | tf_op jit(solution)/shard_map/ppermute | solution.py:221
  17.7 8.9 %collective-permute-start.3 = (f32[256,256]{1,0:T(8,128)S(1)}, f32[256,256]{1,0:T(8,128)}, u32[]{:S(2)}, u32[]{:S(2)}) collective-permute-start(f32[256,256]{1,0:T(8,128)S(1)} %slice.9), channel_id=1, source_target_pairs={{0,96},{16,112},{32,0},{48,16},{64,32},{80,48},{96,64},{112,80},{1... | collective-permute-start | bytes 786440 | tf_op jit(solution)/shard_map/ppermute | solution.py:218
  25.8 5.7 %collective-permute-start.7 = (f32[256,256]{1,0:T(8,128)S(1)}, f32[256,256]{1,0:T(8,128)}, u32[]{:S(2)}, u32[]{:S(2)}) collective-permute-start(f32[256,256]{1,0:T(8,128)S(1)} %collective-permute-done.2.r_3_), channel_id=1, source_target_pairs={{0,16},{16,0},{32,48},{48,32},{64,80},{80,64},{96,112},{112,96},{1... | collective-permute-start | bytes 786440 | tf_op jit(solution)/shard_map/ppermute | solution.py:221
  26.6 4.8 %collective-permute-start.8 = (f32[256,256]{1,0:T(8,128)}, f32[256,256]{1,0:T(8,128)}, u32[]{:S(2)}, u32[]{:S(2)}) collective-permute-start(f32[256,256]{1,0:T(8,128)} %collective-permute-done.3.r_4_), channel_id=1, source_target_pairs={{0,16},{16,0},{32,48},{48,32},{64,80},{80,64},{96,112},{112,96},{1... | collective-permute-start | bytes 786440 | tf_op jit(solution)/shard_map/ppermute | solution.py:221
  96.2 11.0 %collective-permute-start.9 = (f32[256,256]{1,0:T(8,128)S(1)}, f32[256,256]{1,0:T(8,128)S(1)}, u32[]{:S(2)}, u32[]{:S(2)}) collective-permute-start(f32[256,256]{1,0:T(8,128)S(1)} %shard_map.58), channel_id=1, source_target_pairs={{0,8},{1,9},{2,10},{3,11},{4,12},{5,13},{6,14},{7,15},{8,0},{9,1},... | collective-permute-start | bytes 786440 | tf_op jit(solution)/shard_map/ppermute | solution.py:262
  99.6 11.8 %collective-permute-start.10 = (f32[256,256]{1,0:T(8,128)S(1)}, f32[256,256]{1,0:T(8,128)S(1)}, u32[]{:S(2)}, u32[]{:S(2)}) collective-permute-start(f32[256,256]{1,0:T(8,128)S(1)} %shard_map.60), channel_id=1, source_target_pairs={{0,4},{1,5},{2,6},{3,7},{4,8},{5,9},{6,10},{7,11},{8,12},{9,13},{1... | collective-permute-start | bytes 786440 | tf_op jit(solution)/shard_map/ppermute | solution.py:262
  102.4 9.1 %collective-permute-start.11 = (f32[256,256]{1,0:T(8,128)S(1)}, f32[256,256]{1,0:T(8,128)S(1)}, u32[]{:S(2)}, u32[]{:S(2)}) collective-permute-start(f32[256,256]{1,0:T(8,128)S(1)} %shard_map.62), channel_id=1, source_target_pairs={{0,12},{1,13},{2,14},{3,15},{4,0},{5,1},{6,2},{7,3},{8,4},{9,5},{1... | collective-permute-start | bytes 786440 | tf_op jit(solution)/shard_map/ppermute | solution.py:262
  111.5 6.6 %collective-permute-start.12 = (f32[64,256]{1,0:T(8,128)S(1)}, f32[64,256]{1,0:T(8,128)S(1)}, u32[]{:S(2)}, u32[]{:S(2)}) collective-permute-start(f32[64,256]{1,0:T(8,128)S(1)} %get-tuple-element.36), channel_id=1, source_target_pairs={{0,2},{1,3},{2,0},{3,1},{4,6},{5,7},{6,4},{7,5},{8,10},{9,11},{10,... | collective-permute-start | bytes 196616 | tf_op jit(solution)/shard_map/ppermute | solution.py:265
  113.0 5.6 %collective-permute-start.13 = (f32[64,256]{1,0:T(8,128)S(1)}, f32[64,256]{1,0:T(8,128)S(1)}, u32[]{:S(2)}, u32[]{:S(2)}) collective-permute-start(f32[64,256]{1,0:T(8,128)S(1)} %get-tuple-element.37), channel_id=1, source_target_pairs={{0,1},{1,2},{2,3},{3,0},{4,5},{5,6},{6,7},{7,4},{8,9},{9,10},{10,1... | collective-permute-start | bytes 196616 | tf_op jit(solution)/shard_map/ppermute | solution.py:265
  113.7 4.9 %collective-permute-start.14 = (f32[64,256]{1,0:T(8,128)S(1)}, f32[64,256]{1,0:T(8,128)S(1)}, u32[]{:S(2)}, u32[]{:S(2)}) collective-permute-start(f32[64,256]{1,0:T(8,128)S(1)} %get-tuple-element.38), channel_id=1, source_target_pairs={{0,3},{1,0},{2,1},{3,2},{4,7},{5,4},{6,5},{7,6},{8,11},{9,8},{10,9... | collective-permute-start | bytes 196616 | tf_op jit(solution)/shard_map/ppermute | solution.py:265

commit v6 on v5

--- a/solution.py
+++ b/solution.py
@@ -36,21 +36,26 @@
         out_ref[d] = a_ref[...]
 
 
-def prepare_kernel(eps, a_ref, left_ref, a2_ref):
+def pieces_kernel(eps, places, a_ref, *refs):
+    pieces, (left_ref, a2_ref, bhi_ref, blo_ref, b2_ref, held, sems) = refs[:len(places)], refs[len(places):]
+    spots, at = [], 0
+    for ref in pieces:
+        spots.append(pl.ds(at, ref.shape[0]))
+        at += ref.shape[0]
+    loads = [pltpu.make_async_copy(ref, held.at[spot], sems.at[k]) for k, (ref, spot) in enumerate(zip(pieces, spots))]
+    for load in loads:
+        load.start()
     x = a_ref[...]
     a2_ref[...] = row_norms(x) * (LOG2E / eps)
     hi, lo = split(x * (2.0 * LOG2E / eps))
     left_ref[...] = jnp.concatenate([hi, hi, lo], axis=1)
-
-
-def pieces_kernel(eps, places, *refs):
-    pieces, (bhi_ref, blo_ref, b2_ref) = refs[:len(places)], refs[-3:]
     me = lax.axis_index("aa")
-    for ref, place in zip(pieces, places):
-        y = ref[...]
-        at = pl.ds(pl.multiple_of(place(me), y.shape[0]), y.shape[0])
-        b2_ref[:, at] = row_norms(y) * (LOG2E / eps)
-        bhi_ref[at, :], blo_ref[at, :] = split(y)
+    for load, spot, place in zip(loads, spots, places):
+        load.wait()
+        y = held[spot, :]
+        to = pl.ds(pl.multiple_of(place(me), spot.size), spot.size)
+        b2_ref[:, to] = row_norms(y) * (LOG2E / eps)
+        bhi_ref[to, :], blo_ref[to, :] = split(y)
 
 
 def scores_kernel(n, left, bhi_ref, blo_ref, b2_ref, s_ref, out_ref, top_ref, tot_ref):
@@ -114,9 +119,8 @@
     return xs[0]
 
 
-def col_pass_kernel(log_b, eps, part_ref, a2_ref, s_ref, out_ref, alpha_ref, pot_ref, wide):
+def col_pass_kernel(log_b, eps, part_ref, a2_ref, s_ref, out_ref, wide, pot_ref):
     alpha = -combine(part_ref[...]) - log_b
-    alpha_ref[...] = alpha
     pot_ref[...] = (alpha + a2_ref[...]) * (eps / LOG2E)
     wide[...] = jnp.broadcast_to(alpha, (LANES, alpha.shape[1])).T
     rows = s_ref.shape[0]
@@ -135,13 +139,6 @@
             out_ref[:, cols[k]] = jnp.broadcast_to(peak + jnp.log2(total), (out_ref.shape[0], LANES))
 
 
-def weights_kernel(log_a, log_b, eps, part_ref, alpha_ref, b2_ref, awide_ref, bwide_ref, pot_ref):
-    beta = -combine(part_ref[...]) - log_a
-    pot_ref[...] = (beta + b2_ref[...]) * (eps / LOG2E)
-    bwide_ref[...] = jnp.broadcast_to(beta + log_b, bwide_ref.shape)
-    awide_ref[...] = jnp.broadcast_to(alpha_ref[...], (LANES, alpha_ref.shape[1])).T
-
-
 def grad_kernel(first, awide_ref, bwide_ref, a_ref, bhi_ref, blo_ref, s_ref, g_ref, mass):
     n = g_ref.shape[0]
     rows = pl.ds(pl.multiple_of(first(), n), n)
@@ -162,6 +159,14 @@
     g_ref[...] = 2.0 * (a_ref[rows, :] * jnp.sum(mass[...], axis=1, keepdims=True) - g_ref[...])
 
 
+def first_grad_kernel(log_a, log_b, eps, first, part_ref, b2_ref, awide_ref, a_ref, bhi_ref, blo_ref, s_ref,
+                      bwide_ref, pot_ref, g_ref, mass):
+    beta = -combine(part_ref[...]) - log_a
+    pot_ref[...] = (beta + b2_ref[...]) * (eps / LOG2E)
+    bwide_ref[...] = jnp.broadcast_to(beta + log_b, bwide_ref.shape)
+    grad_kernel(first, awide_ref, bwide_ref, a_ref, bhi_ref, blo_ref, s_ref, g_ref, mass)
+
+
 def turn_sum_kernel(order, *refs):
     parts, outs = refs[:2], refs[2:]
     n = outs[0].shape[0]
@@ -177,11 +182,11 @@
 VM = pl.BlockSpec(memory_space=pltpu.VMEM)
 
 
-def call(kernel, outs, scratch, *args, limit=6 * MIB, cost=None):
+def call(kernel, outs, scratch, *args, limit=6 * MIB, cost=None, ins=None):
     return pl.pallas_call(
         kernel,
         out_shape=outs,
-        in_specs=[VM] * len(args),
+        in_specs=ins or [VM] * len(args),
         out_specs=[VM] * len(outs),
         scratch_shapes=scratch,
         cost_estimate=cost,
@@ -232,11 +237,12 @@
         (points_b, place(0, 0)), (up, place(3, 0)), (down, place(1, 0)), (low, place(2, 0)), (high, place(2, 0, half)),
         (swap(points_b), place(0, 1)), (swap(up), place(3, 1)), (swap(down), place(1, 1)),
         (swap(low), place(2, 1)), (swap(high), place(2, 1, half))]
-    bhi, blo, b2 = call(
+    left, a2, bhi, blo, b2 = call(
         lambda *r: pieces_kernel(eps, [p for x, p in pieces], *r),
-        [v16(rows_b, width), v16(rows_b, width), v32(1, rows_b)], [], *[x for x, p in pieces],
-        cost=pl.CostEstimate(flops=0, bytes_accessed=64 * MIB, transcendentals=0))
-    left, a2 = call(lambda *r: prepare_kernel(eps, *r), [v16(rows_a, 3 * width), v32(1, rows_a)], [], whole_a)
+        [v16(rows_a, 3 * width), v32(1, rows_a), v16(rows_b, width), v16(rows_b, width), v32(1, rows_b)],
+        [v32(rows_b, width), pltpu.SemaphoreType.DMA((len(pieces),))],
+        whole_a, *[x for x, p in pieces], limit=12 * MIB,
+        ins=[VM] + [pl.BlockSpec(memory_space=pl.ANY)] * len(pieces))
     s, rows = call(
         lambda *r: scores_kernel(piece, *r),
         [v32(rows_a, rows_b), v32(nb, rows_a)], [v32(rows_a, LANES), v32(rows_a, LANES)],
@@ -248,16 +254,11 @@
                 [f32(nb, rows_a)],
                 [v32(8, rows_b), v32(rows_a, LANES), v32(rows_a, LANES)],
                 part, s)
-        cols, alpha, pot_a = call(
+        cols, awide, pot_a = call(
             lambda *r: col_pass_kernel(log_b, eps, *r),
-            [f32(na, rows_b), v32(1, rows_a), f32(1, rows_a)],
-            [v32(rows_a, LANES)],
+            [f32(na, rows_b), v32(rows_a, LANES), f32(1, rows_a)], [],
             spread(rows, "ba"), a2, s)
         part = spread(cols, "aa")
-    awide, bwide, pot_b = call(
-        lambda *r: weights_kernel(log_a, log_b, eps, *r),
-        [v32(rows_a, LANES), v32(8, rows_b), f32(1, rows_b)], [], part, alpha, b2)
-
     def along_x(v, by):
         return lax.ppermute(v, "ba", [(i, (i + side * by) % nb) for i in range(nb)])
 
@@ -267,11 +268,22 @@
     side = math.isqrt(nb)
     step = pl.CostEstimate(flops=2 * rows_a // side * width * rows_b, bytes_accessed=MIB, transcendentals=0)
     held = []
+    group = rows_a // side
+    shared = awide, whole_a, bhi, blo, s
     for by in [2, 1, 3, 0]:
-        g, = call(
-            lambda *r: grad_kernel(lambda: lax.rem(lax.axis_index("ba") // side + by, side) * (rows_a // side), *r),
-            [v32(rows_a // side, width)], [v32(rows_a // side, LANES)],
-            awide, bwide, whole_a, bhi, blo, s, limit=12 * MIB, cost=step)
+        def first():
+            return lax.rem(lax.axis_index("ba") // side + by, side) * group
+
+        if not held:
+            bwide, pot_b, g = call(
+                lambda *r: first_grad_kernel(log_a, log_b, eps, first, *r),
+                [v32(8, rows_b), f32(1, rows_b), v32(group, width)], [v32(group, LANES)],
+                part, b2, *shared, limit=12 * MIB, cost=step)
+        else:
+            g, = call(
+                lambda awide, a, bhi, blo, s, bwide, *r: grad_kernel(first, awide, bwide, a, bhi, blo, s, *r),
+                [v32(group, width)], [v32(group, LANES)],
+                *shared, bwide, limit=12 * MIB, cost=step)
         held.append(along_x(g, by) if by else g)
     *arrived, total = held
     long = pl.CostEstimate(flops=9 * step.flops, bytes_accessed=4 * MIB, transcendentals=0)

time: 120 us -> 119 us (level)
    pallas_call x16 -> x14, Pallas kernels: 29.9 us -> 29.8 us  [call(): pl.pallas_call(kernel, out_shape=outs, in_specs=ins or [VM] * len(args),...]
  transfers between devices with their start and end apart: 16 -> 16, of which waited for: 8 -> 7; matrix products, arithmetic and copies ran while one was open for 0% -> 0% of each run, Pallas kernels for 6% -> 6%
where the time goes in v6:
time: 119 us
  blocking collectives  42.3 us (36%)
  Pallas kernels  29.8 us (25%)
  starting transfers between devices  24.5 us (21%)
  waiting for transfers between devices  19.9 us (17%)
  local copies, waits for them, and re-layouts  1.48 us (1%)
    all_to_all x4, blocking collectives, spread(): return lax.all_to_all(x, axis, 0, 0, tiled=True)  42.3 us
    pallas_call x14, Pallas kernels, call(): pl.pallas_call(kernel, out_shape=outs, in_specs=ins or [VM] * len(args),...  29.8 us
    ppermute x4, waiting for transfers between devices, move(): return lax.ppermute(x, 'aa', [(i, (i + 2 * by) % na) for i in range(na)])  8.74 us
    ppermute x4, starting transfers between devices, move(): return lax.ppermute(x, 'aa', [(i, (i + 2 * by) % na) for i in range(na)])  7.56 us
    all_to_all x1, starting transfers between devices, spread(): return lax.all_to_all(x, axis, 0, 0, tiled=True)  7.03 us
    ppermute x3, starting transfers between devices, along_y(): lax.ppermute(v, 'ba', [(i, i // side * side + (i + by) % side) for i in r...  4.71 us
    ppermute x3, starting transfers between devices, along_x(): return lax.ppermute(v, 'ba', [(i, (i + side * by) % nb) for i in range(nb)])  4.58 us
    all_to_all x1, waiting for transfers between devices, spread(): return lax.all_to_all(x, axis, 0, 0, tiled=True)  4.48 us
  transfers between devices with their start and end apart: 16, of which 7 were waited for; matrix products, arithmetic and copies ran while one was open for 0% of the time, Pallas kernels for 6%

profile of v6, /device:TPU:0, one launch (start us, length us, event | category | flops | bytes accessed | tf_op | source)
XLA Modules:
  0.0 118.8 jit_solution(9491118776464827823)
XLA Ops:
  0.6 2.1 %collective-permute-start = (f32[512,256]{1,0:T(8,128)}, f32[512,256]{1,0:T(8,128)S(1)}, u32[]{:S(2)}, u32[]{:S(2)}) collective-permute-start(f32[512,256]{1,0:T(8,128)} %r_1_.1), channel_id=1, source_target_pairs={{0,32},{16,48},{32,64},{48,80},{64,96},{80,112},{96,0},{112,16},{1... | collective-permute-start | bytes 1572872 | tf_op jit(solution)/shard_map/ppermute | solution.py:223
  2.7 2.2 %collective-permute-start.1 = (f32[512,256]{1,0:T(8,128)}, f32[512,256]{1,0:T(8,128)S(1)}, u32[]{:S(2)}, u32[]{:S(2)}) collective-permute-start(f32[512,256]{1,0:T(8,128)} %r_1_.1), channel_id=1, source_target_pairs={{0,96},{16,112},{32,0},{48,16},{64,32},{80,48},{96,64},{112,80},{1... | collective-permute-start | bytes 1572872 | tf_op jit(solution)/shard_map/ppermute | solution.py:223
  6.8 7.0 %all-to-all-start = ((f32[16,64,256]{2,1,0:T(8,128)}), f32[16,64,256]{2,1,0:T(8,128)S(1)}, u32[]{:S(2)}, u32[]{:S(2)}) async-start(f32[16,64,256]{2,1,0:T(8,128)} %shard_map.49), calls=%async_computation | async-start | bytes 2097152 | tf_op jit(solution)/shard_map/all_to_all | solution.py:210
  14.0 3.0 %collective-permute-done.r_2_ = f32[512,256]{1,0:T(8,128)S(1)} collective-permute-done((f32[512,256]{1,0:T(8,128)}, f32[512,256]{1,0:T(8,128)S(1)}, u32[]{:S(2)}, u32[]{:S(2)}) %collective-permute-start) | collective-permute-done | bytes 524320 | tf_op jit(solution)/shard_map/ppermute | solution.py:223
  17.7 3.2 %collective-permute-start.3 = (f32[256,256]{1,0:T(8,128)S(1)}, f32[256,256]{1,0:T(8,128)}, u32[]{:S(2)}, u32[]{:S(2)}) collective-permute-start(f32[256,256]{1,0:T(8,128)S(1)} %slice.9), channel_id=1, source_target_pairs={{0,96},{16,112},{32,0},{48,16},{64,32},{80,48},{96,64},{112,80},{1... | collective-permute-start | bytes 786440 | tf_op jit(solution)/shard_map/ppermute | solution.py:223
  20.9 4.9 %collective-permute-done.2.r_4_ = f32[256,256]{1,0:T(8,128)S(1)} collective-permute-done((f32[256,256]{1,0:T(8,128)S(1)}, f32[256,256]{1,0:T(8,128)S(1)}, u32[]{:S(2)}, u32[]{:S(2)}) %collective-permute-start.2) | collective-permute-done | bytes 262176 | tf_op jit(solution)/shard_map/ppermute | solution.py:223
  26.6 4.5 %all-to-all-done = f32[16,64,256]{2,1,0:T(8,128)S(1)} async-done(((f32[16,64,256]{2,1,0:T(8,128)}), f32[16,64,256]{2,1,0:T(8,128)S(1)}, u32[]{:S(2)}, u32[]{:S(2)}) %all-to-all-start) | async-done | bytes 1048608 | tf_op jit(solution)/shard_map/all_to_all | solution.py:210
  31.1 2.1 %shard_map.50 = (bf16[1024,768]{1,0:T(8,128)(2,1)S(1)}, f32[1,1024]{1,0:T(1,128)S(1)}, bf16[4096,256]{1,0:T(8,128)(2,1)S(1)}, bf16[4096,256]{1,0:T(8,128)(2,1)S(1)}, f32[1,4096]{1,0:T(1,128)S(1)}) custom-call(f32[1024,256]{1,0:T(8,128)S(1)} %bitcast.19, f32[512,256]{1,0:T(8,128)S(1)} %copy-done, f32[512,256]{1,0:T(8,128)S(1)} %collective-permute-done.r_2_, ...), custom_call_target="tpu_custom_call" | custom-call | tf_op jit(solution)/shard_map/pallas_call | solution.py:186
  33.2 7.5 %shard_map.51 = (f32[1024,4096]{1,0:T(8,128)S(1)}, f32[16,1024]{1,0:T(8,128)S(1)}) custom-call(bf16[1024,768]{1,0:T(8,128)(2,1)S(1)} %get-tuple-element.21.r_0_, bf16[4096,256]{1,0:T(8,128)(2,1)S(1)} %get-tuple-element.22.r_1_.r_4_.bhi, bf16[4096,256]{1,0:T(8,128)(2,1)S(1)} %get-tuple-element.23.r_2_.r_5_.blo, f32[1,4096]{1,0:T(1,128)S(1)} %get-tuple-element.24.r_3_.r_1_), custom_call_target="tpu_custom_call" | custom-call | tf_op jit(solution)/shard_map/pallas_call | solution.py:186
  40.8 11.9 %all_to_all.49 = f32[16,1,1024]{2,1,0:T(1,128)S(1)} all-to-all(f32[16,1,1024]{2,1,0:T(1,128)S(1)} %copy.5), channel_id=1, replica_groups=mesh['aa'=8,'ba'=16] {'ba'}, dimensions={0} | all-to-all | bytes 131072 | tf_op jit(solution)/shard_map/all_to_all | solution.py:210
  52.7 3.1 %shard_map.52 = (f32[8,4096]{1,0:T(8,128)S(1)}, f32[1024,128]{1,0:T(8,128)}, f32[1,1024]{1,0:T(1,128)}) custom-call(f32[16,1024]{1,0:T(8,128)S(1)} %bitcast.26, f32[1,1024]{1,0:T(1,128)S(1)} %get-tuple-element.26.r_1_, f32[1024,4096]{1,0:T(8,128)S(1)} %get-tuple-element.27.r_2_.r_1_.r_6_.s), custom_call_target="tpu_custom_call" | custom-call | tf_op jit(solution)/shard_map/pallas_call | solution.py:186
  56.0 11.0 %all_to_all.50 = f32[8,1,4096]{2,1,0:T(1,128)S(1)} all-to-all(f32[8,1,4096]{2,1,0:T(1,128)S(1)} %copy.6), channel_id=1, replica_groups=mesh['aa'=8,'ba'=16] {'aa'}, dimensions={0} | all-to-all | bytes 262144 | tf_op jit(solution)/shard_map/all_to_all | solution.py:210
  67.0 3.3 %shard_map.53 = f32[16,1024]{1,0:T(8,128)S(1)} custom-call(f32[8,4096]{1,0:T(8,128)S(1)} %bitcast.25, f32[1024,4096]{1,0:T(8,128)S(1)} %get-tuple-element.27.r_2_.r_1_.r_6_.s), custom_call_target="tpu_custom_call" | custom-call | tf_op jit(solution)/shard_map/pallas_call | solution.py:186
  70.4 10.9 %all_to_all.51 = f32[16,1,1024]{2,1,0:T(1,128)S(1)} all-to-all(f32[16,1,1024]{2,1,0:T(1,128)S(1)} %copy.7), channel_id=1, replica_groups=mesh['aa'=8,'ba'=16] {'ba'}, dimensions={0} | all-to-all | bytes 131072 | tf_op jit(solution)/shard_map/all_to_all | solution.py:210
  81.3 3.1 %shard_map.54 = (f32[8,4096]{1,0:T(8,128)S(1)}, f32[1024,128]{1,0:T(8,128)S(1)}, f32[1,1024]{1,0:T(1,128)}) custom-call(f32[16,1024]{1,0:T(8,128)S(1)} %bitcast.27, f32[1,1024]{1,0:T(1,128)S(1)} %get-tuple-element.26.r_1_, f32[1024,4096]{1,0:T(8,128)S(1)} %get-tuple-element.27.r_2_.r_1_.r_6_.s), custom_call_target="tpu_custom_call" | custom-call | tf_op jit(solution)/shard_map/pallas_call | solution.py:186
  84.6 8.5 %all_to_all.52 = f32[8,1,4096]{2,1,0:T(1,128)S(1)} all-to-all(f32[8,1,4096]{2,1,0:T(1,128)S(1)} %copy.8), channel_id=1, replica_groups=mesh['aa'=8,'ba'=16] {'aa'}, dimensions={0} | all-to-all | bytes 262144 | tf_op jit(solution)/shard_map/all_to_all | solution.py:210
  93.2 2.8 %shard_map.55 = (f32[8,4096]{1,0:T(8,128)S(1)}, f32[1,4096]{1,0:T(1,128)}, f32[256,256]{1,0:T(8,128)S(1)}) custom-call(f32[8,4096]{1,0:T(8,128)S(1)} %bitcast.24, f32[1,4096]{1,0:T(1,128)S(1)} %get-tuple-element.24.r_3_.r_1_, f32[1024,128]{1,0:T(8,128)S(1)} %get-tuple-element.31.r_2_.awide, f32[1024,256]{1,0:T(8,128)S(1)} %bitcast.20, ...), custom_call_target="tpu_custom_call" | custom-call | flops 536870912 | bytes 1048576 | tf_op jit(solution)/shard_map/pallas_call | solution.py:186
  97.1 2.0 %shard_map.58 = f32[256,256]{1,0:T(8,128)S(1)} custom-call(f32[1024,128]{1,0:T(8,128)S(1)} %get-tuple-element.31.r_2_.awide, f32[1024,256]{1,0:T(8,128)S(1)} %bitcast.21, bf16[4096,256]{1,0:T(8,128)(2,1)S(1)} %get-tuple-element.22.r_1_.r_4_.bhi, bf16[4096,256]{1,0:T(8,128)(2,1)S(1)} %get-tuple-element.23.r_2_.r_5_.blo, ...), custom_call_target="tpu_custom_call" | custom-call | flops 536870912 | bytes 1048576 | tf_op jit(solution)/shard_map/pallas_call | solution.py:186
  100.0 2.0 %shard_map.60 = f32[256,256]{1,0:T(8,128)S(1)} custom-call(f32[1024,128]{1,0:T(8,128)S(1)} %get-tuple-element.31.r_2_.awide, f32[1024,256]{1,0:T(8,128)S(1)} %bitcast.22, bf16[4096,256]{1,0:T(8,128)(2,1)S(1)} %get-tuple-element.22.r_1_.r_4_.bhi, bf16[4096,256]{1,0:T(8,128)(2,1)S(1)} %get-tuple-element.23.r_2_.r_5_.blo, ...), custom_call_target="tpu_custom_call" | custom-call | flops 536870912 | bytes 1048576 | tf_op jit(solution)/shard_map/pallas_call | solution.py:186
  102.1 2.5 %collective-permute-start.11 = (f32[256,256]{1,0:T(8,128)S(1)}, f32[256,256]{1,0:T(8,128)S(1)}, u32[]{:S(2)}, u32[]{:S(2)}) collective-permute-start(f32[256,256]{1,0:T(8,128)S(1)} %shard_map.60), channel_id=1, source_target_pairs={{0,12},{1,13},{2,14},{3,15},{4,0},{5,1},{6,2},{7,3},{8,4},{9,5},{1... | collective-permute-start | bytes 786440 | tf_op jit(solution)/shard_map/ppermute | solution.py:263
  104.6 2.0 %shard_map.56.refs_0_ = f32[256,256]{1,0:T(8,128)S(1)} custom-call(f32[1024,128]{1,0:T(8,128)S(1)} %get-tuple-element.31.r_2_.awide, f32[1024,256]{1,0:T(8,128)S(1)} %bitcast.23, bf16[4096,256]{1,0:T(8,128)(2,1)S(1)} %get-tuple-element.22.r_1_.r_4_.bhi, bf16[4096,256]{1,0:T(8,128)(2,1)S(1)} %get-tuple-element.23.r_2_.r_5_.blo, ...), custom_call_target="tpu_custom_call" | custom-call | flops 536870912 | bytes 1048576 | tf_op jit(solution)/shard_map/pallas_call | solution.py:186
  106.7 4.2 %collective-permute-done.10.refs_1_ = f32[256,256]{1,0:T(8,128)S(1)} collective-permute-done((f32[256,256]{1,0:T(8,128)S(1)}, f32[256,256]{1,0:T(8,128)S(1)}, u32[]{:S(2)}, u32[]{:S(2)}) %collective-permute-start.10) | collective-permute-done | bytes 262176 | tf_op jit(solution)/shard_map/ppermute | solution.py:263
  113.2 2.5 %collective-permute-start.14 = (f32[64,256]{1,0:T(8,128)S(1)}, f32[64,256]{1,0:T(8,128)S(1)}, u32[]{:S(2)}, u32[]{:S(2)}) collective-permute-start(f32[64,256]{1,0:T(8,128)S(1)} %get-tuple-element.38), channel_id=1, source_target_pairs={{0,3},{1,0},{2,1},{3,2},{4,7},{5,4},{6,5},{7,6},{8,11},{9,8},{10,9... | collective-permute-start | bytes 196616 | tf_op jit(solution)/shard_map/ppermute | solution.py:266
  115.7 1.9 %collective-permute-done.12.refs_1_ = f32[64,256]{1,0:T(8,128)S(1)} collective-permute-done((f32[64,256]{1,0:T(8,128)S(1)}, f32[64,256]{1,0:T(8,128)S(1)}, u32[]{:S(2)}, u32[]{:S(2)}) %collective-permute-start.12) | collective-permute-done | bytes 65568 | tf_op jit(solution)/shard_map/ppermute | solution.py:266
  (40 shorter events, 9.7 us)
Async XLA Ops:
  0.6 13.2 %copy-start = (f32[512,256]{1,0:T(8,128)S(1)}, f32[512,256]{1,0:T(8,128)}, u32[]{:S(2)}) copy-start(f32[512,256]{1,0:T(8,128)} %r_1_.1) | copy-start | bytes 1572868
  0.6 16.3 %collective-permute-start = (f32[512,256]{1,0:T(8,128)}, f32[512,256]{1,0:T(8,128)S(1)}, u32[]{:S(2)}, u32[]{:S(2)}) collective-permute-start(f32[512,256]{1,0:T(8,128)} %r_1_.1), channel_id=1, source_target_pairs={{0,32},{16,48},{32,64},{48,80},{64,96},{80,112},{96,0},{112,16},{1... | collective-permute-start | bytes 1572872 | tf_op jit(solution)/shard_map/ppermute | solution.py:223
  2.7 14.5 %collective-permute-start.1 = (f32[512,256]{1,0:T(8,128)}, f32[512,256]{1,0:T(8,128)S(1)}, u32[]{:S(2)}, u32[]{:S(2)}) collective-permute-start(f32[512,256]{1,0:T(8,128)} %r_1_.1), channel_id=1, source_target_pairs={{0,96},{16,112},{32,0},{48,16},{64,32},{80,48},{96,64},{112,80},{1... | collective-permute-start | bytes 1572872 | tf_op jit(solution)/shard_map/ppermute | solution.py:223
  4.9 0.8 copy-start.1
  6.8 24.3 %all-to-all-start = ((f32[16,64,256]{2,1,0:T(8,128)}), f32[16,64,256]{2,1,0:T(8,128)S(1)}, u32[]{:S(2)}, u32[]{:S(2)}) async-start(f32[16,64,256]{2,1,0:T(8,128)} %shard_map.49), calls=%async_computation | async-start | bytes 2097152 | tf_op jit(solution)/shard_map/all_to_all | solution.py:210
  13.9 12.8 %collective-permute-start.4 = (f32[512,256]{1,0:T(8,128)S(1)}, f32[512,256]{1,0:T(8,128)S(1)}, u32[]{:S(2)}, u32[]{:S(2)}) collective-permute-start(f32[512,256]{1,0:T(8,128)S(1)} %copy-done), channel_id=1, source_target_pairs={{0,16},{16,0},{32,48},{48,32},{64,80},{80,64},{96,112},{112,96},{1... | collective-permute-start | bytes 1572872 | tf_op jit(solution)/shard_map/ppermute | solution.py:226
  17.0 8.8 %collective-permute-start.2 = (f32[256,256]{1,0:T(8,128)S(1)}, f32[256,256]{1,0:T(8,128)S(1)}, u32[]{:S(2)}, u32[]{:S(2)}) collective-permute-start(f32[256,256]{1,0:T(8,128)S(1)} %slice.8), channel_id=1, source_target_pairs={{0,32},{16,48},{32,64},{48,80},{64,96},{80,112},{96,0},{112,16},{1... | collective-permute-start | bytes 786440 | tf_op jit(solution)/shard_map/ppermute | solution.py:223
  17.1 14.1 %collective-permute-start.5 = (f32[512,256]{1,0:T(8,128)S(1)}, f32[512,256]{1,0:T(8,128)}, u32[]{:S(2)}, u32[]{:S(2)}) collective-permute-start(f32[512,256]{1,0:T(8,128)S(1)} %collective-permute-done.r_2_), channel_id=1, source_target_pairs={{0,16},{16,0},{32,48},{48,32},{64,80},{80,64},{96,112},{112,96},{1... | collective-permute-start | bytes 1572872 | tf_op jit(solution)/shard_map/ppermute | solution.py:226
  17.2 14.0 %collective-permute-start.6 = (f32[512,256]{1,0:T(8,128)S(1)}, f32[512,256]{1,0:T(8,128)}, u32[]{:S(2)}, u32[]{:S(2)}) collective-permute-start(f32[512,256]{1,0:T(8,128)S(1)} %collective-permute-done.1.r_3_), channel_id=1, source_target_pairs={{0,16},{16,0},{32,48},{48,32},{64,80},{80,64},{96,112},{112,96},{1... | collective-permute-start | bytes 1572872 | tf_op jit(solution)/shard_map/ppermute | solution.py:226
  17.7 8.9 %collective-permute-start.3 = (f32[256,256]{1,0:T(8,128)S(1)}, f32[256,256]{1,0:T(8,128)}, u32[]{:S(2)}, u32[]{:S(2)}) collective-permute-start(f32[256,256]{1,0:T(8,128)S(1)} %slice.9), channel_id=1, source_target_pairs={{0,96},{16,112},{32,0},{48,16},{64,32},{80,48},{96,64},{112,80},{1... | collective-permute-start | bytes 786440 | tf_op jit(solution)/shard_map/ppermute | solution.py:223
  25.8 5.4 %collective-permute-start.7 = (f32[256,256]{1,0:T(8,128)S(1)}, f32[256,256]{1,0:T(8,128)}, u32[]{:S(2)}, u32[]{:S(2)}) collective-permute-start(f32[256,256]{1,0:T(8,128)S(1)} %collective-permute-done.2.r_4_), channel_id=1, source_target_pairs={{0,16},{16,0},{32,48},{48,32},{64,80},{80,64},{96,112},{112,96},{1... | collective-permute-start | bytes 786440 | tf_op jit(solution)/shard_map/ppermute | solution.py:226
  26.6 4.5 %collective-permute-start.8 = (f32[256,256]{1,0:T(8,128)}, f32[256,256]{1,0:T(8,128)}, u32[]{:S(2)}, u32[]{:S(2)}) collective-permute-start(f32[256,256]{1,0:T(8,128)} %collective-permute-done.3.r_5_), channel_id=1, source_target_pairs={{0,16},{16,0},{32,48},{48,32},{64,80},{80,64},{96,112},{112,96},{1... | collective-permute-start | bytes 786440 | tf_op jit(solution)/shard_map/ppermute | solution.py:226
  95.9 10.7 %collective-permute-start.9 = (f32[256,256]{1,0:T(8,128)S(1)}, f32[256,256]{1,0:T(8,128)S(1)}, u32[]{:S(2)}, u32[]{:S(2)}) collective-permute-start(f32[256,256]{1,0:T(8,128)S(1)} %get-tuple-element.34), channel_id=1, source_target_pairs={{0,8},{1,9},{2,10},{3,11},{4,12},{5,13},{6,14},{7,15},{8,0},{9,1},... | collective-permute-start | bytes 786440 | tf_op jit(solution)/shard_map/ppermute | solution.py:263
  99.2 11.7 %collective-permute-start.10 = (f32[256,256]{1,0:T(8,128)S(1)}, f32[256,256]{1,0:T(8,128)S(1)}, u32[]{:S(2)}, u32[]{:S(2)}) collective-permute-start(f32[256,256]{1,0:T(8,128)S(1)} %shard_map.58), channel_id=1, source_target_pairs={{0,4},{1,5},{2,6},{3,7},{4,8},{5,9},{6,10},{7,11},{8,12},{9,13},{1... | collective-permute-start | bytes 786440 | tf_op jit(solution)/shard_map/ppermute | solution.py:263
  102.1 8.9 %collective-permute-start.11 = (f32[256,256]{1,0:T(8,128)S(1)}, f32[256,256]{1,0:T(8,128)S(1)}, u32[]{:S(2)}, u32[]{:S(2)}) collective-permute-start(f32[256,256]{1,0:T(8,128)S(1)} %shard_map.60), channel_id=1, source_target_pairs={{0,12},{1,13},{2,14},{3,15},{4,0},{5,1},{6,2},{7,3},{8,4},{9,5},{1... | collective-permute-start | bytes 786440 | tf_op jit(solution)/shard_map/ppermute | solution.py:263
  111.0 6.6 %collective-permute-start.12 = (f32[64,256]{1,0:T(8,128)S(1)}, f32[64,256]{1,0:T(8,128)S(1)}, u32[]{:S(2)}, u32[]{:S(2)}) collective-permute-start(f32[64,256]{1,0:T(8,128)S(1)} %get-tuple-element.36), channel_id=1, source_target_pairs={{0,2},{1,3},{2,0},{3,1},{4,6},{5,7},{6,4},{7,5},{8,10},{9,11},{10,... | collective-permute-start | bytes 196616 | tf_op jit(solution)/shard_map/ppermute | solution.py:266
  112.5 5.6 %collective-permute-start.13 = (f32[64,256]{1,0:T(8,128)S(1)}, f32[64,256]{1,0:T(8,128)S(1)}, u32[]{:S(2)}, u32[]{:S(2)}) collective-permute-start(f32[64,256]{1,0:T(8,128)S(1)} %get-tuple-element.37), channel_id=1, source_target_pairs={{0,1},{1,2},{2,3},{3,0},{4,5},{5,6},{6,7},{7,4},{8,9},{9,10},{10,1... | collective-permute-start | bytes 196616 | tf_op jit(solution)/shard_map/ppermute | solution.py:266
  113.2 4.9 %collective-permute-start.14 = (f32[64,256]{1,0:T(8,128)S(1)}, f32[64,256]{1,0:T(8,128)S(1)}, u32[]{:S(2)}, u32[]{:S(2)}) collective-permute-start(f32[64,256]{1,0:T(8,128)S(1)} %get-tuple-element.38), channel_id=1, source_target_pairs={{0,3},{1,0},{2,1},{3,2},{4,7},{5,4},{6,5},{7,6},{8,11},{9,8},{10,9... | collective-permute-start | bytes 196616 | tf_op jit(solution)/shard_map/ppermute | solution.py:266

commit v7 on v6

--- a/solution.py
+++ b/solution.py
@@ -119,7 +119,7 @@
     return xs[0]
 
 
-def col_pass_kernel(log_b, eps, part_ref, a2_ref, s_ref, out_ref, wide, pot_ref):
+def col_pass_kernel(log_b, eps, part_ref, a2_ref, s_ref, out_ref, pot_ref, wide):
     alpha = -combine(part_ref[...]) - log_b
     pot_ref[...] = (alpha + a2_ref[...]) * (eps / LOG2E)
     wide[...] = jnp.broadcast_to(alpha, (LANES, alpha.shape[1])).T
@@ -159,12 +159,10 @@
     g_ref[...] = 2.0 * (a_ref[rows, :] * jnp.sum(mass[...], axis=1, keepdims=True) - g_ref[...])
 
 
-def first_grad_kernel(log_a, log_b, eps, first, part_ref, b2_ref, awide_ref, a_ref, bhi_ref, blo_ref, s_ref,
-                      bwide_ref, pot_ref, g_ref, mass):
+def weights_kernel(log_a, log_b, eps, part_ref, b2_ref, bwide_ref, pot_ref):
     beta = -combine(part_ref[...]) - log_a
     pot_ref[...] = (beta + b2_ref[...]) * (eps / LOG2E)
     bwide_ref[...] = jnp.broadcast_to(beta + log_b, bwide_ref.shape)
-    grad_kernel(first, awide_ref, bwide_ref, a_ref, bhi_ref, blo_ref, s_ref, g_ref, mass)
 
 
 def turn_sum_kernel(order, *refs):
@@ -254,9 +252,11 @@
                 [f32(nb, rows_a)],
                 [v32(8, rows_b), v32(rows_a, LANES), v32(rows_a, LANES)],
                 part, s)
-        cols, awide, pot_a = call(
+        final = turn == ITERS - 1
+        wide_shape = [v32(rows_a, LANES)]
+        cols, pot_a, *awide = call(
             lambda *r: col_pass_kernel(log_b, eps, *r),
-            [f32(na, rows_b), v32(rows_a, LANES), f32(1, rows_a)], [],
+            [f32(na, rows_b), f32(1, rows_a)] + wide_shape * final, wide_shape * (not final),
             spread(rows, "ba"), a2, s)
         part = spread(cols, "aa")
     def along_x(v, by):
@@ -268,22 +268,13 @@
     side = math.isqrt(nb)
     step = pl.CostEstimate(flops=2 * rows_a // side * width * rows_b, bytes_accessed=MIB, transcendentals=0)
     held = []
-    group = rows_a // side
-    shared = awide, whole_a, bhi, blo, s
+    bwide, pot_b = call(
+        lambda *r: weights_kernel(log_a, log_b, eps, *r), [v32(8, rows_b), f32(1, rows_b)], [], part, b2)
     for by in [2, 1, 3, 0]:
-        def first():
-            return lax.rem(lax.axis_index("ba") // side + by, side) * group
-
-        if not held:
-            bwide, pot_b, g = call(
-                lambda *r: first_grad_kernel(log_a, log_b, eps, first, *r),
-                [v32(8, rows_b), f32(1, rows_b), v32(group, width)], [v32(group, LANES)],
-                part, b2, *shared, limit=12 * MIB, cost=step)
-        else:
-            g, = call(
-                lambda awide, a, bhi, blo, s, bwide, *r: grad_kernel(first, awide, bwide, a, bhi, blo, s, *r),
-                [v32(group, width)], [v32(group, LANES)],
-                *shared, bwide, limit=12 * MIB, cost=step)
+        g, = call(
+            lambda *r: grad_kernel(lambda: lax.rem(lax.axis_index("ba") // side + by, side) * (rows_a // side), *r),
+            [v32(rows_a // side, width)], [v32(rows_a // side, LANES)],
+            *awide, bwide, whole_a, bhi, blo, s, limit=12 * MIB, cost=step)
         held.append(along_x(g, by) if by else g)
     *arrived, total = held
     long = pl.CostEstimate(flops=9 * step.flops, bytes_accessed=4 * MIB, transcendentals=0)

time: 119 us -> 120 us (level)
    pallas_call x14 -> x15, Pallas kernels: 29.8 us -> 29.8 us  [call(): pl.pallas_call(kernel, out_shape=outs, in_specs=ins or [VM] * len(args),...]
where the time goes in v7:
time: 120 us; the launch traced here: 119 us
  blocking collectives  42.3 us (35%)
  Pallas kernels  29.8 us (25%)
  starting transfers between devices  24.8 us (21%)
  waiting for transfers between devices  19.9 us (17%)
  local copies, waits for them, and re-layouts  1.48 us (1%)
    all_to_all x4, blocking collectives, spread(): return lax.all_to_all(x, axis, 0, 0, tiled=True)  42.3 us
    pallas_call x15, Pallas kernels, call(): pl.pallas_call(kernel, out_shape=outs, in_specs=ins or [VM] * len(args),...  29.8 us
    ppermute x4, waiting for transfers between devices, move(): return lax.ppermute(x, 'aa', [(i, (i + 2 * by) % na) for i in range(na)])  8.74 us
    ppermute x4, starting transfers between devices, move(): return lax.ppermute(x, 'aa', [(i, (i + 2 * by) % na) for i in range(na)])  7.56 us
    all_to_all x1, starting transfers between devices, spread(): return lax.all_to_all(x, axis, 0, 0, tiled=True)  7.03 us
    ppermute x3, starting transfers between devices, along_x(): return lax.ppermute(v, 'ba', [(i, (i + side * by) % nb) for i in range(nb)])  4.88 us
    ppermute x3, starting transfers between devices, along_y(): lax.ppermute(v, 'ba', [(i, i // side * side + (i + by) % side) for i in r...  4.7 us
    all_to_all x1, waiting for transfers between devices, spread(): return lax.all_to_all(x, axis, 0, 0, tiled=True)  4.48 us
  transfers between devices with their start and end apart: 16, of which 7 were waited for; matrix products, arithmetic and copies ran while one was open for 0% of the time, Pallas kernels for 6%

profile of v7, /device:TPU:0, one launch (start us, length us, event | category | flops | bytes accessed | tf_op | source)
XLA Modules:
  0.0 119.0 jit_solution(9933837265455057269)
XLA Ops:
  0.6 2.1 %collective-permute-start = (f32[512,256]{1,0:T(8,128)}, f32[512,256]{1,0:T(8,128)S(1)}, u32[]{:S(2)}, u32[]{:S(2)}) collective-permute-start(f32[512,256]{1,0:T(8,128)} %r_1_.1), channel_id=1, source_target_pairs={{0,32},{16,48},{32,64},{48,80},{64,96},{80,112},{96,0},{112,16},{1... | collective-permute-start | bytes 1572872 | tf_op jit(solution)/shard_map/ppermute | solution.py:221
  2.7 2.2 %collective-permute-start.1 = (f32[512,256]{1,0:T(8,128)}, f32[512,256]{1,0:T(8,128)S(1)}, u32[]{:S(2)}, u32[]{:S(2)}) collective-permute-start(f32[512,256]{1,0:T(8,128)} %r_1_.1), channel_id=1, source_target_pairs={{0,96},{16,112},{32,0},{48,16},{64,32},{80,48},{96,64},{112,80},{1... | collective-permute-start | bytes 1572872 | tf_op jit(solution)/shard_map/ppermute | solution.py:221
  6.8 7.0 %all-to-all-start = ((f32[16,64,256]{2,1,0:T(8,128)}), f32[16,64,256]{2,1,0:T(8,128)S(1)}, u32[]{:S(2)}, u32[]{:S(2)}) async-start(f32[16,64,256]{2,1,0:T(8,128)} %shard_map.49), calls=%async_computation | async-start | bytes 2097152 | tf_op jit(solution)/shard_map/all_to_all | solution.py:208
  14.0 3.0 %collective-permute-done.r_2_ = f32[512,256]{1,0:T(8,128)S(1)} collective-permute-done((f32[512,256]{1,0:T(8,128)}, f32[512,256]{1,0:T(8,128)S(1)}, u32[]{:S(2)}, u32[]{:S(2)}) %collective-permute-start) | collective-permute-done | bytes 524320 | tf_op jit(solution)/shard_map/ppermute | solution.py:221
  17.7 3.2 %collective-permute-start.3 = (f32[256,256]{1,0:T(8,128)S(1)}, f32[256,256]{1,0:T(8,128)}, u32[]{:S(2)}, u32[]{:S(2)}) collective-permute-start(f32[256,256]{1,0:T(8,128)S(1)} %slice.9), channel_id=1, source_target_pairs={{0,96},{16,112},{32,0},{48,16},{64,32},{80,48},{96,64},{112,80},{1... | collective-permute-start | bytes 786440 | tf_op jit(solution)/shard_map/ppermute | solution.py:221
  20.9 4.9 %collective-permute-done.2.r_4_ = f32[256,256]{1,0:T(8,128)S(1)} collective-permute-done((f32[256,256]{1,0:T(8,128)S(1)}, f32[256,256]{1,0:T(8,128)S(1)}, u32[]{:S(2)}, u32[]{:S(2)}) %collective-permute-start.2) | collective-permute-done | bytes 262176 | tf_op jit(solution)/shard_map/ppermute | solution.py:221
  26.6 4.5 %all-to-all-done = f32[16,64,256]{2,1,0:T(8,128)S(1)} async-done(((f32[16,64,256]{2,1,0:T(8,128)}), f32[16,64,256]{2,1,0:T(8,128)S(1)}, u32[]{:S(2)}, u32[]{:S(2)}) %all-to-all-start) | async-done | bytes 1048608 | tf_op jit(solution)/shard_map/all_to_all | solution.py:208
  31.1 2.1 %shard_map.50 = (bf16[1024,768]{1,0:T(8,128)(2,1)S(1)}, f32[1,1024]{1,0:T(1,128)S(1)}, bf16[4096,256]{1,0:T(8,128)(2,1)S(1)}, bf16[4096,256]{1,0:T(8,128)(2,1)S(1)}, f32[1,4096]{1,0:T(1,128)S(1)}) custom-call(f32[1024,256]{1,0:T(8,128)S(1)} %bitcast.19, f32[512,256]{1,0:T(8,128)S(1)} %copy-done, f32[512,256]{1,0:T(8,128)S(1)} %collective-permute-done.r_2_, ...), custom_call_target="tpu_custom_call" | custom-call | tf_op jit(solution)/shard_map/pallas_call | solution.py:184
  33.2 7.5 %shard_map.51 = (f32[1024,4096]{1,0:T(8,128)S(1)}, f32[16,1024]{1,0:T(8,128)S(1)}) custom-call(bf16[1024,768]{1,0:T(8,128)(2,1)S(1)} %get-tuple-element.20.r_0_, bf16[4096,256]{1,0:T(8,128)(2,1)S(1)} %get-tuple-element.21.r_1_.r_3_, bf16[4096,256]{1,0:T(8,128)(2,1)S(1)} %get-tuple-element.22.r_2_.r_4_, f32[1,4096]{1,0:T(1,128)S(1)} %get-tuple-element.23.r_3_.r_1_), custom_call_target="tpu_custom_call" | custom-call | tf_op jit(solution)/shard_map/pallas_call | solution.py:184
  40.8 11.9 %all_to_all.49 = f32[16,1,1024]{2,1,0:T(1,128)S(1)} all-to-all(f32[16,1,1024]{2,1,0:T(1,128)S(1)} %copy.5), channel_id=1, replica_groups=mesh['aa'=8,'ba'=16] {'ba'}, dimensions={0} | all-to-all | bytes 131072 | tf_op jit(solution)/shard_map/all_to_all | solution.py:208
  52.7 3.1 %shard_map.52 = (f32[8,4096]{1,0:T(8,128)S(1)}, f32[1,1024]{1,0:T(1,128)}) custom-call(f32[16,1024]{1,0:T(8,128)S(1)} %bitcast.26, f32[1,1024]{1,0:T(1,128)S(1)} %get-tuple-element.25.r_1_, f32[1024,4096]{1,0:T(8,128)S(1)} %get-tuple-element.26.r_2_.r_1_.r_5_), custom_call_target="tpu_custom_call" | custom-call | tf_op jit(solution)/shard_map/pallas_call | solution.py:184
  55.9 11.0 %all_to_all.50 = f32[8,1,4096]{2,1,0:T(1,128)S(1)} all-to-all(f32[8,1,4096]{2,1,0:T(1,128)S(1)} %copy.6), channel_id=1, replica_groups=mesh['aa'=8,'ba'=16] {'aa'}, dimensions={0} | all-to-all | bytes 262144 | tf_op jit(solution)/shard_map/all_to_all | solution.py:208
  67.0 3.3 %shard_map.53 = f32[16,1024]{1,0:T(8,128)S(1)} custom-call(f32[8,4096]{1,0:T(8,128)S(1)} %bitcast.24, f32[1024,4096]{1,0:T(8,128)S(1)} %get-tuple-element.26.r_2_.r_1_.r_5_), custom_call_target="tpu_custom_call" | custom-call | tf_op jit(solution)/shard_map/pallas_call | solution.py:184
  70.4 10.9 %all_to_all.51 = f32[16,1,1024]{2,1,0:T(1,128)S(1)} all-to-all(f32[16,1,1024]{2,1,0:T(1,128)S(1)} %copy.7), channel_id=1, replica_groups=mesh['aa'=8,'ba'=16] {'ba'}, dimensions={0} | all-to-all | bytes 131072 | tf_op jit(solution)/shard_map/all_to_all | solution.py:208
  81.3 3.1 %shard_map.54 = (f32[8,4096]{1,0:T(8,128)S(1)}, f32[1,1024]{1,0:T(1,128)}, f32[1024,128]{1,0:T(8,128)S(1)}) custom-call(f32[16,1024]{1,0:T(8,128)S(1)} %bitcast.27, f32[1,1024]{1,0:T(1,128)S(1)} %get-tuple-element.25.r_1_, f32[1024,4096]{1,0:T(8,128)S(1)} %get-tuple-element.26.r_2_.r_1_.r_5_), custom_call_target="tpu_custom_call" | custom-call | tf_op jit(solution)/shard_map/pallas_call | solution.py:184
  84.6 8.5 %all_to_all.52 = f32[8,1,4096]{2,1,0:T(1,128)S(1)} all-to-all(f32[8,1,4096]{2,1,0:T(1,128)S(1)} %copy.8), channel_id=1, replica_groups=mesh['aa'=8,'ba'=16] {'aa'}, dimensions={0} | all-to-all | bytes 262144 | tf_op jit(solution)/shard_map/all_to_all | solution.py:208
  93.9 2.0 %shard_map.57 = f32[256,256]{1,0:T(8,128)S(1)} custom-call(f32[1024,128]{1,0:T(8,128)S(1)} %get-tuple-element.31.r_0_, f32[8,4096]{1,0:T(8,128)S(1)} %get-tuple-element.32.r_1_, f32[1024,256]{1,0:T(8,128)S(1)} %bitcast.20, bf16[4096,256]{1,0:T(8,128)(2,1)S(1)} %get-tuple-element.21.r_1_.r_3_, bf16[4096,256]{1,0:T(8,128)(2,1)S(1)} %get-tuple-element.22.r_2_.r_4_, ...), custom_call_target="tpu_custom_call" | custom-call | flops 536870912 | bytes 1048576 | tf_op jit(solution)/shard_map/pallas_call | solution.py:184
  97.4 2.0 %shard_map.59 = f32[256,256]{1,0:T(8,128)S(1)} custom-call(f32[1024,128]{1,0:T(8,128)S(1)} %get-tuple-element.31.r_0_, f32[8,4096]{1,0:T(8,128)S(1)} %get-tuple-element.32.r_1_, f32[1024,256]{1,0:T(8,128)S(1)} %bitcast.21, bf16[4096,256]{1,0:T(8,128)(2,1)S(1)} %get-tuple-element.21.r_1_.r_3_, bf16[4096,256]{1,0:T(8,128)(2,1)S(1)} %get-tuple-element.22.r_2_.r_4_, ...), custom_call_target="tpu_custom_call" | custom-call | flops 536870912 | bytes 1048576 | tf_op jit(solution)/shard_map/pallas_call | solution.py:184
  100.3 2.0 %shard_map.61 = f32[256,256]{1,0:T(8,128)S(1)} custom-call(f32[1024,128]{1,0:T(8,128)S(1)} %get-tuple-element.31.r_0_, f32[8,4096]{1,0:T(8,128)S(1)} %get-tuple-element.32.r_1_, f32[1024,256]{1,0:T(8,128)S(1)} %bitcast.22, bf16[4096,256]{1,0:T(8,128)(2,1)S(1)} %get-tuple-element.21.r_1_.r_3_, bf16[4096,256]{1,0:T(8,128)(2,1)S(1)} %get-tuple-element.22.r_2_.r_4_, ...), custom_call_target="tpu_custom_call" | custom-call | flops 536870912 | bytes 1048576 | tf_op jit(solution)/shard_map/pallas_call | solution.py:184
  102.3 2.5 %collective-permute-start.11 = (f32[256,256]{1,0:T(8,128)S(1)}, f32[256,256]{1,0:T(8,128)S(1)}, u32[]{:S(2)}, u32[]{:S(2)}) collective-permute-start(f32[256,256]{1,0:T(8,128)S(1)} %shard_map.61), channel_id=1, source_target_pairs={{0,12},{1,13},{2,14},{3,15},{4,0},{5,1},{6,2},{7,3},{8,4},{9,5},{1... | collective-permute-start | bytes 786440 | tf_op jit(solution)/shard_map/ppermute | solution.py:263
  104.9 2.0 %shard_map.56.refs_0_ = f32[256,256]{1,0:T(8,128)S(1)} custom-call(f32[1024,128]{1,0:T(8,128)S(1)} %get-tuple-element.31.r_0_, f32[8,4096]{1,0:T(8,128)S(1)} %get-tuple-element.32.r_1_, f32[1024,256]{1,0:T(8,128)S(1)} %bitcast.23, bf16[4096,256]{1,0:T(8,128)(2,1)S(1)} %get-tuple-element.21.r_1_.r_3_, bf16[4096,256]{1,0:T(8,128)(2,1)S(1)} %get-tuple-element.22.r_2_.r_4_, ...), custom_call_target="tpu_custom_call" | custom-call | flops 536870912 | bytes 1048576 | tf_op jit(solution)/shard_map/pallas_call | solution.py:184
  107.0 4.2 %collective-permute-done.10.refs_1_ = f32[256,256]{1,0:T(8,128)S(1)} collective-permute-done((f32[256,256]{1,0:T(8,128)S(1)}, f32[256,256]{1,0:T(8,128)S(1)}, u32[]{:S(2)}, u32[]{:S(2)}) %collective-permute-start.10) | collective-permute-done | bytes 262176 | tf_op jit(solution)/shard_map/ppermute | solution.py:263
  113.5 2.5 %collective-permute-start.14 = (f32[64,256]{1,0:T(8,128)S(1)}, f32[64,256]{1,0:T(8,128)S(1)}, u32[]{:S(2)}, u32[]{:S(2)}) collective-permute-start(f32[64,256]{1,0:T(8,128)S(1)} %get-tuple-element.36), channel_id=1, source_target_pairs={{0,3},{1,0},{2,1},{3,2},{4,7},{5,4},{6,5},{7,6},{8,11},{9,8},{10,9... | collective-permute-start | bytes 196616 | tf_op jit(solution)/shard_map/ppermute | solution.py:266
  116.0 1.9 %collective-permute-done.12.refs_1_ = f32[64,256]{1,0:T(8,128)S(1)} collective-permute-done((f32[64,256]{1,0:T(8,128)S(1)}, f32[64,256]{1,0:T(8,128)S(1)}, u32[]{:S(2)}, u32[]{:S(2)}) %collective-permute-start.12) | collective-permute-done | bytes 65568 | tf_op jit(solution)/shard_map/ppermute | solution.py:266
  (41 shorter events, 10.7 us)
Async XLA Ops:
  0.6 13.2 %copy-start = (f32[512,256]{1,0:T(8,128)S(1)}, f32[512,256]{1,0:T(8,128)}, u32[]{:S(2)}) copy-start(f32[512,256]{1,0:T(8,128)} %r_1_.1) | copy-start | bytes 1572868
  0.6 16.3 %collective-permute-start = (f32[512,256]{1,0:T(8,128)}, f32[512,256]{1,0:T(8,128)S(1)}, u32[]{:S(2)}, u32[]{:S(2)}) collective-permute-start(f32[512,256]{1,0:T(8,128)} %r_1_.1), channel_id=1, source_target_pairs={{0,32},{16,48},{32,64},{48,80},{64,96},{80,112},{96,0},{112,16},{1... | collective-permute-start | bytes 1572872 | tf_op jit(solution)/shard_map/ppermute | solution.py:221
  2.7 14.5 %collective-permute-start.1 = (f32[512,256]{1,0:T(8,128)}, f32[512,256]{1,0:T(8,128)S(1)}, u32[]{:S(2)}, u32[]{:S(2)}) collective-permute-start(f32[512,256]{1,0:T(8,128)} %r_1_.1), channel_id=1, source_target_pairs={{0,96},{16,112},{32,0},{48,16},{64,32},{80,48},{96,64},{112,80},{1... | collective-permute-start | bytes 1572872 | tf_op jit(solution)/shard_map/ppermute | solution.py:221
  4.9 0.8 copy-start.1
  6.8 24.3 %all-to-all-start = ((f32[16,64,256]{2,1,0:T(8,128)}), f32[16,64,256]{2,1,0:T(8,128)S(1)}, u32[]{:S(2)}, u32[]{:S(2)}) async-start(f32[16,64,256]{2,1,0:T(8,128)} %shard_map.49), calls=%async_computation | async-start | bytes 2097152 | tf_op jit(solution)/shard_map/all_to_all | solution.py:208
  13.9 12.8 %collective-permute-start.4 = (f32[512,256]{1,0:T(8,128)S(1)}, f32[512,256]{1,0:T(8,128)S(1)}, u32[]{:S(2)}, u32[]{:S(2)}) collective-permute-start(f32[512,256]{1,0:T(8,128)S(1)} %copy-done), channel_id=1, source_target_pairs={{0,16},{16,0},{32,48},{48,32},{64,80},{80,64},{96,112},{112,96},{1... | collective-permute-start | bytes 1572872 | tf_op jit(solution)/shard_map/ppermute | solution.py:224
  17.0 8.8 %collective-permute-start.2 = (f32[256,256]{1,0:T(8,128)S(1)}, f32[256,256]{1,0:T(8,128)S(1)}, u32[]{:S(2)}, u32[]{:S(2)}) collective-permute-start(f32[256,256]{1,0:T(8,128)S(1)} %slice.8), channel_id=1, source_target_pairs={{0,32},{16,48},{32,64},{48,80},{64,96},{80,112},{96,0},{112,16},{1... | collective-permute-start | bytes 786440 | tf_op jit(solution)/shard_map/ppermute | solution.py:221
  17.1 14.1 %collective-permute-start.5 = (f32[512,256]{1,0:T(8,128)S(1)}, f32[512,256]{1,0:T(8,128)}, u32[]{:S(2)}, u32[]{:S(2)}) collective-permute-start(f32[512,256]{1,0:T(8,128)S(1)} %collective-permute-done.r_2_), channel_id=1, source_target_pairs={{0,16},{16,0},{32,48},{48,32},{64,80},{80,64},{96,112},{112,96},{1... | collective-permute-start | bytes 1572872 | tf_op jit(solution)/shard_map/ppermute | solution.py:224
  17.2 14.0 %collective-permute-start.6 = (f32[512,256]{1,0:T(8,128)S(1)}, f32[512,256]{1,0:T(8,128)}, u32[]{:S(2)}, u32[]{:S(2)}) collective-permute-start(f32[512,256]{1,0:T(8,128)S(1)} %collective-permute-done.1.r_3_), channel_id=1, source_target_pairs={{0,16},{16,0},{32,48},{48,32},{64,80},{80,64},{96,112},{112,96},{1... | collective-permute-start | bytes 1572872 | tf_op jit(solution)/shard_map/ppermute | solution.py:224
  17.7 8.9 %collective-permute-start.3 = (f32[256,256]{1,0:T(8,128)S(1)}, f32[256,256]{1,0:T(8,128)}, u32[]{:S(2)}, u32[]{:S(2)}) collective-permute-start(f32[256,256]{1,0:T(8,128)S(1)} %slice.9), channel_id=1, source_target_pairs={{0,96},{16,112},{32,0},{48,16},{64,32},{80,48},{96,64},{112,80},{1... | collective-permute-start | bytes 786440 | tf_op jit(solution)/shard_map/ppermute | solution.py:221
  25.8 5.4 %collective-permute-start.7 = (f32[256,256]{1,0:T(8,128)S(1)}, f32[256,256]{1,0:T(8,128)}, u32[]{:S(2)}, u32[]{:S(2)}) collective-permute-start(f32[256,256]{1,0:T(8,128)S(1)} %collective-permute-done.2.r_4_), channel_id=1, source_target_pairs={{0,16},{16,0},{32,48},{48,32},{64,80},{80,64},{96,112},{112,96},{1... | collective-permute-start | bytes 786440 | tf_op jit(solution)/shard_map/ppermute | solution.py:224
  26.6 4.5 %collective-permute-start.8 = (f32[256,256]{1,0:T(8,128)}, f32[256,256]{1,0:T(8,128)}, u32[]{:S(2)}, u32[]{:S(2)}) collective-permute-start(f32[256,256]{1,0:T(8,128)} %collective-permute-done.3.r_5_), channel_id=1, source_target_pairs={{0,16},{16,0},{32,48},{48,32},{64,80},{80,64},{96,112},{112,96},{1... | collective-permute-start | bytes 786440 | tf_op jit(solution)/shard_map/ppermute | solution.py:224
  95.9 11.0 %collective-permute-start.9 = (f32[256,256]{1,0:T(8,128)S(1)}, f32[256,256]{1,0:T(8,128)S(1)}, u32[]{:S(2)}, u32[]{:S(2)}) collective-permute-start(f32[256,256]{1,0:T(8,128)S(1)} %shard_map.57), channel_id=1, source_target_pairs={{0,8},{1,9},{2,10},{3,11},{4,12},{5,13},{6,14},{7,15},{8,0},{9,1},... | collective-permute-start | bytes 786440 | tf_op jit(solution)/shard_map/ppermute | solution.py:263
  99.5 11.7 %collective-permute-start.10 = (f32[256,256]{1,0:T(8,128)S(1)}, f32[256,256]{1,0:T(8,128)S(1)}, u32[]{:S(2)}, u32[]{:S(2)}) collective-permute-start(f32[256,256]{1,0:T(8,128)S(1)} %shard_map.59), channel_id=1, source_target_pairs={{0,4},{1,5},{2,6},{3,7},{4,8},{5,9},{6,10},{7,11},{8,12},{9,13},{1... | collective-permute-start | bytes 786440 | tf_op jit(solution)/shard_map/ppermute | solution.py:263
  102.3 8.9 %collective-permute-start.11 = (f32[256,256]{1,0:T(8,128)S(1)}, f32[256,256]{1,0:T(8,128)S(1)}, u32[]{:S(2)}, u32[]{:S(2)}) collective-permute-start(f32[256,256]{1,0:T(8,128)S(1)} %shard_map.61), channel_id=1, source_target_pairs={{0,12},{1,13},{2,14},{3,15},{4,0},{5,1},{6,2},{7,3},{8,4},{9,5},{1... | collective-permute-start | bytes 786440 | tf_op jit(solution)/shard_map/ppermute | solution.py:263
  111.3 6.6 %collective-permute-start.12 = (f32[64,256]{1,0:T(8,128)S(1)}, f32[64,256]{1,0:T(8,128)S(1)}, u32[]{:S(2)}, u32[]{:S(2)}) collective-permute-start(f32[64,256]{1,0:T(8,128)S(1)} %get-tuple-element.34), channel_id=1, source_target_pairs={{0,2},{1,3},{2,0},{3,1},{4,6},{5,7},{6,4},{7,5},{8,10},{9,11},{10,... | collective-permute-start | bytes 196616 | tf_op jit(solution)/shard_map/ppermute | solution.py:266
  112.8 5.6 %collective-permute-start.13 = (f32[64,256]{1,0:T(8,128)S(1)}, f32[64,256]{1,0:T(8,128)S(1)}, u32[]{:S(2)}, u32[]{:S(2)}) collective-permute-start(f32[64,256]{1,0:T(8,128)S(1)} %get-tuple-element.35), channel_id=1, source_target_pairs={{0,1},{1,2},{2,3},{3,0},{4,5},{5,6},{6,7},{7,4},{8,9},{9,10},{10,1... | collective-permute-start | bytes 196616 | tf_op jit(solution)/shard_map/ppermute | solution.py:266
  113.5 4.9 %collective-permute-start.14 = (f32[64,256]{1,0:T(8,128)S(1)}, f32[64,256]{1,0:T(8,128)S(1)}, u32[]{:S(2)}, u32[]{:S(2)}) collective-permute-start(f32[64,256]{1,0:T(8,128)S(1)} %get-tuple-element.36), channel_id=1, source_target_pairs={{0,3},{1,0},{2,1},{3,2},{4,7},{5,4},{6,5},{7,6},{8,11},{9,8},{10,9... | collective-permute-start | bytes 196616 | tf_op jit(solution)/shard_map/ppermute | solution.py:266

commit v8 on v7

--- a/solution.py
+++ b/solution.py
@@ -142,7 +142,7 @@
 def grad_kernel(first, awide_ref, bwide_ref, a_ref, bhi_ref, blo_ref, s_ref, g_ref, mass):
     n = g_ref.shape[0]
     rows = pl.ds(pl.multiple_of(first(), n), n)
-    step = 1024
+    step = 256
 
     for start in range(0, s_ref.shape[1], step):
         at = pl.ds(start, step)

time: 120 us -> 120 us (level)
  transfers between devices with their start and end apart: 16 -> 16, of which waited for: 7 -> 8; matrix products, arithmetic and copies ran while one was open for 0% -> 0% of each run, Pallas kernels for 6% -> 6%
where the time goes in v8:
time: 120 us; the launch traced here: 119 us
  blocking collectives  42.3 us (35%)
  Pallas kernels  29.4 us (24%)
  starting transfers between devices  24.9 us (21%)
  waiting for transfers between devices  20.1 us (17%)
  local copies, waits for them, and re-layouts  1.48 us (1%)
    all_to_all x4, blocking collectives, spread(): return lax.all_to_all(x, axis, 0, 0, tiled=True)  42.3 us
    pallas_call x15, Pallas kernels, call(): pl.pallas_call(kernel, out_shape=outs, in_specs=ins or [VM] * len(args),...  29.4 us
    ppermute x4, waiting for transfers between devices, move(): return lax.ppermute(x, 'aa', [(i, (i + 2 * by) % na) for i in range(na)])  8.74 us
    ppermute x4, starting transfers between devices, move(): return lax.ppermute(x, 'aa', [(i, (i + 2 * by) % na) for i in range(na)])  7.56 us
    all_to_all x1, starting transfers between devices, spread(): return lax.all_to_all(x, axis, 0, 0, tiled=True)  7.03 us
    ppermute x3, starting transfers between devices, along_x(): return lax.ppermute(v, 'ba', [(i, (i + side * by) % nb) for i in range(nb)])  4.89 us
    ppermute x3, starting transfers between devices, along_y(): lax.ppermute(v, 'ba', [(i, i // side * side + (i + by) % side) for i in r...  4.71 us
    all_to_all x1, waiting for transfers between devices, spread(): return lax.all_to_all(x, axis, 0, 0, tiled=True)  4.48 us
  transfers between devices with their start and end apart: 16, of which 8 were waited for; matrix products, arithmetic and copies ran while one was open for 0% of the time, Pallas kernels for 6%

profile of v8, /device:TPU:0, one launch (start us, length us, event | category | flops | bytes accessed | tf_op | source)
XLA Modules:
  0.0 119.0 jit_solution(13306049801552150339)
XLA Ops:
  0.6 2.1 %collective-permute-start = (f32[512,256]{1,0:T(8,128)}, f32[512,256]{1,0:T(8,128)S(1)}, u32[]{:S(2)}, u32[]{:S(2)}) collective-permute-start(f32[512,256]{1,0:T(8,128)} %r_1_.1), channel_id=1, source_target_pairs={{0,32},{16,48},{32,64},{48,80},{64,96},{80,112},{96,0},{112,16},{1... | collective-permute-start | bytes 1572872 | tf_op jit(solution)/shard_map/ppermute | solution.py:221
  2.7 2.2 %collective-permute-start.1 = (f32[512,256]{1,0:T(8,128)}, f32[512,256]{1,0:T(8,128)S(1)}, u32[]{:S(2)}, u32[]{:S(2)}) collective-permute-start(f32[512,256]{1,0:T(8,128)} %r_1_.1), channel_id=1, source_target_pairs={{0,96},{16,112},{32,0},{48,16},{64,32},{80,48},{96,64},{112,80},{1... | collective-permute-start | bytes 1572872 | tf_op jit(solution)/shard_map/ppermute | solution.py:221
  6.8 7.0 %all-to-all-start = ((f32[16,64,256]{2,1,0:T(8,128)}), f32[16,64,256]{2,1,0:T(8,128)S(1)}, u32[]{:S(2)}, u32[]{:S(2)}) async-start(f32[16,64,256]{2,1,0:T(8,128)} %shard_map.49), calls=%async_computation | async-start | bytes 2097152 | tf_op jit(solution)/shard_map/all_to_all | solution.py:208
  14.0 3.0 %collective-permute-done.r_2_ = f32[512,256]{1,0:T(8,128)S(1)} collective-permute-done((f32[512,256]{1,0:T(8,128)}, f32[512,256]{1,0:T(8,128)S(1)}, u32[]{:S(2)}, u32[]{:S(2)}) %collective-permute-start) | collective-permute-done | bytes 524320 | tf_op jit(solution)/shard_map/ppermute | solution.py:221
  17.7 3.2 %collective-permute-start.3 = (f32[256,256]{1,0:T(8,128)S(1)}, f32[256,256]{1,0:T(8,128)}, u32[]{:S(2)}, u32[]{:S(2)}) collective-permute-start(f32[256,256]{1,0:T(8,128)S(1)} %slice.9), channel_id=1, source_target_pairs={{0,96},{16,112},{32,0},{48,16},{64,32},{80,48},{96,64},{112,80},{1... | collective-permute-start | bytes 786440 | tf_op jit(solution)/shard_map/ppermute | solution.py:221
  20.9 4.9 %collective-permute-done.2.r_4_ = f32[256,256]{1,0:T(8,128)S(1)} collective-permute-done((f32[256,256]{1,0:T(8,128)S(1)}, f32[256,256]{1,0:T(8,128)S(1)}, u32[]{:S(2)}, u32[]{:S(2)}) %collective-permute-start.2) | collective-permute-done | bytes 262176 | tf_op jit(solution)/shard_map/ppermute | solution.py:221
  26.6 4.5 %all-to-all-done = f32[16,64,256]{2,1,0:T(8,128)S(1)} async-done(((f32[16,64,256]{2,1,0:T(8,128)}), f32[16,64,256]{2,1,0:T(8,128)S(1)}, u32[]{:S(2)}, u32[]{:S(2)}) %all-to-all-start) | async-done | bytes 1048608 | tf_op jit(solution)/shard_map/all_to_all | solution.py:208
  31.1 2.1 %shard_map.50 = (bf16[1024,768]{1,0:T(8,128)(2,1)S(1)}, f32[1,1024]{1,0:T(1,128)S(1)}, bf16[4096,256]{1,0:T(8,128)(2,1)S(1)}, bf16[4096,256]{1,0:T(8,128)(2,1)S(1)}, f32[1,4096]{1,0:T(1,128)S(1)}) custom-call(f32[1024,256]{1,0:T(8,128)S(1)} %bitcast.19, f32[512,256]{1,0:T(8,128)S(1)} %copy-done, f32[512,256]{1,0:T(8,128)S(1)} %collective-permute-done.r_2_, ...), custom_call_target="tpu_custom_call" | custom-call | tf_op jit(solution)/shard_map/pallas_call | solution.py:184
  33.2 7.5 %shard_map.51 = (f32[1024,4096]{1,0:T(8,128)S(1)}, f32[16,1024]{1,0:T(8,128)S(1)}) custom-call(bf16[1024,768]{1,0:T(8,128)(2,1)S(1)} %get-tuple-element.20.r_0_, bf16[4096,256]{1,0:T(8,128)(2,1)S(1)} %get-tuple-element.21.r_1_.r_3_, bf16[4096,256]{1,0:T(8,128)(2,1)S(1)} %get-tuple-element.22.r_2_.r_4_, f32[1,4096]{1,0:T(1,128)S(1)} %get-tuple-element.23.r_3_.r_1_), custom_call_target="tpu_custom_call" | custom-call | tf_op jit(solution)/shard_map/pallas_call | solution.py:184
  40.8 11.9 %all_to_all.49 = f32[16,1,1024]{2,1,0:T(1,128)S(1)} all-to-all(f32[16,1,1024]{2,1,0:T(1,128)S(1)} %copy.5), channel_id=1, replica_groups=mesh['aa'=8,'ba'=16] {'ba'}, dimensions={0} | all-to-all | bytes 131072 | tf_op jit(solution)/shard_map/all_to_all | solution.py:208
  52.7 3.1 %shard_map.52 = (f32[8,4096]{1,0:T(8,128)S(1)}, f32[1,1024]{1,0:T(1,128)}) custom-call(f32[16,1024]{1,0:T(8,128)S(1)} %bitcast.26, f32[1,1024]{1,0:T(1,128)S(1)} %get-tuple-element.25.r_1_, f32[1024,4096]{1,0:T(8,128)S(1)} %get-tuple-element.26.r_2_.r_1_.r_5_), custom_call_target="tpu_custom_call" | custom-call | tf_op jit(solution)/shard_map/pallas_call | solution.py:184
  55.9 11.0 %all_to_all.50 = f32[8,1,4096]{2,1,0:T(1,128)S(1)} all-to-all(f32[8,1,4096]{2,1,0:T(1,128)S(1)} %copy.6), channel_id=1, replica_groups=mesh['aa'=8,'ba'=16] {'aa'}, dimensions={0} | all-to-all | bytes 262144 | tf_op jit(solution)/shard_map/all_to_all | solution.py:208
  67.0 3.3 %shard_map.53 = f32[16,1024]{1,0:T(8,128)S(1)} custom-call(f32[8,4096]{1,0:T(8,128)S(1)} %bitcast.24, f32[1024,4096]{1,0:T(8,128)S(1)} %get-tuple-element.26.r_2_.r_1_.r_5_), custom_call_target="tpu_custom_call" | custom-call | tf_op jit(solution)/shard_map/pallas_call | solution.py:184
  70.4 10.9 %all_to_all.51 = f32[16,1,1024]{2,1,0:T(1,128)S(1)} all-to-all(f32[16,1,1024]{2,1,0:T(1,128)S(1)} %copy.7), channel_id=1, replica_groups=mesh['aa'=8,'ba'=16] {'ba'}, dimensions={0} | all-to-all | bytes 131072 | tf_op jit(solution)/shard_map/all_to_all | solution.py:208
  81.3 3.1 %shard_map.54 = (f32[8,4096]{1,0:T(8,128)S(1)}, f32[1,1024]{1,0:T(1,128)}, f32[1024,128]{1,0:T(8,128)S(1)}) custom-call(f32[16,1024]{1,0:T(8,128)S(1)} %bitcast.27, f32[1,1024]{1,0:T(1,128)S(1)} %get-tuple-element.25.r_1_, f32[1024,4096]{1,0:T(8,128)S(1)} %get-tuple-element.26.r_2_.r_1_.r_5_), custom_call_target="tpu_custom_call" | custom-call | tf_op jit(solution)/shard_map/pallas_call | solution.py:184
  84.6 8.5 %all_to_all.52 = f32[8,1,4096]{2,1,0:T(1,128)S(1)} all-to-all(f32[8,1,4096]{2,1,0:T(1,128)S(1)} %copy.8), channel_id=1, replica_groups=mesh['aa'=8,'ba'=16] {'aa'}, dimensions={0} | all-to-all | bytes 262144 | tf_op jit(solution)/shard_map/all_to_all | solution.py:208
  93.9 2.0 %shard_map.57 = f32[256,256]{1,0:T(8,128)S(1)} custom-call(f32[1024,128]{1,0:T(8,128)S(1)} %get-tuple-element.31.r_0_, f32[8,4096]{1,0:T(8,128)S(1)} %get-tuple-element.32.r_1_, f32[1024,256]{1,0:T(8,128)S(1)} %bitcast.20, bf16[4096,256]{1,0:T(8,128)(2,1)S(1)} %get-tuple-element.21.r_1_.r_3_, bf16[4096,256]{1,0:T(8,128)(2,1)S(1)} %get-tuple-element.22.r_2_.r_4_, ...), custom_call_target="tpu_custom_call" | custom-call | flops 536870912 | bytes 1048576 | tf_op jit(solution)/shard_map/pallas_call | solution.py:184
  97.3 2.0 %shard_map.59 = f32[256,256]{1,0:T(8,128)S(1)} custom-call(f32[1024,128]{1,0:T(8,128)S(1)} %get-tuple-element.31.r_0_, f32[8,4096]{1,0:T(8,128)S(1)} %get-tuple-element.32.r_1_, f32[1024,256]{1,0:T(8,128)S(1)} %bitcast.21, bf16[4096,256]{1,0:T(8,128)(2,1)S(1)} %get-tuple-element.21.r_1_.r_3_, bf16[4096,256]{1,0:T(8,128)(2,1)S(1)} %get-tuple-element.22.r_2_.r_4_, ...), custom_call_target="tpu_custom_call" | custom-call | flops 536870912 | bytes 1048576 | tf_op jit(solution)/shard_map/pallas_call | solution.py:184
  100.2 2.0 %shard_map.61 = f32[256,256]{1,0:T(8,128)S(1)} custom-call(f32[1024,128]{1,0:T(8,128)S(1)} %get-tuple-element.31.r_0_, f32[8,4096]{1,0:T(8,128)S(1)} %get-tuple-element.32.r_1_, f32[1024,256]{1,0:T(8,128)S(1)} %bitcast.22, bf16[4096,256]{1,0:T(8,128)(2,1)S(1)} %get-tuple-element.21.r_1_.r_3_, bf16[4096,256]{1,0:T(8,128)(2,1)S(1)} %get-tuple-element.22.r_2_.r_4_, ...), custom_call_target="tpu_custom_call" | custom-call | flops 536870912 | bytes 1048576 | tf_op jit(solution)/shard_map/pallas_call | solution.py:184
  102.1 2.5 %collective-permute-start.11 = (f32[256,256]{1,0:T(8,128)S(1)}, f32[256,256]{1,0:T(8,128)S(1)}, u32[]{:S(2)}, u32[]{:S(2)}) collective-permute-start(f32[256,256]{1,0:T(8,128)S(1)} %shard_map.61), channel_id=1, source_target_pairs={{0,12},{1,13},{2,14},{3,15},{4,0},{5,1},{6,2},{7,3},{8,4},{9,5},{1... | collective-permute-start | bytes 786440 | tf_op jit(solution)/shard_map/ppermute | solution.py:263
  104.7 2.0 %shard_map.56.refs_0_ = f32[256,256]{1,0:T(8,128)S(1)} custom-call(f32[1024,128]{1,0:T(8,128)S(1)} %get-tuple-element.31.r_0_, f32[8,4096]{1,0:T(8,128)S(1)} %get-tuple-element.32.r_1_, f32[1024,256]{1,0:T(8,128)S(1)} %bitcast.23, bf16[4096,256]{1,0:T(8,128)(2,1)S(1)} %get-tuple-element.21.r_1_.r_3_, bf16[4096,256]{1,0:T(8,128)(2,1)S(1)} %get-tuple-element.22.r_2_.r_4_, ...), custom_call_target="tpu_custom_call" | custom-call | flops 536870912 | bytes 1048576 | tf_op jit(solution)/shard_map/pallas_call | solution.py:184
  106.9 4.2 %collective-permute-done.10.refs_1_ = f32[256,256]{1,0:T(8,128)S(1)} collective-permute-done((f32[256,256]{1,0:T(8,128)S(1)}, f32[256,256]{1,0:T(8,128)S(1)}, u32[]{:S(2)}, u32[]{:S(2)}) %collective-permute-start.10) | collective-permute-done | bytes 262176 | tf_op jit(solution)/shard_map/ppermute | solution.py:263
  113.4 2.5 %collective-permute-start.14 = (f32[64,256]{1,0:T(8,128)S(1)}, f32[64,256]{1,0:T(8,128)S(1)}, u32[]{:S(2)}, u32[]{:S(2)}) collective-permute-start(f32[64,256]{1,0:T(8,128)S(1)} %get-tuple-element.36), channel_id=1, source_target_pairs={{0,3},{1,0},{2,1},{3,2},{4,7},{5,4},{6,5},{7,6},{8,11},{9,8},{10,9... | collective-permute-start | bytes 196616 | tf_op jit(solution)/shard_map/ppermute | solution.py:266
  115.9 1.9 %collective-permute-done.12.refs_1_ = f32[64,256]{1,0:T(8,128)S(1)} collective-permute-done((f32[64,256]{1,0:T(8,128)S(1)}, f32[64,256]{1,0:T(8,128)S(1)}, u32[]{:S(2)}, u32[]{:S(2)}) %collective-permute-start.12) | collective-permute-done | bytes 65568 | tf_op jit(solution)/shard_map/ppermute | solution.py:266
  (41 shorter events, 10.9 us)
Async XLA Ops:
  0.6 13.2 %copy-start = (f32[512,256]{1,0:T(8,128)S(1)}, f32[512,256]{1,0:T(8,128)}, u32[]{:S(2)}) copy-start(f32[512,256]{1,0:T(8,128)} %r_1_.1) | copy-start | bytes 1572868
  0.6 16.3 %collective-permute-start = (f32[512,256]{1,0:T(8,128)}, f32[512,256]{1,0:T(8,128)S(1)}, u32[]{:S(2)}, u32[]{:S(2)}) collective-permute-start(f32[512,256]{1,0:T(8,128)} %r_1_.1), channel_id=1, source_target_pairs={{0,32},{16,48},{32,64},{48,80},{64,96},{80,112},{96,0},{112,16},{1... | collective-permute-start | bytes 1572872 | tf_op jit(solution)/shard_map/ppermute | solution.py:221
  2.7 14.5 %collective-permute-start.1 = (f32[512,256]{1,0:T(8,128)}, f32[512,256]{1,0:T(8,128)S(1)}, u32[]{:S(2)}, u32[]{:S(2)}) collective-permute-start(f32[512,256]{1,0:T(8,128)} %r_1_.1), channel_id=1, source_target_pairs={{0,96},{16,112},{32,0},{48,16},{64,32},{80,48},{96,64},{112,80},{1... | collective-permute-start | bytes 1572872 | tf_op jit(solution)/shard_map/ppermute | solution.py:221
  4.9 0.8 copy-start.1
  6.8 24.3 %all-to-all-start = ((f32[16,64,256]{2,1,0:T(8,128)}), f32[16,64,256]{2,1,0:T(8,128)S(1)}, u32[]{:S(2)}, u32[]{:S(2)}) async-start(f32[16,64,256]{2,1,0:T(8,128)} %shard_map.49), calls=%async_computation | async-start | bytes 2097152 | tf_op jit(solution)/shard_map/all_to_all | solution.py:208
  13.9 12.8 %collective-permute-start.4 = (f32[512,256]{1,0:T(8,128)S(1)}, f32[512,256]{1,0:T(8,128)S(1)}, u32[]{:S(2)}, u32[]{:S(2)}) collective-permute-start(f32[512,256]{1,0:T(8,128)S(1)} %copy-done), channel_id=1, source_target_pairs={{0,16},{16,0},{32,48},{48,32},{64,80},{80,64},{96,112},{112,96},{1... | collective-permute-start | bytes 1572872 | tf_op jit(solution)/shard_map/ppermute | solution.py:224
  17.0 8.8 %collective-permute-start.2 = (f32[256,256]{1,0:T(8,128)S(1)}, f32[256,256]{1,0:T(8,128)S(1)}, u32[]{:S(2)}, u32[]{:S(2)}) collective-permute-start(f32[256,256]{1,0:T(8,128)S(1)} %slice.8), channel_id=1, source_target_pairs={{0,32},{16,48},{32,64},{48,80},{64,96},{80,112},{96,0},{112,16},{1... | collective-permute-start | bytes 786440 | tf_op jit(solution)/shard_map/ppermute | solution.py:221
  17.1 14.1 %collective-permute-start.5 = (f32[512,256]{1,0:T(8,128)S(1)}, f32[512,256]{1,0:T(8,128)}, u32[]{:S(2)}, u32[]{:S(2)}) collective-permute-start(f32[512,256]{1,0:T(8,128)S(1)} %collective-permute-done.r_2_), channel_id=1, source_target_pairs={{0,16},{16,0},{32,48},{48,32},{64,80},{80,64},{96,112},{112,96},{1... | collective-permute-start | bytes 1572872 | tf_op jit(solution)/shard_map/ppermute | solution.py:224
  17.2 14.0 %collective-permute-start.6 = (f32[512,256]{1,0:T(8,128)S(1)}, f32[512,256]{1,0:T(8,128)}, u32[]{:S(2)}, u32[]{:S(2)}) collective-permute-start(f32[512,256]{1,0:T(8,128)S(1)} %collective-permute-done.1.r_3_), channel_id=1, source_target_pairs={{0,16},{16,0},{32,48},{48,32},{64,80},{80,64},{96,112},{112,96},{1... | collective-permute-start | bytes 1572872 | tf_op jit(solution)/shard_map/ppermute | solution.py:224
  17.7 8.9 %collective-permute-start.3 = (f32[256,256]{1,0:T(8,128)S(1)}, f32[256,256]{1,0:T(8,128)}, u32[]{:S(2)}, u32[]{:S(2)}) collective-permute-start(f32[256,256]{1,0:T(8,128)S(1)} %slice.9), channel_id=1, source_target_pairs={{0,96},{16,112},{32,0},{48,16},{64,32},{80,48},{96,64},{112,80},{1... | collective-permute-start | bytes 786440 | tf_op jit(solution)/shard_map/ppermute | solution.py:221
  25.8 5.4 %collective-permute-start.7 = (f32[256,256]{1,0:T(8,128)S(1)}, f32[256,256]{1,0:T(8,128)}, u32[]{:S(2)}, u32[]{:S(2)}) collective-permute-start(f32[256,256]{1,0:T(8,128)S(1)} %collective-permute-done.2.r_4_), channel_id=1, source_target_pairs={{0,16},{16,0},{32,48},{48,32},{64,80},{80,64},{96,112},{112,96},{1... | collective-permute-start | bytes 786440 | tf_op jit(solution)/shard_map/ppermute | solution.py:224
  26.6 4.5 %collective-permute-start.8 = (f32[256,256]{1,0:T(8,128)}, f32[256,256]{1,0:T(8,128)}, u32[]{:S(2)}, u32[]{:S(2)}) collective-permute-start(f32[256,256]{1,0:T(8,128)} %collective-permute-done.3.r_5_), channel_id=1, source_target_pairs={{0,16},{16,0},{32,48},{48,32},{64,80},{80,64},{96,112},{112,96},{1... | collective-permute-start | bytes 786440 | tf_op jit(solution)/shard_map/ppermute | solution.py:224
  95.8 11.0 %collective-permute-start.9 = (f32[256,256]{1,0:T(8,128)S(1)}, f32[256,256]{1,0:T(8,128)S(1)}, u32[]{:S(2)}, u32[]{:S(2)}) collective-permute-start(f32[256,256]{1,0:T(8,128)S(1)} %shard_map.57), channel_id=1, source_target_pairs={{0,8},{1,9},{2,10},{3,11},{4,12},{5,13},{6,14},{7,15},{8,0},{9,1},... | collective-permute-start | bytes 786440 | tf_op jit(solution)/shard_map/ppermute | solution.py:263
  99.3 11.8 %collective-permute-start.10 = (f32[256,256]{1,0:T(8,128)S(1)}, f32[256,256]{1,0:T(8,128)S(1)}, u32[]{:S(2)}, u32[]{:S(2)}) collective-permute-start(f32[256,256]{1,0:T(8,128)S(1)} %shard_map.59), channel_id=1, source_target_pairs={{0,4},{1,5},{2,6},{3,7},{4,8},{5,9},{6,10},{7,11},{8,12},{9,13},{1... | collective-permute-start | bytes 786440 | tf_op jit(solution)/shard_map/ppermute | solution.py:263
  102.1 9.0 %collective-permute-start.11 = (f32[256,256]{1,0:T(8,128)S(1)}, f32[256,256]{1,0:T(8,128)S(1)}, u32[]{:S(2)}, u32[]{:S(2)}) collective-permute-start(f32[256,256]{1,0:T(8,128)S(1)} %shard_map.61), channel_id=1, source_target_pairs={{0,12},{1,13},{2,14},{3,15},{4,0},{5,1},{6,2},{7,3},{8,4},{9,5},{1... | collective-permute-start | bytes 786440 | tf_op jit(solution)/shard_map/ppermute | solution.py:263
  111.2 6.6 %collective-permute-start.12 = (f32[64,256]{1,0:T(8,128)S(1)}, f32[64,256]{1,0:T(8,128)S(1)}, u32[]{:S(2)}, u32[]{:S(2)}) collective-permute-start(f32[64,256]{1,0:T(8,128)S(1)} %get-tuple-element.34), channel_id=1, source_target_pairs={{0,2},{1,3},{2,0},{3,1},{4,6},{5,7},{6,4},{7,5},{8,10},{9,11},{10,... | collective-permute-start | bytes 196616 | tf_op jit(solution)/shard_map/ppermute | solution.py:266
  112.7 5.6 %collective-permute-start.13 = (f32[64,256]{1,0:T(8,128)S(1)}, f32[64,256]{1,0:T(8,128)S(1)}, u32[]{:S(2)}, u32[]{:S(2)}) collective-permute-start(f32[64,256]{1,0:T(8,128)S(1)} %get-tuple-element.35), channel_id=1, source_target_pairs={{0,1},{1,2},{2,3},{3,0},{4,5},{5,6},{6,7},{7,4},{8,9},{9,10},{10,1... | collective-permute-start | bytes 196616 | tf_op jit(solution)/shard_map/ppermute | solution.py:266
  113.4 4.9 %collective-permute-start.14 = (f32[64,256]{1,0:T(8,128)S(1)}, f32[64,256]{1,0:T(8,128)S(1)}, u32[]{:S(2)}, u32[]{:S(2)}) collective-permute-start(f32[64,256]{1,0:T(8,128)S(1)} %get-tuple-element.36), channel_id=1, source_target_pairs={{0,3},{1,0},{2,1},{3,2},{4,7},{5,4},{6,5},{7,6},{8,11},{9,8},{10,9... | collective-permute-start | bytes 196616 | tf_op jit(solution)/shard_map/ppermute | solution.py:266
